TPU v7x, 32 devices: a whole 2x2x4 slice. The times are simulated.
32 devices in a mesh: seq: 8 (over z, y), res: 4 (over x, core).
Axes of the slice: x: 2, y: 2, z: 4, core: 2. Of those that a mesh axis runs over, the one named last changes fastest.
Arguments:
- alignment_query: bfloat16 [64, 256, 256], P(('seq', 'res')), may hold values from -8 to 8
- alignment_key: bfloat16 [64, 256, 256], P(('seq', 'res')), may hold values from -8 to 8
- attended_vectors: bfloat16 [64, 256, 256], P(('seq', 'res')), may hold values from -6 to 6
- attended_cotangent: bfloat16 [64, 256, 256], P(('seq', 'res')), may hold values from -6 to 6
- chain_index_per_residue: int32 [256], replicated, may hold values from 0 to 3, as said below
- pair: bfloat16 [256, 256, 128], P('res', 'seq'), may hold values from -6 to 6
- pair_bias_matrix: bfloat16 [128, 8], replicated, may hold values from -0.5 to 0.5
- left_operand_input: bfloat16 [256, 256, 128], P('seq', 'res'), may hold values from -6 to 6
- right_operand_input: bfloat16 [256, 256, 128], P('res', 'seq'), may hold values from -6 to 6
Outputs:
- query_gradient: bfloat16 [64, 256, 256], P(('seq', 'res'))
- key_gradient: bfloat16 [64, 256, 256], P(('seq', 'res'))
- value_gradient: bfloat16 [64, 256, 256], P(('seq', 'res'))
- d_bias_weight: float32 [128, 8], replicated
- d_left: bfloat16 [256, 256, 128], P('seq', 'res')
- d_right: bfloat16 [256, 256, 128], P('res', 'seq')
Inputs may be any that keep to these rules, and one draw needn't show every extreme that they name: `chain_index_per_residue`: chain numbers never fall along the residues; four chains, each of at least 32 residues.
All inputs are finite; a program needn't handle non-finite values.
Results may differ from a plain program's by a relative error of at most 0.0074.
Values may be sent and summed in bfloat16 or wider, within the bound.
No kernel may reach another device: no remote copies, remote signals or barrier semaphores. Data moves between devices by JAX's collectives and lax.ppermute only.
A program may use at most 64 MiB of HBM per device.

v0:
```python
import jax
import jax.numpy as jnp
from jax import lax
from jax.sharding import PartitionSpec as P

HEADS = 8
HEAD_DIM = 32


big_negative = -1e30


def shards(
    alignment_query,
    alignment_key,
    attended_vectors,
    attended_cotangent,
    chain_index_per_residue,
    pair,
    pair_bias_matrix,
    left_operand_input,
    right_operand_input,
):
    f32 = jnp.float32
    reduced_mantissa_type = jnp.bfloat16
    rows_per_shard, residue_total, slice_width = alignment_query.shape
    logit_multiplier = HEAD_DIM ** (-0.5)
    bias_local = jnp.einsum("ijc,ch->hij", pair, pair_bias_matrix, preferred_element_type=f32)
    bias_rows = lax.all_gather(bias_local, "seq", axis=2, tiled=True)
    bias = lax.all_gather(bias_rows, "res", axis=1, tiled=True)
    allowed = chain_index_per_residue[:, None] == chain_index_per_residue[None, :]

    def single_row(carry, row):
        query, keys, content_entries, grads = row
        query_h = query.reshape(residue_total, HEADS, HEAD_DIM)
        keys_h = keys.reshape(residue_total, HEADS, HEAD_DIM)
        values_h = content_entries.reshape(residue_total, HEADS, HEAD_DIM)
        grads_h = grads.reshape(residue_total, HEADS, HEAD_DIM)
        scores = (
            jnp.einsum("ihd,jhd->hij", query_h, keys_h, preferred_element_type=f32)
            * logit_multiplier
            + bias
        )
        scores = jnp.where(allowed[None], scores, big_negative)
        top = jnp.max(scores, axis=-1, keepdims=True)
        expo = jnp.exp(scores - top)
        probs = expo / jnp.sum(expo, axis=-1, keepdims=True)
        dprobs = jnp.einsum("ihd,jhd->hij", grads_h, values_h, preferred_element_type=f32)
        dscores = probs * (dprobs - jnp.sum(probs * dprobs, axis=-1, keepdims=True))
        logit_cotangent_coarse = dscores.astype(reduced_mantissa_type)
        softmax_weights_coarse = probs.astype(reduced_mantissa_type)
        asking_cotangent_unit = (
            jnp.einsum("ayw,wak->yak", logit_cotangent_coarse, keys_h, preferred_element_type=f32)
            * logit_multiplier
        ).astype(reduced_mantissa_type)
        lookup_cotangent_unit = (
            jnp.einsum("lzx,zlf->xlf", logit_cotangent_coarse, query_h, preferred_element_type=f32)
            * logit_multiplier
        ).astype(reduced_mantissa_type)
        content_cotangent_unit = jnp.einsum(
            "lzx,zlf->xlf", softmax_weights_coarse, grads_h, preferred_element_type=f32
        ).astype(reduced_mantissa_type)
        return (
            carry + dscores,
            (
                asking_cotangent_unit.reshape(residue_total, slice_width),
                lookup_cotangent_unit.reshape(residue_total, slice_width),
                content_cotangent_unit.reshape(residue_total, slice_width),
            ),
        )

    start_offset = jnp.zeros((HEADS, residue_total, residue_total), f32)
    bias_part, (query_gradient, key_gradient, value_gradient) = lax.scan(
        single_row,
        start_offset,
        (alignment_query, alignment_key, attended_vectors, attended_cotangent),
    )
    row_sum = lax.psum_scatter(bias_part, "res", scatter_dimension=1, tiled=True)
    bias_gradient = lax.psum_scatter(row_sum, "seq", scatter_dimension=2, tiled=True)
    weight_term = jnp.einsum(
        "ijc,hij->ch", pair.astype(f32), bias_gradient, precision=lax.Precision.HIGHEST
    )
    d_bias_weight = lax.psum(weight_term, ("seq", "res"))
    pair_grad = jnp.einsum(
        "hij,ch->ijc", bias_gradient, pair_bias_matrix.astype(f32), precision=lax.Precision.HIGHEST
    ).astype(reduced_mantissa_type)
    right_all = lax.all_gather(right_operand_input, "res", axis=0, tiled=True)
    d_left = lax.psum_scatter(
        jnp.einsum("kjc,ijc->kic", right_all, pair_grad, preferred_element_type=f32),
        "seq",
        scatter_dimension=0,
        tiled=True,
    ).astype(reduced_mantissa_type)
    left_all = lax.all_gather(left_operand_input, "seq", axis=0, tiled=True)
    d_right = lax.psum_scatter(
        jnp.einsum("kic,ijc->kjc", left_all, pair_grad, preferred_element_type=f32),
        "res",
        scatter_dimension=0,
        tiled=True,
    ).astype(reduced_mantissa_type)
    return (query_gradient, key_gradient, value_gradient, d_bias_weight, d_left, d_right)


def solution(mesh):
    placed = (
        P(("seq", "res"), None, None),
        P(("seq", "res"), None, None),
        P(("seq", "res"), None, None),
        P(("seq", "res"), None, None),
        P(),
        P("res", "seq", None),
        P(),
        P("seq", "res", None),
        P("res", "seq", None),
    )
    return jax.shard_map(
        shards,
        mesh=mesh,
        in_specs=placed,
        out_specs=(
            P(("seq", "res"), None, None),
            P(("seq", "res"), None, None),
            P(("seq", "res"), None, None),
            P(),
            P("seq", "res", None),
            P("res", "seq", None),
        ),
        check_vma=False,
    )
```

profile of v0, /device:TPU:0, one launch (start us, length us, event | category | flops | bytes accessed | tf_op | source)
XLA Modules:
  0.0 568.8 jit_solution(15609963274614333338)
XLA Ops:
  7.2 1.0 copy-done
  8.2 1.2 fusion.8
  9.4 34.6 %all_gather.12 = f32[8,64,256]{1,0,2:T(8,128)S(1)} all-gather(f32[8,64,32]{1,0,2:T(8,128)S(1)} %fusion.8), channel_id=1, replica_groups=mesh['seq'=8,'res'=4] {'seq'}, dimensions={2}, use_global_device_ids=true | all-gather | bytes 589824 | tf_op jit(solution)/shard_map/all_gather | solution.py:29
  44.0 1.2 copy.62
  45.3 23.5 %all-gather.4.cloned.1.call-done = f32[8,256,256]{2,0,1:T(8,128)} async-done(((f32[8,64,256]{2,0,1:T(8,128)}), f32[8,256,256]{2,0,1:T(8,128)}) %all-gather.4.cloned.1.call-update) | async-done | bytes 2097168 | tf_op jit(solution)/shard_map/all_gather | solution.py:30
  68.8 2.9 copy.65
  71.8 36.8 %while.17 = (s32[]{:T(128)}, f32[8,256,256]{1,2,0:T(8,128)}, bf16[2,256,256]{2,1,0:T(8,128)(2,1)}, bf16[2,256,256]{2,1,0:T(8,128)(2,1)}, bf16[2,256,256]{2,1,0:T...) while((s32[]{:T(128)}, f32[8,256,256]{1,2,0:T(8,128)}, ...), condition=%wide.region_4.5_spmd.clone, body=%wide.region_0.4_spmd.clone.sunk | while | flops 177078784 | bytes 54445444 | solution.py:73
  71.8 0.1 copy.106
  71.9 0.9 constant_dynamic-slice_fusion.9
  72.8 0.1 copy.107
  72.9 0.1 broadcast_compare_fusion.2
  73.0 2.1 add_select_fusion.2
  75.2 1.6 fusion.58
  76.8 1.1 constant_dynamic-slice_fusion.10
  78.0 0.9 constant_dynamic-slice_fusion.11
  78.9 0.1 copy.109
  79.0 1.8 multiply_reduce_fusion.2
  80.8 4.2 fusion.59
  85.0 0.3 fusion.60
  85.3 0.1 copy.110
  85.5 2.9 convolution_convert_fusion.3
  88.4 0.1 copy.111
  88.5 0.4 fusion.61
  88.9 0.1 copy.112
  89.1 0.7 copy-done.11
  90.0 0.9 constant_dynamic-slice_fusion.9
  91.0 0.1 broadcast_compare_fusion.2
  91.1 2.1 add_select_fusion.2
  93.2 1.6 fusion.58
  94.9 1.1 constant_dynamic-slice_fusion.10
  96.1 0.9 constant_dynamic-slice_fusion.11
  97.0 0.1 copy.109
  97.1 1.8 multiply_reduce_fusion.2
  98.9 4.8 fusion.59
  103.7 0.3 fusion.60
  104.0 0.1 copy.110
  104.2 2.9 convolution_convert_fusion.3
  107.1 0.1 copy.111
  107.2 0.4 fusion.61
  107.6 0.1 copy.112
  107.8 0.7 copy-done.11
  108.5 3.1 copy.68
  111.7 31.5 %reduce-scatter.5.cloned.1.call-done = f32[8,64,256]{2,0,1:T(8,128)} async-done(((f32[8,256,256]{2,0,1:T(8,128)}), f32[8,64,256]{2,0,1:T(8,128)}) %reduce-scatter.5.cloned.1.call-update) | async-done | bytes 524304 | tf_op jit(solution)/shard_map/reduce_scatter | solution.py:78
  143.2 2.5 copy.69
  145.8 2.5 copy.75
  148.3 0.5 all-gather.6.cloned.1.call-update
  148.9 61.6 %reduce-scatter.7.cloned.1.call-done = f32[8,64,32]{1,0,2:T(8,128)} async-done(((f32[8,64,256]{1,0,2:T(8,128)}), f32[8,64,32]{1,0,2:T(8,128)}) %reduce-scatter.7.cloned.1.call-update) | async-done | bytes 65552 | tf_op jit(solution)/shard_map/reduce_scatter | solution.py:79
  210.5 1.1 copy.71
  211.6 1.0 convolution_convert_fusion.1
  212.6 1.7 copy.72
  214.3 122.5 %all-gather.8.cloned.1.call-done = bf16[256,64,128]{1,0,2:T(8,128)(2,1)} async-done(((bf16[32,64,128]{1,0,2:T(8,128)(2,1)}), bf16[256,64,128]{1,0,2:T(8,128)(2,1)}) %all-gather.8.cloned.1.call-update) | async-done | bytes 4194320 | tf_op jit(solution)/shard_map/all_gather | solution.py:94
  336.8 8.2 %convolution_bitcast_fusion.1 = f32[256,32,128]{0,1,2:T(8,128)} fusion(bf16[64,32,128]{0,1,2:T(8,128)(2,1)S(1)} %copy.72, bf16[256,64,128]{1,0,2:T(8,128)(2,1)} %all-gather.8.cloned.1.call-done), kind=kOutput, calls=%fused_computation.24 | convolution fusion | flops 134217728 | bytes 8912896 | tf_op jit(solution)/shard_map/kic,ijc->kjc/dot_general | solution.py:96
  345.1 5.9 %copy.77 = f32[256,32,128]{2,1,0:T(8,128)} copy(f32[256,32,128]{0,1,2:T(8,128)} %convolution_bitcast_fusion.1) | data formatting | bytes 8388608 | tf_op jit(solution)/shard_map/kic,ijc->kjc/transpose | solution.py:96
  351.0 0.2 reduce-scatter.9.cloned.1.call-start
  351.2 7.8 %all-gather.6.cloned.1.call-done = bf16[256,32,128]{2,1,0:T(8,128)(2,1)} async-done(((bf16[64,32,128]{2,1,0:T(8,128)(2,1)}), bf16[256,32,128]{2,1,0:T(8,128)(2,1)}) %all-gather.6.cloned.1.call-update) | async-done | bytes 2097168 | tf_op jit(solution)/shard_map/all_gather | solution.py:87
  359.0 4.9 copy.73
  364.0 6.8 %convolution_bitcast_fusion = f32[256,64,128]{0,1,2:T(8,128)} fusion(bf16[64,32,128]{0,1,2:T(8,128)(2,1)S(1)} %copy.72, bf16[256,32,128]{0,1,2:T(8,128)(2,1)} %copy.73), kind=kOutput, calls=%fused_computation.23 | convolution fusion | flops 134217728 | bytes 11010048 | tf_op jit(solution)/shard_map/kjc,ijc->kic/dot_general | solution.py:89
  370.8 8.9 %copy.74 = f32[256,64,128]{2,1,0:T(8,128)} copy(f32[256,64,128]{0,1,2:T(8,128)} %convolution_bitcast_fusion) | data formatting | bytes 16777216 | tf_op jit(solution)/shard_map/kjc,ijc->kic/transpose | solution.py:89
  379.8 0.9 copy-done.5
  380.7 0.4 convolution_bitcast_fusion.2
  381.1 40.1 %psum.7 = f32[128,8]{0,1:T(8,128)} all-reduce(f32[128,8]{0,1:T(8,128)S(1)} %convolution_bitcast_fusion.2), channel_id=1, replica_groups=mesh['seq'=8,'res'=4] {'seq','res'}, use_global_device_ids=true, to_apply=%region_7.8 | all-reduce | flops 1024 | bytes 8192 | tf_op jit(solution)/shard_map/psum | solution.py:83
  421.2 2.1 convert_element_type.37
  423.3 136.5 %reduce-scatter.9.cloned.1.call-done = f32[32,64,128]{2,1,0:T(8,128)} async-done(((f32[256,64,128]{2,1,0:T(8,128)}), f32[32,64,128]{2,1,0:T(8,128)}) %reduce-scatter.9.cloned.1.call-update) | async-done | bytes 1048592 | tf_op jit(solution)/shard_map/reduce_scatter | solution.py:88
  559.8 2.1 convert_element_type.36
  (67 shorter events, 1.1 us)
Async XLA Ops:
  7.2 1.0 copy-start
  7.2 61.7 %all-gather.4.cloned.1.call-start = ((), (), s32[]{:S(2)}) async-start(), calls=%async_computation.4 | async-start | bytes 2621440 | tf_op jit(solution)/shard_map/all_gather | solution.py:30
  45.2 98.0 %reduce-scatter.5.cloned.1.call-start = ((), (), s32[]{:S(2)}) async-start(), calls=%async_computation.5 | async-start | bytes 2621440 | tf_op jit(solution)/shard_map/reduce_scatter | solution.py:78
  45.3 26.5 %copy-start.3 = (bf16[2,256,256]{2,1,0:T(8,128)(2,1)S(1)}, bf16[2,256,256]{2,1,0:T(8,128)(2,1)}, u32[]{:S(2)}) copy-start(bf16[2,256,256]{2,1,0:T(8,128)(2,1)} %param.11) | copy-start | bytes 786436
  45.3 26.5 %copy-start.6 = (s32[256]{0:T(256)S(1)}, s32[256]{0:T(256)}, u32[]{:S(2)}) copy-start(s32[256]{0:T(256)} %param.15) | copy-start | bytes 3076
  75.2 1.6 copy-start.2
  76.8 4.0 copy-start.1
  80.8 4.6 copy-start.8
  85.4 2.9 copy-start.9
  85.4 3.6 copy-start.10
  85.5 3.6 copy-start.12
  89.0 0.7 copy-start.11
  89.1 0.8 copy-start.13
  93.2 1.6 copy-start.2
  94.9 4.0 copy-start.1
  98.9 5.2 copy-start.8
  104.1 2.9 copy-start.9
  104.1 3.6 copy-start.10
  104.2 3.6 copy-start.12
  107.8 0.7 copy-start.11
  107.8 0.8 copy-start.13
  111.6 34.1 %copy-start.4 = (bf16[32,64,128]{2,1,0:T(8,128)(2,1)S(1)}, bf16[32,64,128]{2,1,0:T(8,128)(2,1)}, u32[]{:S(2)}) copy-start(bf16[32,64,128]{2,1,0:T(8,128)(2,1)} %param.18) | copy-start | bytes 1572868
  111.6 98.9 %reduce-scatter.7.cloned.1.call-start = ((), (), s32[]{:S(2)}) async-start(), calls=%async_computation.6 | async-start | bytes 1179648 | tf_op jit(solution)/shard_map/reduce_scatter | solution.py:79
  145.7 65.9 %copy-start.7 = (bf16[128,8]{0,1:T(8,128)(2,1)S(1)}, bf16[128,8]{0,1:T(8,128)(2,1)}, u32[]{:S(2)}) copy-start(bf16[128,8]{0,1:T(8,128)(2,1)} %param.17) | copy-start | bytes 6148
  145.7 191.1 %all-gather.8.cloned.1.call-start = ((), (), s32[]{:S(2)}) async-start(), calls=%async_computation.9 | async-start | bytes 9437184 | tf_op jit(solution)/shard_map/all_gather | solution.py:94
  148.3 210.8 %all-gather.6.cloned.1.call-start = ((), (), s32[]{:S(2)}) async-start(), calls=%async_computation.7 | async-start | bytes 2621440 | tf_op jit(solution)/shard_map/all_gather | solution.py:87
  148.9 272.4 %reduce-scatter.11.cloned.1.call-start = ((), (), s32[]{:S(2)}) async-start(), calls=%async_computation.10 | async-start | bytes 5242880 | tf_op jit(solution)/shard_map/reduce_scatter | solution.py:95
  351.0 208.8 %reduce-scatter.9.cloned.1.call-start = ((), (), s32[]{:S(2)}) async-start(), calls=%async_computation.8 | async-start | bytes 9437184 | tf_op jit(solution)/shard_map/reduce_scatter | solution.py:88
  379.7 1.0 copy-start.5
Sparse Core Ops, SparseCore 0:
  45.3 23.4 all-gather.3
  111.8 31.4 reduce-scatter.4
  147.0 63.4 reduce-scatter.6
  212.4 124.3 all-gather.7
  338.2 20.7 all-gather.5
  361.4 45.1 reduce-scatter.10
  410.7 149.0 reduce-scatter.8
where the time goes:
time: 570 us; the launch traced here: 569 us
  waiting for transfers between devices  384 us (67%)
  blocking collectives  74.7 us (13%)
  local copies, waits for them, and re-layouts  45.6 us (8%)
  matrix products  32.7 us (6%)
  other arithmetic  16.6 us (3%)
  between operations  14.2 us (2%)
    reduce_scatter x1, waiting for transfers between devices, shards(): lax.psum_scatter(jnp.einsum('kjc,ijc->kic', right_all, pair_grad, preferr...  136 us
    all_gather x1, waiting for transfers between devices, shards(): left_all = lax.all_gather(left_operand_input, 'seq', axis=0, tiled=True)  123 us
    reduce_scatter x1, waiting for transfers between devices, shards(): lax.psum_scatter(row_sum, 'seq', scatter_dimension=2, tiled=True)  61.6 us
    psum x1, blocking collectives, shards(): d_bias_weight = lax.psum(weight_term, ('seq', 'res'))  40.1 us
    all_gather x1, blocking collectives, shards(): bias_rows = lax.all_gather(bias_local, 'seq', axis=2, tiled=True)  34.6 us
    reduce_scatter x1, waiting for transfers between devices, shards(): lax.psum_scatter(bias_part, 'res', scatter_dimension=1, tiled=True)  31.5 us
    all_gather x1, waiting for transfers between devices, shards(): bias = lax.all_gather(bias_rows, 'res', axis=1, tiled=True)  23.5 us
  transfers between devices with their start and end apart: 7, of which 6 were waited for; matrix products, arithmetic and copies ran while one was open for 8% of the time, Pallas kernels for 0%

commit v1 on v0

v1 whole, which is shorter than its diff:
```python
import functools
import math

import jax
import jax.numpy as jnp
from jax import lax
from jax.experimental import pallas as pl
from jax.experimental.pallas import tpu as pltpu
from jax.sharding import PartitionSpec as P

HEADS = 8
HEAD_DIM = 32
BIG_NEGATIVE = -1e30
BOTH = ("seq", "res")
NT = (((1,), (1,)), ((), ()))
TN = (((0,), (0,)), ((), ()))

f32 = jnp.float32
bf16 = jnp.bfloat16


def attention_kernel(
    n_seq, n_res, x_ref, bias_ref, chain_row_ref, chain_col_ref, grads_ref, share_ref, masked, total
):
    step = pl.program_id(0)
    heads, residues, _ = masked.shape
    cols, rows = residues // n_seq, residues // n_res
    width = heads * HEAD_DIM
    scale = HEAD_DIM**-0.5

    @pl.when(step == 0)
    def _():
        for h in range(heads):
            for a in range(n_seq):
                band = jnp.concatenate(
                    [bias_ref[a * n_res + b, :, h * rows : (h + 1) * rows] for b in range(n_res)],
                    axis=-1,
                )
                allowed = chain_col_ref[a * cols : (a + 1) * cols, :] == chain_row_ref[...]
                masked[h, a * cols : (a + 1) * cols, :] = jnp.where(allowed, band, BIG_NEGATIVE)
        total[...] = jnp.zeros_like(total)

    query_parts, key_parts, value_parts = [], [], []
    for h in range(heads):
        q, k, v, g = [
            x_ref[0, :, t * width + h * HEAD_DIM : t * width + (h + 1) * HEAD_DIM] for t in range(4)
        ]
        scores = lax.dot_general(k, q, NT, preferred_element_type=f32) * scale + masked[h]
        top = jnp.max(scores, axis=0, keepdims=True)
        expo = jnp.exp(scores - top)
        probs = expo * (1.0 / jnp.sum(expo, axis=0, keepdims=True))
        dprobs = lax.dot_general(v, g, NT, preferred_element_type=f32)
        dscores = probs * (dprobs - jnp.sum(probs * dprobs, axis=0, keepdims=True))
        total[h] += dscores
        dscores_b = dscores.astype(bf16)
        query_parts.append(lax.dot_general(dscores_b, k, TN, preferred_element_type=f32) * scale)
        key_parts.append(jnp.dot(dscores_b, q, preferred_element_type=f32) * scale)
        value_parts.append(jnp.dot(probs.astype(bf16), g, preferred_element_type=f32))
    grads_ref[0] = jnp.concatenate(query_parts + key_parts + value_parts, axis=-1).astype(bf16)

    @pl.when(step == pl.num_programs(0) - 1)
    def _():
        for a in range(n_seq):
            for b in range(n_res):
                share_ref[a * n_res + b] = jnp.concatenate(
                    [
                        total[h, a * cols : (a + 1) * cols, b * rows : (b + 1) * rows]
                        for h in range(heads)
                    ],
                    axis=-1,
                ).astype(bf16)


def triangle_kernel(
    n_seq, n_res, bias_grad_ref, weight_ref, left_ref, right_ref, d_left_ref, d_right_ref, flat, turned
):
    heads, residues, _ = flat.shape
    groups = bias_grad_ref.shape[1]
    held = heads // groups
    cols, rows = residues // n_seq, residues // n_res
    for h in range(heads):
        group, place = h // held, h % held
        for a in range(n_seq):
            turned[h, a * cols : (a + 1) * cols, :] = jnp.concatenate(
                [
                    bias_grad_ref[a * n_res + b, group, :, place * rows : (place + 1) * rows]
                    for b in range(n_res)
                ],
                axis=-1,
            )
        flat[h] = turned[h].astype(f32).T.astype(bf16)
    for operand, grad, out in ((right_ref, flat, d_left_ref), (left_ref, turned, d_right_ref)):
        for k in range(operand.shape[0]):
            row = jnp.zeros(operand.shape[1:], f32)
            for h in range(heads):
                product = jnp.dot(grad[h], operand[k], preferred_element_type=f32)
                row += product * weight_ref[h : h + 1, :]
            out[k] = row.astype(bf16)


def shards(
    n_seq,
    n_res,
    alignment_query,
    alignment_key,
    attended_vectors,
    attended_cotangent,
    chain_index_per_residue,
    pair,
    pair_bias_matrix,
    left_operand_input,
    right_operand_input,
):
    own, residues, channels = alignment_query.shape
    devices = n_seq * n_res
    groups = math.gcd(HEADS, n_res)
    held = HEADS // groups
    width = held * HEAD_DIM
    rows, cols, pair_channels = pair.shape
    sequences = own * groups
    index_groups = None
    if groups != n_res:
        index_groups = [list(range(s, s + groups)) for s in range(0, n_res, groups)]

    def over_heads(x):
        return lax.all_to_all(x, "res", 0, 0, axis_index_groups=index_groups, tiled=True)

    bias = jnp.einsum("ijc,ch->hij", pair, pair_bias_matrix, preferred_element_type=f32)
    bias = bias.reshape(groups, held, rows, cols).transpose(0, 3, 1, 2)
    bias = bias.reshape(groups, cols, held * rows)
    bias = jnp.broadcast_to(bias[None], (devices // groups, groups, cols, held * rows))
    bias = lax.all_to_all(
        bias.reshape(devices, cols, held * rows), BOTH, 0, 0, tiled=True
    )

    arrays = jnp.stack([alignment_query, alignment_key, attended_vectors, attended_cotangent])
    arrays = arrays.reshape(4, own, residues, groups, width).transpose(3, 1, 2, 0, 4)
    arrays = over_heads(arrays.reshape(sequences, residues, 4 * width))

    left_rows = lax.all_to_all(left_operand_input, "res", 0, 1, tiled=True)
    left_rows = lax.ppermute(
        left_rows, BOTH, [(d, (d % n_seq) * n_res + d // n_seq) for d in range(devices)]
    )
    right_rows = lax.all_to_all(right_operand_input, "seq", 0, 1, tiled=True)
    right_rows = lax.ppermute(
        right_rows, BOTH, [((d % n_seq) * n_res + d // n_seq, d) for d in range(devices)]
    )

    whole = lambda shape: pl.BlockSpec(shape, lambda s: (0,) * len(shape))
    grads, share = pl.pallas_call(
        functools.partial(attention_kernel, n_seq, n_res),
        grid=(sequences,),
        in_specs=[
            pl.BlockSpec((1, residues, 4 * width), lambda s: (s, 0, 0)),
            whole(bias.shape),
            whole((1, residues)),
            whole((residues, 1)),
        ],
        out_specs=[
            pl.BlockSpec((1, residues, 3 * width), lambda s: (s, 0, 0)),
            whole(bias.shape),
        ],
        out_shape=[
            jax.ShapeDtypeStruct((sequences, residues, 3 * width), bf16),
            jax.ShapeDtypeStruct(bias.shape, bf16),
        ],
        scratch_shapes=[pltpu.VMEM((held, residues, residues), f32)] * 2,
        compiler_params=pltpu.CompilerParams(vmem_limit_bytes=32 * 1024 * 1024),
        name="attention",
    )(
        arrays,
        bias,
        chain_index_per_residue.reshape(1, residues),
        chain_index_per_residue.reshape(residues, 1),
    )

    share = lax.all_to_all(share, BOTH, 0, 0, tiled=True)
    block = jnp.sum(
        share.astype(f32).reshape(devices // groups, groups, cols, held * rows), axis=0
    )
    bias_grad = jnp.broadcast_to(block.astype(bf16)[None], (devices,) + block.shape)
    bias_grad = lax.all_to_all(bias_grad, BOTH, 0, 0, tiled=True)

    own_grad = block.reshape(groups, cols, held, rows).transpose(0, 2, 3, 1)
    own_grad = own_grad.reshape(HEADS, rows, cols)
    weight_term = jnp.einsum(
        "ijc,hij->ch", pair.astype(f32), own_grad, precision=lax.Precision.HIGHEST
    )
    d_bias_weight = lax.psum(weight_term, BOTH)

    share_rows = left_rows.shape
    d_left, d_right = pl.pallas_call(
        functools.partial(triangle_kernel, n_seq, n_res),
        out_shape=[jax.ShapeDtypeStruct(share_rows, bf16)] * 2,
        scratch_shapes=[pltpu.VMEM((HEADS, residues, residues), bf16)] * 2,
        compiler_params=pltpu.CompilerParams(vmem_limit_bytes=32 * 1024 * 1024),
        name="triangle",
    )(bias_grad, pair_bias_matrix.astype(f32).T, left_rows, right_rows)
    d_left = lax.all_to_all(d_left, "res", 1, 0, tiled=True)
    d_right = lax.all_to_all(d_right, "seq", 1, 0, tiled=True)

    grads = over_heads(grads).reshape(groups, own, residues, 3, width)
    grads = grads.transpose(3, 1, 2, 0, 4).reshape(3, own, residues, channels)
    return (grads[0], grads[1], grads[2], d_bias_weight, d_left, d_right)


def solution(mesh):
    placed = (
        P(BOTH, None, None),
        P(BOTH, None, None),
        P(BOTH, None, None),
        P(BOTH, None, None),
        P(),
        P("res", "seq", None),
        P(),
        P("seq", "res", None),
        P("res", "seq", None),
    )
    return jax.shard_map(
        functools.partial(shards, mesh.shape["seq"], mesh.shape["res"]),
        mesh=mesh,
        in_specs=placed,
        out_specs=(
            P(BOTH, None, None),
            P(BOTH, None, None),
            P(BOTH, None, None),
            P(),
            P("seq", "res", None),
            P("res", "seq", None),
        ),
        check_vma=False,
    )
```

time: 570 us -> 251 us (0.44)
  waiting for transfers between devices: 384 us -> 76 us
  starting transfers between devices: 0.47 us -> 65.9 us
  matrix products: 32.7 us -> 0.93 us
  local copies, waits for them, and re-layouts: 45.6 us -> 16.1 us
  other arithmetic: 16.6 us -> 0.18 us
  Pallas kernels: 0 us -> 15 us
  between operations: 14.2 us -> 0.92 us
    reduce_scatter x4 -> x0, waiting for transfers between devices: 230 us -> none  [the longest x1 136 us: shards(): lax.psum_scatter(jnp.einsum('kjc,ijc->kic', right_all, pair_grad, preferr...]
    all_gather x3 -> x0, waiting for transfers between devices: 154 us -> none  [the longest x1 123 us: shards(): left_all = lax.all_gather(left_operand_input, 'seq', axis=0, tiled=True)]
    all_to_all x0 -> x7, waiting for transfers between devices: none -> 76 us  [the longest x2 28.6 us: over_heads(): lax.all_to_all(x, 'res', 0, 0, axis_index_groups=index_groups, tiled=True)]
    all_to_all x0 -> x7, starting transfers between devices: none -> 64.5 us  [the longest x1 42.5 us: shards(): d_left = lax.all_to_all(d_left, 'res', 1, 0, tiled=True)]
    all_to_all x0 -> x2, blocking collectives: none -> 35 us  [the longest x1 21 us: shards(): lax.all_to_all(bias.reshape(devices, cols, held * rows), BOTH, 0, 0, tile...]
    all_gather x1 -> x0, blocking collectives: 34.6 us -> none  [shards(): bias_rows = lax.all_gather(bias_local, 'seq', axis=2, tiled=True)]
    dot_general x14 -> x1, matrix products: 31.5 us -> 0.42 us  [shards(): jnp.einsum('ijc,hij->ch', pair.astype(f32), own_grad, precision=lax.Preci...]
    pallas_call x0 -> x2, Pallas kernels: none -> 15 us  [the longest x1 10.1 us: shards(): pl.pallas_call(functools.partial(attention_kernel, n_seq, n_res), grid=(s...]
  transfers between devices with their start and end apart: 7 -> 9, of which waited for: 6 -> 5; matrix products, arithmetic and copies ran while one was open for 8% -> 4% of each run, Pallas kernels for 0% -> 6%
where the time goes in v1:
time: 251 us; the launch traced here: 250 us
  waiting for transfers between devices  76 us (30%)
  blocking collectives  75.2 us (30%)
  starting transfers between devices  65.9 us (26%)
  local copies, waits for them, and re-layouts  16.1 us (6%)
  Pallas kernels  15 us (6%)
    all_to_all x1, starting transfers between devices, shards(): d_left = lax.all_to_all(d_left, 'res', 1, 0, tiled=True)  42.5 us
    psum x1, blocking collectives, shards(): d_bias_weight = lax.psum(weight_term, BOTH)  40.2 us
    all_to_all x2, waiting for transfers between devices, over_heads(): lax.all_to_all(x, 'res', 0, 0, axis_index_groups=index_groups, tiled=True)  28.6 us
    all_to_all x1, waiting for transfers between devices, shards(): bias_grad = lax.all_to_all(bias_grad, BOTH, 0, 0, tiled=True)  25 us
    all_to_all x1, blocking collectives, shards(): lax.all_to_all(bias.reshape(devices, cols, held * rows), BOTH, 0, 0, tile...  21 us
    all_to_all x1, waiting for transfers between devices, shards(): right_rows = lax.all_to_all(right_operand_input, 'seq', 0, 1, tiled=True)  14.7 us
    all_to_all x1, blocking collectives, shards(): share = lax.all_to_all(share, BOTH, 0, 0, tiled=True)  14 us
    pallas_call x1, Pallas kernels, shards(): pl.pallas_call(functools.partial(attention_kernel, n_seq, n_res), grid=(s...  10.1 us
  transfers between devices with their start and end apart: 9, of which 5 were waited for; matrix products, arithmetic and copies ran while one was open for 4% of the time, Pallas kernels for 6%

profile of v1, /device:TPU:0, one launch (start us, length us, event | category | flops | bytes accessed | tf_op | source)
XLA Modules:
  0.0 250.2 jit_solution(12713894742647005280)
XLA Ops:
  0.6 0.0 copy-start
  0.6 0.0 copy-start.2
  0.7 1.2 copy.55
  1.8 0.0 copy-done.2
  1.8 0.0 copy-start.3
  1.8 0.1 copy.54
  2.0 0.8 copy-done.3
  2.8 0.0 copy-start.4
  2.8 0.1 copy.53
  2.9 0.8 copy-done.4
  3.7 0.1 copy.52
  3.9 0.1 maximum_bitcast_fusion
  4.0 0.1 copy.56
  4.1 1.3 copy.57
  5.4 0.0 copy-start.5
  5.4 4.3 %all-to-all-start = ((bf16[8,256,256]{2,1,0:T(8,128)(2,1)}), bf16[8,256,256]{2,1,0:T(8,128)(2,1)S(1)}, u32[]{:S(2)}, u32[]{:S(2)}) async-start(bf16[8,256,256]{2,1,0:T(8,128)(2,1)} %copy.57), calls=%async_computation | async-start | bytes 2097152 | tf_op jit(solution)/shard_map/all_to_all | solution.py:126
  9.8 0.0 copy-done
  9.8 0.0 copy-done.5
  9.8 0.5 fusion.1
  10.3 0.2 broadcast_in_dim.6
  10.5 13.8 %all-to-all-done.x_ref = bf16[8,256,256]{2,1,0:T(8,128)(2,1)S(1)} async-done(((bf16[8,256,256]{2,1,0:T(8,128)(2,1)}), bf16[8,256,256]{2,1,0:T(8,128)(2,1)S(1)}, u32[]{:S(2)}, u32[]{:S(2)}) %all-to-all-start) | async-done | bytes 1048608 | tf_op jit(solution)/shard_map/all_to_all | solution.py:126
  24.3 21.0 %all_to_all.97.bias_ref = f32[32,32,128]{2,1,0:T(8,128)S(1)} all-to-all(f32[32,32,128]{2,1,0:T(8,128)S(1)} %bitcast.59), channel_id=1, replica_groups=mesh['seq'=8,'res'=4] {'seq','res'}, dimensions={0} | all-to-all | bytes 1048576 | tf_op jit(solution)/shard_map/all_to_all | solution.py:132
  45.3 4.1 %all-to-all-start.5 = ((bf16[32,64,128]{2,1,0:T(8,128)(2,1)}), bf16[32,64,128]{2,1,0:T(8,128)(2,1)}, u32[]{:S(2)}, u32[]{:S(2)}) async-start(bf16[32,64,128]{2,1,0:T(8,128)(2,1)} %param.16), calls=%async_computation.5 | async-start | bytes 1048576 | tf_op jit(solution)/shard_map/all_to_all | solution.py:140
  49.4 0.0 copy-start.1
  49.5 0.7 copy-done.1
  50.1 0.1 copy.60.chain_col_ref
  50.3 10.1 %attention.1 = (bf16[8,256,192]{2,1,0:T(8,128)(2,1)S(1)}, bf16[32,32,128]{2,1,0:T(8,128)(2,1)S(1)}) custom-call(bf16[8,256,256]{2,1,0:T(8,128)(2,1)S(1)} %all-to-all-done.x_ref, f32[32,32,128]{2,1,0:T(8,128)S(1)} %all_to_all.97.bias_ref, s32[1,256]{1,0:T(1,128)S(1)} %bitcast.53, s32[256,1]{1,0:T(8,128)S(1)} %copy.60.chain_col_ref), custom_call_target="tpu_custom_call" | custom-call | tf_op jit(solution)/shard_map/attention/pallas_call | solution.py:150
  60.4 0.0 all-to-all-done.5
  60.4 14.0 %all_to_all.98 = bf16[32,32,128]{2,1,0:T(8,128)(2,1)S(1)} all-to-all(bf16[32,32,128]{2,1,0:T(8,128)(2,1)S(1)} %get-tuple-element.11), channel_id=1, replica_groups=mesh['seq'=8,'res'=4] {'seq','res'}, dimensions={0} | all-to-all | bytes 524288 | tf_op jit(solution)/shard_map/all_to_all | solution.py:177
  74.4 3.5 %all-to-all-start.6 = ((bf16[64,32,128]{2,1,0:T(8,128)(2,1)}), bf16[64,32,128]{2,1,0:T(8,128)(2,1)S(1)}, u32[]{:S(2)}, u32[]{:S(2)}) async-start(bf16[64,32,128]{2,1,0:T(8,128)(2,1)} %param.17), calls=%async_computation.6 | async-start | bytes 1048576 | tf_op jit(solution)/shard_map/all_to_all | solution.py:144
  77.9 14.7 %all-to-all-done.6 = bf16[64,32,128]{2,1,0:T(8,128)(2,1)S(1)} async-done(((bf16[64,32,128]{2,1,0:T(8,128)(2,1)}), bf16[64,32,128]{2,1,0:T(8,128)(2,1)S(1)}, u32[]{:S(2)}, u32[]{:S(2)}) %all-to-all-start.6) | async-done | bytes 524320 | tf_op jit(solution)/shard_map/all_to_all | solution.py:144
  92.6 1.2 broadcast_in_dim.15
  93.9 3.1 %all-to-all-start.4 = ((bf16[32,4,32,128]{3,2,1,0:T(8,128)(2,1)}), bf16[32,4,32,128]{3,2,1,0:T(8,128)(2,1)S(1)}, u32[]{:S(2)}, u32[]{:S(2)}) async-start(bf16[32,4,32,128]{3,2,1,0:T(8,128)(2,1)} %broadcast_in_dim.15), calls=%async_computation.4 | async-start | bytes 2097152 | tf_op jit(solution)/shard_map/all_to_all | solution.py:182
  96.9 1.3 copy.61
  98.2 25.0 %all-to-all-done.4.bias_grad_ref = bf16[32,4,32,128]{3,2,1,0:T(8,128)(2,1)S(1)} async-done(((bf16[32,4,32,128]{3,2,1,0:T(8,128)(2,1)}), bf16[32,4,32,128]{3,2,1,0:T(8,128)(2,1)S(1)}, u32[]{:S(2)}, u32[]{:S(2)}) %all-to-all-start.4) | async-done | bytes 1048608 | tf_op jit(solution)/shard_map/all_to_all | solution.py:182
  123.2 3.5 %all-to-all-start.2 = ((bf16[8,256,192]{1,2,0:T(8,128)(2,1)}), bf16[8,256,192]{1,2,0:T(8,128)(2,1)S(1)}, u32[]{:S(2)}, u32[]{:S(2)}) async-start(bf16[8,256,192]{1,2,0:T(8,128)(2,1)} %copy.61), calls=%async_computation.2 | async-start | bytes 1572864 | tf_op jit(solution)/shard_map/all_to_all | solution.py:126
  126.7 1.1 copy.67
  127.7 0.7 collective-permute-start
  128.5 0.7 collective-permute-start.1
  129.2 0.0 collective-permute-done.left_ref
  129.2 0.0 collective-permute-done.1.right_ref
  129.2 4.9 %triangle.1 = (bf16[8,256,128]{2,1,0:T(8,128)(2,1)S(1)}, bf16[8,256,128]{2,1,0:T(8,128)(2,1)S(1)}) custom-call(bf16[32,4,32,128]{3,2,1,0:T(8,128)(2,1)S(1)} %all-to-all-done.4.bias_grad_ref, f32[8,128]{1,0:T(8,128)S(1)} %convert_bitcast_fusion.weight_ref, bf16[8,256,128]{2,1,0:T(8,128)(2,1)S(1)} %collective-permute-done.left_ref, ...), custom_call_target="tpu_custom_call" | custom-call | tf_op jit(solution)/shard_map/triangle/pallas_call | solution.py:192
  134.1 1.1 copy.69
  135.2 14.8 %all-to-all-done.2 = bf16[8,256,192]{1,2,0:T(8,128)(2,1)S(1)} async-done(((bf16[8,256,192]{1,2,0:T(8,128)(2,1)}), bf16[8,256,192]{1,2,0:T(8,128)(2,1)S(1)}, u32[]{:S(2)}, u32[]{:S(2)}) %all-to-all-start.2) | async-done | bytes 786464 | tf_op jit(solution)/shard_map/all_to_all | solution.py:126
  150.1 42.5 %all-to-all-start.7 = ((bf16[8,256,128]{2,0,1:T(8,128)(2,1)}), bf16[8,256,128]{2,0,1:T(8,128)(2,1)S(1)}, u32[]{:S(2)}, u32[]{:S(2)}) async-start(bf16[8,256,128]{2,0,1:T(8,128)(2,1)} %copy.69), calls=%async_computation.7 | async-start | bytes 1048576 | tf_op jit(solution)/shard_map/all_to_all | solution.py:199
  192.6 1.1 copy.71
  193.7 7.7 %all-to-all-done.7 = bf16[8,256,128]{2,0,1:T(8,128)(2,1)S(1)} async-done(((bf16[8,256,128]{2,0,1:T(8,128)(2,1)}), bf16[8,256,128]{2,0,1:T(8,128)(2,1)S(1)}, u32[]{:S(2)}, u32[]{:S(2)}) %all-to-all-start.7) | async-done | bytes 524320 | tf_op jit(solution)/shard_map/all_to_all | solution.py:199
  201.4 3.5 %all-to-all-start.8 = ((bf16[8,256,128]{2,0,1:T(8,128)(2,1)}), bf16[8,256,128]{2,0,1:T(8,128)(2,1)S(1)}, u32[]{:S(2)}, u32[]{:S(2)}) async-start(bf16[8,256,128]{2,0,1:T(8,128)(2,1)} %copy.71), calls=%async_computation.8 | async-start | bytes 1048576 | tf_op jit(solution)/shard_map/all_to_all | solution.py:200
  204.9 0.1 reshape.70
  205.1 0.4 convolution_bitcast_fusion
  205.5 40.2 %psum.7 = f32[128,8]{0,1:T(8,128)} all-reduce(f32[128,8]{0,1:T(8,128)S(1)} %convolution_bitcast_fusion), channel_id=1, replica_groups=mesh['seq'=8,'res'=4] {'seq','res'}, use_global_device_ids=true, to_apply=%region_1.0 | all-reduce | flops 1024 | bytes 8192 | tf_op jit(solution)/shard_map/psum | solution.py:189
  245.7 0.1 fusion.4
  245.8 0.8 copy.73
  246.7 0.8 copy.74
  247.6 0.8 copy.75
  248.4 0.9 copy.70
  249.3 0.0 all-to-all-done.8
  249.3 0.9 copy.72
  (10 shorter events, 0.2 us)
Async XLA Ops:
  0.6 9.1 %copy-start = (bf16[64,32,128]{2,1,0:T(8,128)(2,1)S(1)}, bf16[64,32,128]{2,1,0:T(8,128)(2,1)}, u32[]{:S(2)}) copy-start(bf16[64,32,128]{2,1,0:T(8,128)(2,1)} %param.14) | copy-start | bytes 1572868
  0.6 1.2 copy-start.2
  1.8 1.0 copy-start.3
  2.8 0.9 copy-start.4
  5.4 4.3 %copy-start.5 = (bf16[128,8]{0,1:T(8,128)(2,1)S(1)}, bf16[128,8]{0,1:T(8,128)(2,1)}, u32[]{:S(2)}) copy-start(bf16[128,8]{0,1:T(8,128)(2,1)} %param.15) | copy-start | bytes 6148
  5.4 18.8 %all-to-all-start = ((bf16[8,256,256]{2,1,0:T(8,128)(2,1)}), bf16[8,256,256]{2,1,0:T(8,128)(2,1)S(1)}, u32[]{:S(2)}, u32[]{:S(2)}) async-start(bf16[8,256,256]{2,1,0:T(8,128)(2,1)} %copy.57), calls=%async_computation | async-start | bytes 2097152 | tf_op jit(solution)/shard_map/all_to_all | solution.py:126
  45.3 15.1 %all-to-all-start.5 = ((bf16[32,64,128]{2,1,0:T(8,128)(2,1)}), bf16[32,64,128]{2,1,0:T(8,128)(2,1)}, u32[]{:S(2)}, u32[]{:S(2)}) async-start(bf16[32,64,128]{2,1,0:T(8,128)(2,1)} %param.16), calls=%async_computation.5 | async-start | bytes 1048576 | tf_op jit(solution)/shard_map/all_to_all | solution.py:140
  49.4 0.7 copy-start.1
  74.4 18.3 %all-to-all-start.6 = ((bf16[64,32,128]{2,1,0:T(8,128)(2,1)}), bf16[64,32,128]{2,1,0:T(8,128)(2,1)S(1)}, u32[]{:S(2)}, u32[]{:S(2)}) async-start(bf16[64,32,128]{2,1,0:T(8,128)(2,1)} %param.17), calls=%async_computation.6 | async-start | bytes 1048576 | tf_op jit(solution)/shard_map/all_to_all | solution.py:144
  93.9 29.3 %all-to-all-start.4 = ((bf16[32,4,32,128]{3,2,1,0:T(8,128)(2,1)}), bf16[32,4,32,128]{3,2,1,0:T(8,128)(2,1)S(1)}, u32[]{:S(2)}, u32[]{:S(2)}) async-start(bf16[32,4,32,128]{3,2,1,0:T(8,128)(2,1)} %broadcast_in_dim.15), calls=%async_computation.4 | async-start | bytes 2097152 | tf_op jit(solution)/shard_map/all_to_all | solution.py:182
  123.2 26.9 %all-to-all-start.2 = ((bf16[8,256,192]{1,2,0:T(8,128)(2,1)}), bf16[8,256,192]{1,2,0:T(8,128)(2,1)S(1)}, u32[]{:S(2)}, u32[]{:S(2)}) async-start(bf16[8,256,192]{1,2,0:T(8,128)(2,1)} %copy.61), calls=%async_computation.2 | async-start | bytes 1572864 | tf_op jit(solution)/shard_map/all_to_all | solution.py:126
  127.7 1.5 collective-permute-start
  128.5 0.7 collective-permute-start.1
  150.1 51.4 %all-to-all-start.7 = ((bf16[8,256,128]{2,0,1:T(8,128)(2,1)}), bf16[8,256,128]{2,0,1:T(8,128)(2,1)S(1)}, u32[]{:S(2)}, u32[]{:S(2)}) async-start(bf16[8,256,128]{2,0,1:T(8,128)(2,1)} %copy.69), calls=%async_computation.7 | async-start | bytes 1048576 | tf_op jit(solution)/shard_map/all_to_all | solution.py:199
  201.4 47.9 %all-to-all-start.8 = ((bf16[8,256,128]{2,0,1:T(8,128)(2,1)}), bf16[8,256,128]{2,0,1:T(8,128)(2,1)S(1)}, u32[]{:S(2)}, u32[]{:S(2)}) async-start(bf16[8,256,128]{2,0,1:T(8,128)(2,1)} %copy.71), calls=%async_computation.8 | async-start | bytes 1048576 | tf_op jit(solution)/shard_map/all_to_all | solution.py:200

commit v2 on v1

v2 whole, which is shorter than its diff:
```python
import functools
import math

import jax
import jax.numpy as jnp
from jax import lax
from jax.experimental import pallas as pl
from jax.experimental.pallas import tpu as pltpu
from jax.sharding import PartitionSpec as P

HEADS = 8
HEAD_DIM = 32
BIG_NEGATIVE = -1e30
BOTH = ("seq", "res")
NT = (((1,), (1,)), ((), ()))
TN = (((0,), (0,)), ((), ()))

f32 = jnp.float32
bf16 = jnp.bfloat16


def attention_kernel(
    n_seq, n_res, groups, bias_ref, chain_ref, *refs
):
    arrays, grads = refs[:groups], refs[groups : 2 * groups]
    share_ref, masked, total = refs[2 * groups :]
    heads, residues, _ = masked.shape
    cols, rows = residues // n_seq, residues // n_res
    width = heads * HEAD_DIM
    scale = HEAD_DIM**-0.5

    chain_row = chain_ref[...].astype(f32)
    chain_col = jnp.broadcast_to(chain_row, (8, residues)).T[:, :1]
    for h in range(heads):
        for a in range(n_seq):
            band = jnp.concatenate(
                [bias_ref[a * n_res + b, :, h * rows : (h + 1) * rows] for b in range(n_res)],
                axis=-1,
            )
            allowed = chain_col[a * cols : (a + 1) * cols] == chain_row
            masked[h, a * cols : (a + 1) * cols, :] = jnp.where(allowed, band, BIG_NEGATIVE)
    total[...] = jnp.zeros_like(total)

    def sequence(x_ref, n):
        query_parts, key_parts, value_parts = [], [], []
        for h in range(heads):
            q, k, v, g = [
                x_ref[n, :, t * width + h * HEAD_DIM : t * width + (h + 1) * HEAD_DIM]
                for t in range(4)
            ]
            scores = lax.dot_general(k, q, NT, preferred_element_type=f32) * scale + masked[h]
            top = jnp.max(scores, axis=0, keepdims=True)
            expo = jnp.exp(scores - top)
            probs = expo * (1.0 / jnp.sum(expo, axis=0, keepdims=True))
            dprobs = lax.dot_general(v, g, NT, preferred_element_type=f32)
            dscores = probs * (dprobs - jnp.sum(probs * dprobs, axis=0, keepdims=True))
            total[h] += dscores
            dscores_b = dscores.astype(bf16)
            query_parts.append(
                lax.dot_general(dscores_b, k, TN, preferred_element_type=f32) * scale
            )
            key_parts.append(jnp.dot(dscores_b, q, preferred_element_type=f32) * scale)
            value_parts.append(jnp.dot(probs.astype(bf16), g, preferred_element_type=f32))
        return [
            jnp.concatenate(parts, axis=-1).astype(bf16)
            for parts in (query_parts, key_parts, value_parts)
        ]

    for s in range(groups):
        units = sum([sequence(arrays[s], n) for n in range(arrays[s].shape[0])], [])
        slots = grads[s].shape[0]
        each = len(units) // slots
        for n in range(slots):
            grads[s][n] = jnp.concatenate(units[n * each : (n + 1) * each], axis=-1)

    for a in range(n_seq):
        for b in range(n_res):
            share_ref[a * n_res + b] = jnp.concatenate(
                [
                    total[h, a * cols : (a + 1) * cols, b * rows : (b + 1) * rows]
                    for h in range(heads)
                ],
                axis=-1,
            ).astype(bf16)


def unpack_kernel(place_ref, *refs):
    pieces, outs, held = refs[:-4], refs[-4:-1], refs[-1]
    groups = len(pieces)
    own = outs[0].shape[0]
    slots, _, lanes = pieces[0].shape
    each = 3 * own // slots
    width = lanes // each
    for s in range(groups):
        held[s] = pieces[s][...]
    place = place_ref[0]
    for t in range(3):
        for n in range(own):
            slot, start = (3 * n + t) // each, (3 * n + t) % each * width
            outs[t][n] = jnp.concatenate(
                [held[place ^ g, slot, :, start : start + width] for g in range(groups)], axis=-1
            )


def pack_kernel(groups, n_res, scalars, chain_ref, *refs):
    arrays, (left_ref, right_ref), refs = refs[:4], refs[4:6], refs[6:]
    chain_out, outs, triangles = refs[0], refs[1 : 1 + groups], refs[1 + groups : -4]
    whole, held, loaded, sent = refs[-4:]
    place, b = scalars[0], scalars[1]
    block, rows = triangles[0].shape[1:3]
    cols = right_ref.shape[-2]
    loads = [
        pltpu.make_async_copy(x, whole.at[n], loaded.at[n]) for n, x in enumerate(arrays)
    ]
    for load in loads:
        load.start()
    copies = []
    for s in range(n_res):
        t = turn(b ^ s, n_res) * block
        copies.append((left_ref.at[pl.ds(t, block)], triangles[s].at[0]))
        for y in range(rows // cols):
            copies.append(
                (right_ref.at[y, b ^ s], triangles[s].at[1, :, y * cols : (y + 1) * cols])
            )
    copies = [pltpu.make_async_copy(x, y, sent.at[n]) for n, (x, y) in enumerate(copies)]
    for copy in copies:
        copy.start()
    chain_out[...] = chain_ref[...]
    for load in loads:
        load.wait()
    width = whole.shape[-1] // groups
    for g in range(groups):
        held[g] = jnp.concatenate(
            [whole[n, :, :, g * width : (g + 1) * width] for n in range(4)], axis=-1
        )
    for s in range(groups):
        outs[s][...] = held[place ^ s]
    for copy in copies:
        copy.wait()


def turn(b, n_res):
    return b % 2 * (n_res // 2) + b // 2


def order_kernel(scalars, *refs):
    pieces, (left_ref, chunks_ref) = refs[:-2], refs[-2:]
    rows, cols = pieces[0].shape[2], chunks_ref.shape[2]
    each = rows // cols
    for s, piece in enumerate(pieces):
        b = scalars[0] ^ s
        left_ref[:, pl.ds(pl.multiple_of(b * rows, rows), rows), :] = piece[0]
        for y in range(each):
            chunks_ref[b * each + y] = piece[1, :, y * cols : (y + 1) * cols]


def d_left_kernel(n_seq, n_res, scalars, near_ref, extra_ref, *refs):
    rights, outs = refs[:2], refs[2:-2]
    flat, right = refs[-2:]
    heads, count, residues = flat.shape
    held = heads // near_ref.shape[1]
    cols, rows = residues // n_seq, residues // n_res
    across = n_res // 2
    block = rights[0].shape[1]
    core, x = scalars[0], scalars[1]
    for part in range(2):
        where = core ^ part
        for a in range(n_seq):
            right[where, :, a * cols : (a + 1) * cols, :] = rights[part][a]
    for h in range(heads):
        group, place = h // held, h % held
        turned = jnp.concatenate(
            [
                jnp.concatenate(
                    [
                        near_ref[a * across + u, group, :, place * rows : (place + 1) * rows]
                        for u in range(across)
                    ],
                    axis=-1,
                )
                for a in range(n_seq)
            ],
            axis=0,
        )
        flat[h] = turned.astype(f32).T.astype(bf16)
    sums = outs[-1]
    for c in range(2):
        for k in range(block):
            row = jnp.zeros((count, right.shape[-1]), f32)
            for h in range(heads):
                product = jnp.dot(flat[h], right[c, k], preferred_element_type=f32)
                row += product * extra_ref[0, h : h + 1, :]
            for u in range(across):
                sums[u, c * block + k] = row[u * rows : (u + 1) * rows].astype(bf16)
    for s in range(across):
        outs[s][...] = sums[x ^ s]


def d_right_kernel(n_seq, n_res, scalars, near_ref, far_ref, extra_ref, left, out, turned):
    heads, residues, _ = turned.shape
    held = heads // near_ref.shape[1]
    cols, rows = residues // n_seq, residues // n_res
    across = n_res // 2
    block = left.shape[0]
    core = scalars[0]
    for h in range(heads):
        group, place = h // held, h % held
        for a in range(n_seq):
            band = []
            for b in range(n_res):
                piece = (
                    a * across + b // 2, group, slice(None), slice(place * rows, (place + 1) * rows)
                )
                band.append(jnp.where(core == b % 2, near_ref[piece], far_ref[piece]))
            turned[h, a * cols : (a + 1) * cols, :] = jnp.concatenate(band, axis=-1)
    for k in range(block):
        row = jnp.zeros((residues, left.shape[-1]), f32)
        for h in range(heads):
            product = jnp.dot(turned[h], left[k], preferred_element_type=f32)
            row += product * extra_ref[0, h : h + 1, :]
        for a in range(n_seq):
            out[a, k * cols : (k + 1) * cols] = row[a * cols : (a + 1) * cols].astype(bf16)
    term = extra_ref[1]
    high = term.astype(bf16).astype(f32)
    both = jnp.concatenate([high, term - high], axis=0).astype(bf16)
    for a in range(n_seq):
        out[a, block * cols :] = both


def place_kernel(inner, scalars, received_ref, *refs):
    pieces, (term_ref, left_ref, right_ref) = refs[:-3], refs[-3:]
    heads = term_ref.shape[0]
    sources, size, _ = received_ref.shape
    cols = right_ref.shape[1]
    block = right_ref.shape[0] // sources
    total = jnp.zeros_like(term_ref)
    for a in range(sources):
        both = received_ref[a, block * cols :].astype(f32)
        total += both[:heads] + both[heads:]
        p = a % inner * (sources // inner) + a // inner
        for k in range(block):
            right_ref[p * block + k] = received_ref[a, k * cols : (k + 1) * cols]
    term_ref[...] = total
    size = pieces[0].shape[0]
    for s, piece in enumerate(pieces):
        left_ref[pl.ds(pl.multiple_of((scalars[0] ^ s) * size, size), size)] = piece[...]


def shards(
    n_seq,
    n_res,
    alignment_query,
    alignment_key,
    attended_vectors,
    attended_cotangent,
    chain_index_per_residue,
    pair,
    pair_bias_matrix,
    left_operand_input,
    right_operand_input,
):
    own, residues, channels = alignment_query.shape
    devices = n_seq * n_res
    spread = 2 - n_seq % 2, 2 - n_res % 2
    groups = spread[0] * spread[1]
    held = HEADS // groups
    width = held * HEAD_DIM
    rows, cols, pair_channels = pair.shape
    block = residues // devices
    a, b = lax.axis_index("seq"), lax.axis_index("res")
    flat = a * n_res + b

    bias = jnp.einsum("ijc,ch->hij", pair, pair_bias_matrix, preferred_element_type=f32)
    bias = bias.reshape(groups, held, rows, cols).transpose(0, 3, 1, 2)
    bias = bias.reshape(1, spread[0], 1, spread[1], cols, held * rows)
    by_group = (n_seq // spread[0], spread[0], n_res // spread[1], spread[1], cols, held * rows)
    bias = jnp.broadcast_to(bias, by_group)
    bias = lax.all_to_all(
        bias.reshape(devices, cols, held * rows), BOTH, 0, 0, tiled=True
    )

    place = a % spread[0] * spread[1] + b % spread[1]
    smem, vmem = [pl.BlockSpec(memory_space=s) for s in (pltpu.SMEM, pltpu.VMEM)]
    params = pltpu.CompilerParams(vmem_limit_bytes=12 * 1024 * 1024)
    hbm = pl.BlockSpec(memory_space=pl.ANY)
    packed = (own, residues, 4 * width)
    right_parts = (n_seq // n_res, n_res, block, cols, pair_channels)
    pieces = pl.pallas_call(
        functools.partial(pack_kernel, groups, n_res),
        in_specs=[smem, vmem] + [hbm] * 6,
        out_shape=[jax.ShapeDtypeStruct((1, residues), jnp.int32)]
        + [jax.ShapeDtypeStruct(packed, bf16)] * groups
        + [jax.ShapeDtypeStruct((2, block, rows, pair_channels), bf16)] * n_res,
        scratch_shapes=[
            pltpu.VMEM((4,) + alignment_query.shape, bf16),
            pltpu.VMEM((groups,) + packed, bf16),
            pltpu.SemaphoreType.DMA((4,)),
            pltpu.SemaphoreType.DMA((n_res * (1 + n_seq // n_res),)),
        ],
        compiler_params=params,
        name="pack",
    )(
        jnp.stack([place, b]).astype(jnp.int32),
        chain_index_per_residue.reshape(1, residues),
        alignment_query,
        alignment_key,
        attended_vectors,
        attended_cotangent,
        left_operand_input,
        right_operand_input.reshape(right_parts),
    )
    chain, arrays, triangles = pieces[0], pieces[1 : 1 + groups], pieces[1 + groups :]

    def peer(x, s):
        pairs = [
            (d, (d // n_res ^ s // spread[1]) * n_res + (d % n_res ^ s % spread[1]))
            for d in range(devices)
        ]
        return lax.ppermute(x, BOTH, pairs)

    def partner(x, s):
        return lax.ppermute(x, "res", [(i, i ^ s) for i in range(n_res)])

    arrays = list(arrays[:1]) + [peer(arrays[s], s) for s in range(1, groups)]

    inner = 2 - n_seq % 2
    half = n_seq // inner
    triangles = list(triangles[:1]) + [partner(triangles[s], s) for s in range(1, n_res)]
    arrays, triangles = lax.optimization_barrier((arrays, triangles))
    left, rights = pl.pallas_call(
        order_kernel,
        in_specs=[smem] + [vmem] * n_res,
        out_shape=[
            jax.ShapeDtypeStruct((block, residues, pair_channels), bf16),
            jax.ShapeDtypeStruct((n_seq, block, cols, pair_channels), bf16),
        ],
        compiler_params=params,
        name="order",
    )(b.reshape(1), *triangles)
    pairs = []
    for d in range(devices):
        g = d // n_res * n_res + turn(d % n_res, n_res)
        p = g % n_seq
        pairs.append((d, (p % half * inner + p // half) * n_res + g // n_seq))
    left = lax.ppermute(left, BOTH, pairs)
    rights = lax.all_to_all(rights, "seq", 0, 0, tiled=True)

    each = max(1, 128 // width)
    slots = (3 * own // each, residues, each * width)
    outs = pl.pallas_call(
        functools.partial(attention_kernel, n_seq, n_res, groups),
        out_shape=[jax.ShapeDtypeStruct(slots, bf16)] * groups
        + [jax.ShapeDtypeStruct(bias.shape, bf16)],
        scratch_shapes=[pltpu.VMEM((held, residues, residues), f32)] * 2,
        compiler_params=params,
        name="attention",
    )(bias, chain, *arrays)
    grads, share = outs[:groups], outs[groups]

    share, rights = lax.optimization_barrier((share, rights))
    share = lax.all_to_all(share, BOTH, 0, 0, tiled=True)
    share, left = lax.optimization_barrier((share, left))
    share = jnp.sum(share.astype(f32).reshape(by_group), axis=(0, 2))
    share = share.reshape(groups, cols, held * rows)
    parity = [list(range(c, devices, 2)) for c in range(2)]
    near = jnp.broadcast_to(share.astype(bf16)[None], (devices // 2,) + share.shape)
    near = lax.all_to_all(near, BOTH, 0, 0, axis_index_groups=parity, tiled=True)
    own_grad = share.reshape(groups, cols, held, rows).transpose(0, 2, 3, 1)
    own_grad = own_grad.reshape(HEADS, rows, cols)
    term = jnp.einsum(
        "ijc,hij->hc", pair.astype(f32), own_grad, precision=lax.Precision.HIGHEST
    )
    term = sum([term] + [partner(term, s) for s in range(1, n_res)])
    rights = [rights, partner(rights, 1)]
    extra = jnp.stack([pair_bias_matrix.astype(f32).T, term])
    near, extra, rights = lax.optimization_barrier((near, extra, rights))
    far = partner(near, 1)

    across = n_res // 2
    d_right = pl.pallas_call(
        functools.partial(d_right_kernel, n_seq, n_res),
        in_specs=[smem] + [vmem] * 4,
        out_shape=jax.ShapeDtypeStruct((n_seq, block * cols + 2 * HEADS, pair_channels), bf16),
        scratch_shapes=[
            pltpu.VMEM((HEADS, residues, residues), bf16),
        ],
        compiler_params=params,
        name="d_right",
    )((b % 2).reshape(1), near, far, extra, left)
    d_right = lax.all_to_all(d_right, "seq", 0, 0, tiled=True)

    piece = (2 * block, rows, pair_channels)
    d_left = pl.pallas_call(
        functools.partial(d_left_kernel, n_seq, n_res),
        in_specs=[smem] + [vmem] * 4,
        out_shape=[jax.ShapeDtypeStruct(piece, bf16)] * across,
        scratch_shapes=[
            pltpu.VMEM((across,) + piece, bf16),
            pltpu.VMEM((HEADS, across * rows, residues), bf16),
            pltpu.VMEM((2, block, residues, pair_channels), bf16),
        ],
        compiler_params=params,
        name="d_left",
    )(jnp.stack([b % 2, b // 2]).astype(jnp.int32), near, extra, *rights)
    d_left = list(d_left[:1]) + [partner(d_left[s], 2 * s) for s in range(1, across)]
    grads = [grads[0]] + [peer(grads[s], s) for s in range(1, groups)]
    d_left, grads = lax.optimization_barrier((d_left, grads))
    query_gradient, key_gradient, value_gradient = pl.pallas_call(
        unpack_kernel,
        in_specs=[smem] + [vmem] * groups,
        out_shape=[jax.ShapeDtypeStruct(alignment_query.shape, bf16)] * 3,
        scratch_shapes=[pltpu.VMEM((groups,) + slots, bf16)],
        compiler_params=params,
        name="unpack",
    )(place.reshape(1), *grads)

    d_bias_weight, d_left, d_right = pl.pallas_call(
        functools.partial(place_kernel, inner),
        in_specs=[smem] + [vmem] * (1 + across),
        out_shape=[
            jax.ShapeDtypeStruct((HEADS, pair_channels), f32),
            jax.ShapeDtypeStruct((across * 2 * block, rows, pair_channels), bf16),
            jax.ShapeDtypeStruct((n_seq * block, cols, pair_channels), bf16),
        ],
        compiler_params=params,
        name="place",
    )((b // 2).reshape(1), d_right, *d_left)
    d_bias_weight = d_bias_weight.T
    return (query_gradient, key_gradient, value_gradient, d_bias_weight, d_left, d_right)


def solution(mesh):
    placed = (
        P(BOTH, None, None),
        P(BOTH, None, None),
        P(BOTH, None, None),
        P(BOTH, None, None),
        P(),
        P("res", "seq", None),
        P(),
        P("seq", "res", None),
        P("res", "seq", None),
    )
    return jax.shard_map(
        functools.partial(shards, mesh.shape["seq"], mesh.shape["res"]),
        mesh=mesh,
        in_specs=placed,
        out_specs=(
            P(BOTH, None, None),
            P(BOTH, None, None),
            P(BOTH, None, None),
            P(),
            P("seq", "res", None),
            P("res", "seq", None),
        ),
        check_vma=False,
    )
```

time: 251 us -> 122 us (0.49)
  blocking collectives: 75.2 us -> 0 us
  starting transfers between devices: 65.9 us -> 38.6 us
  waiting for transfers between devices: 76 us -> 54.4 us
  local copies, waits for them, and re-layouts: 16.1 us -> 6.67 us
  Pallas kernels: 15 us -> 19.3 us
    all_to_all x7 -> x5, waiting for transfers between devices: 76 us -> 23.8 us  [the longest x1 10.6 us: shards(): share = lax.all_to_all(share, BOTH, 0, 0, tiled=True)]
    psum x1 -> x0, blocking collectives: 40.2 us -> none  [shards(): d_bias_weight = lax.psum(weight_term, BOTH)]
    all_to_all x7 -> x5, starting transfers between devices: 64.5 us -> 27.7 us  [the longest x1 7.32 us: shards(): share = lax.all_to_all(share, BOTH, 0, 0, tiled=True)]
    all_to_all x2 -> x0, blocking collectives: 35 us -> none  [the longest x1 21 us: shards(): lax.all_to_all(bias.reshape(devices, cols, held * rows), BOTH, 0, 0, tile...]
    ppermute x2 -> x16, waiting for transfers between devices: 0.01 us -> 30.6 us  [the longest x6 25.1 us: peer(): return lax.ppermute(x, BOTH, pairs)]
    ppermute x2 -> x16, starting transfers between devices: 1.39 us -> 10.9 us  [the longest x9 5.02 us: partner(): return lax.ppermute(x, 'res', [(i, i ^ s) for i in range(n_res)])]
    pallas_call x2 -> x7, Pallas kernels: 15 us -> 19.3 us  [the longest x1 8.01 us: shards(): pl.pallas_call(functools.partial(attention_kernel, n_seq, n_res, groups),...]
    pallas_call x3 -> x0, local copies, waits for them, and re-layouts: 3.54 us -> none  [the longest x2 2.28 us: shards(): pl.pallas_call(functools.partial(triangle_kernel, n_seq, n_res), out_shap...]
  transfers between devices with their start and end apart: 9 -> 21, of which waited for: 5 -> 11; matrix products, arithmetic and copies ran while one was open for 4% -> 1% of each run, Pallas kernels for 6% -> 12%
where the time goes in v2:
time: 122 us
  waiting for transfers between devices  54.4 us (45%)
  starting transfers between devices  38.6 us (32%)
  Pallas kernels  19.3 us (16%)
  local copies, waits for them, and re-layouts  6.67 us (5%)
  matrix products  1.65 us (1%)
    ppermute x6, waiting for transfers between devices, peer(): return lax.ppermute(x, BOTH, pairs)  25.1 us
    all_to_all x1, waiting for transfers between devices, shards(): share = lax.all_to_all(share, BOTH, 0, 0, tiled=True)  10.6 us
    all_to_all x1, waiting for transfers between devices, shards(): lax.all_to_all(near, BOTH, 0, 0, axis_index_groups=parity, tiled=True)  8.91 us
    pallas_call x1, Pallas kernels, shards(): pl.pallas_call(functools.partial(attention_kernel, n_seq, n_res, groups),...  8.01 us
    all_to_all x1, starting transfers between devices, shards(): share = lax.all_to_all(share, BOTH, 0, 0, tiled=True)  7.32 us
    all_to_all x1, starting transfers between devices, shards(): lax.all_to_all(bias.reshape(devices, cols, held * rows), BOTH, 0, 0, tile...  7.3 us
    all_to_all x1, starting transfers between devices, shards(): rights = lax.all_to_all(rights, 'seq', 0, 0, tiled=True)  5.56 us
    ppermute x9, waiting for transfers between devices, partner(): return lax.ppermute(x, 'res', [(i, i ^ s) for i in range(n_res)])  5.51 us
  transfers between devices with their start and end apart: 21, of which 11 were waited for; matrix products, arithmetic and copies ran while one was open for 1% of the time, Pallas kernels for 12%

profile of v2, /device:TPU:0, one launch (start us, length us, event | category | flops | bytes accessed | tf_op | source)
XLA Modules:
  0.0 121.8 jit_solution(13116308050954012311)
XLA Ops:
  0.6 0.0 copy-start
  0.6 1.0 copy-done
  1.7 1.2 %fusion.1 = f32[8,64,32]{1,0,2:T(8,128)S(1)} fusion(bf16[64,32,128]{2,1,0:T(8,128)(2,1)S(1)} %copy-done, bf16[128,8]{0,1:T(8,128)(2,1)} %param.15), kind=kOutput, calls=%fused_computation.3 | convolution fusion | flops 4194304 | bytes 591872 | tf_op jit(solution)/shard_map/ijc,ch->hij/dot_general | solution.py:273
  2.9 0.2 broadcast_in_dim.6
  3.1 0.0 copy-start.5
  3.1 0.0 copy-start.3
  3.1 0.0 copy-start.4
  3.1 0.9 broadcast_in_dim.14
  4.0 7.3 %all-to-all-start = ((f32[32,32,128]{2,1,0:T(8,128)}), f32[32,32,128]{2,1,0:T(8,128)S(1)}, u32[]{:S(2)}, u32[]{:S(2)}) async-start(f32[32,32,128]{2,1,0:T(8,128)} %bitcast.35), calls=%async_computation | async-start | bytes 1048576 | tf_op jit(solution)/shard_map/all_to_all | solution.py:278
  11.3 0.1 pad_add_fusion.1.scalars
  11.4 0.6 copy-done.7
  12.1 2.0 %pack.1 = (s32[1,256]{1,0:T(1,128)S(1)}, bf16[2,256,256]{2,1,0:T(8,128)(2,1)S(1)}, bf16[2,256,256]{2,1,0:T(8,128)(2,1)S(1)}, bf16[2,256,256]{2,1,0:T(8,128)(2,1)...) custom-call(s32[2]{0:T(128)S(1)} %pad_add_fusion.1.scalars, ...), custom_call_target="tpu_custom_call" | custom-call | tf_op jit(solution)/shard_map/pack/pallas_call | solution.py:288
  14.1 0.3 collective-permute-start
  14.4 1.7 %collective-permute-start.1 = (bf16[2,256,256]{2,1,0:T(8,128)(2,1)S(1)}, bf16[2,256,256]{2,1,0:T(8,128)(2,1)S(1)}, u32[]{:S(2)}, u32[]{:S(2)}) collective-permute-start(bf16[2,256,256]{2,1,0:T(8,128)(2,1)S(1)} %get-tuple-element.55), channel_id=1, source_target_pairs={{0,4},{1,5},{2,6},{3,7},{4,0},{5,1},{6,2},{7,3},{8,12},{9,13},{10,... | collective-permute-start | bytes 786440 | tf_op jit(solution)/shard_map/ppermute | solution.py:319
  16.1 0.0 collective-permute-start.2
  16.1 0.5 collective-permute-start.3
  16.5 1.7 %collective-permute-start.4 = (bf16[2,8,64,128]{3,2,1,0:T(8,128)(2,1)S(1)}, bf16[2,8,64,128]{3,2,1,0:T(8,128)(2,1)S(1)}, u32[]{:S(2)}, u32[]{:S(2)}) collective-permute-start(bf16[2,8,64,128]{3,2,1,0:T(8,128)(2,1)S(1)} %get-tuple-element.59), channel_id=1, source_target_pairs={{0,2},{1,3},{2,0},{3,1},{4,6},{5,7},{6,4},{7,5},{8,10},{9,11},{10,... | collective-permute-start | bytes 786440 | tf_op jit(solution)/shard_map/ppermute | solution.py:322
  18.2 0.0 collective-permute-done.refs_1_
  18.2 0.0 collective-permute-start.5
  18.2 8.1 %collective-permute-done.1.refs_2_ = bf16[2,256,256]{2,1,0:T(8,128)(2,1)S(1)} collective-permute-done((bf16[2,256,256]{2,1,0:T(8,128)(2,1)S(1)}, bf16[2,256,256]{2,1,0:T(8,128)(2,1)S(1)}, u32[]{:S(2)}, u32[]{:S(2)}) %collective-permute-start.1) | collective-permute-done | bytes 262176 | tf_op jit(solution)/shard_map/ppermute | solution.py:319
  26.3 5.2 %collective-permute-done.2.refs_3_ = bf16[2,256,256]{2,1,0:T(8,128)(2,1)S(1)} collective-permute-done((bf16[2,256,256]{2,1,0:T(8,128)(2,1)S(1)}, bf16[2,256,256]{2,1,0:T(8,128)(2,1)S(1)}, u32[]{:S(2)}, u32[]{:S(2)}) %collective-permute-start.2) | collective-permute-done | bytes 262176 | tf_op jit(solution)/shard_map/ppermute | solution.py:319
  31.5 0.0 collective-permute-done.3.refs_1_
  31.5 0.0 collective-permute-done.4.refs_2_
  31.5 0.2 collective-permute-done.5.refs_3_
  31.7 0.9 order.1
  32.6 0.8 copy-done.8
  33.4 0.0 all-to-all-done.bias_ref
  33.4 5.6 %all-to-all-start.1 = ((bf16[8,8,32,128]{3,2,1,0:T(8,128)(2,1)}), bf16[8,8,32,128]{3,2,1,0:T(8,128)(2,1)S(1)}, u32[]{:S(2)}, u32[]{:S(2)}) async-start(bf16[8,8,32,128]{3,2,1,0:T(8,128)(2,1)} %get-tuple-element.70), calls=%async_computation.1 | async-start | bytes 1048576 | tf_op jit(solution)/shard_map/all_to_all | solution.py:346
  38.9 1.7 %collective-permute-start.6 = (bf16[8,256,128]{2,1,0:T(8,128)(2,1)}, bf16[8,256,128]{2,1,0:T(8,128)(2,1)S(1)}, u32[]{:S(2)}, u32[]{:S(2)}) collective-permute-start(bf16[8,256,128]{2,1,0:T(8,128)(2,1)} %copy-done.8), channel_id=1, source_target_pairs={{0,0},{1,16},{2,8},{3,24},{4,4},{5,20},{6,12},{7,28},{8,1},{9,17},... | collective-permute-start | bytes 1572872 | tf_op jit(solution)/shard_map/ppermute | solution.py:345
  40.6 8.0 %attention.1 = (bf16[3,256,128]{2,1,0:T(8,128)(2,1)S(1)}, bf16[3,256,128]{2,1,0:T(8,128)(2,1)S(1)}, bf16[3,256,128]{2,1,0:T(8,128)(2,1)S(1)}, bf16[3,256,128]{2,1,0:T(8,128)(2,1)S(1)}, bf16[32,32,128]{2,1,0:T(8,128)(2,1)}) custom-call(f32[32,32,128]{2,1,0:T(8,128)S(1)} %all-to-all-done.bias_ref, s32[1,256]{1,0:T(1,128)S(1)} %get-tuple-element.52.chain_ref, ...), custom_call_target="tpu_custom_call" | custom-call | tf_op jit(solution)/shard_map/attention/pallas_call | solution.py:350
  48.6 0.7 copy-done.9
  49.3 0.7 copy-done.11
  50.0 0.7 copy-done.13
  50.7 4.3 %all-to-all-done.1.refs_0_ = bf16[8,8,32,128]{3,2,1,0:T(8,128)(2,1)S(1)} async-done(((bf16[8,8,32,128]{3,2,1,0:T(8,128)(2,1)}), bf16[8,8,32,128]{3,2,1,0:T(8,128)(2,1)S(1)}, u32[]{:S(2)}, u32[]{:S(2)}) %all-to-all-start.1) | async-done | bytes 524320 | tf_op jit(solution)/shard_map/all_to_all | solution.py:346
  55.0 7.3 %all-to-all-start.2 = ((bf16[32,32,128]{2,1,0:T(8,128)(2,1)}), bf16[32,32,128]{2,1,0:T(8,128)(2,1)S(1)}, u32[]{:S(2)}, u32[]{:S(2)}) async-start(bf16[32,32,128]{2,1,0:T(8,128)(2,1)} %get-tuple-element.71), calls=%async_computation.2 | async-start | bytes 524288 | tf_op jit(solution)/shard_map/all_to_all | solution.py:361
  62.3 10.6 %all-to-all-done.2 = bf16[32,32,128]{2,1,0:T(8,128)(2,1)S(1)} async-done(((bf16[32,32,128]{2,1,0:T(8,128)(2,1)}), bf16[32,32,128]{2,1,0:T(8,128)(2,1)S(1)}, u32[]{:S(2)}, u32[]{:S(2)}) %all-to-all-start.2) | async-done | bytes 262176 | tf_op jit(solution)/shard_map/all_to_all | solution.py:361
  73.0 0.9 broadcast_in_dim.15
  73.9 3.8 %all-to-all-start.3 = ((bf16[16,4,32,128]{3,2,1,0:T(8,128)(2,1)}), bf16[16,4,32,128]{3,2,1,0:T(8,128)(2,1)S(1)}, u32[]{:S(2)}, u32[]{:S(2)}) async-start(bf16[16,4,32,128]{3,2,1,0:T(8,128)(2,1)} %broadcast_in_dim.15), calls=%async_computation.3 | async-start | bytes 1048576 | tf_op jit(solution)/shard_map/all_to_all | solution.py:367
  77.6 0.1 collective-permute-start.10
  77.7 0.1 copy.17
  77.8 0.1 reshape_reshape.3
  77.9 0.0 copy-start.15
  77.9 0.4 convolution_bitcast_fusion
  78.4 1.9 %collective-permute-start.9 = (f32[8,128]{1,0:T(8,128)S(1)}, f32[8,128]{1,0:T(8,128)S(1)}, u32[]{:S(2)}, u32[]{:S(2)}) collective-permute-start(f32[8,128]{1,0:T(8,128)S(1)} %convolution_bitcast_fusion), channel_id=1, source_target_pairs={{0,3},{1,2},{2,1},{3,0},{4,7},{5,6},{6,5},{7,4},{8,11},{9,10},{10,... | collective-permute-start | bytes 12296 | tf_op jit(solution)/shard_map/ppermute | solution.py:322
  80.3 0.3 collective-permute-start.8
  80.5 0.0 collective-permute-start.7
  80.5 1.1 collective-permute-done.9
  81.6 2.3 %collective-permute-done.8 = f32[8,128]{1,0:T(8,128)S(1)} collective-permute-done((f32[8,128]{1,0:T(8,128)S(1)}, f32[8,128]{1,0:T(8,128)S(1)}, u32[]{:S(2)}, u32[]{:S(2)}) %collective-permute-start.8) | collective-permute-done | bytes 4128 | tf_op jit(solution)/shard_map/ppermute | solution.py:322
  83.9 0.0 collective-permute-done.7
  84.0 8.9 %all-to-all-done.3.near_ref = bf16[16,4,32,128]{3,2,1,0:T(8,128)(2,1)S(1)} async-done(((bf16[16,4,32,128]{3,2,1,0:T(8,128)(2,1)}), bf16[16,4,32,128]{3,2,1,0:T(8,128)(2,1)S(1)}, u32[]{:S(2)}, u32[]{:S(2)}) %all-to-all-start.3) | async-done | bytes 524320 | tf_op jit(solution)/shard_map/all_to_all | solution.py:367
  92.9 1.9 %collective-permute-done.15.far_ref = bf16[16,4,32,128]{3,2,1,0:T(8,128)(2,1)S(1)} collective-permute-done((bf16[16,4,32,128]{3,2,1,0:T(8,128)(2,1)S(1)}, bf16[16,4,32,128]{3,2,1,0:T(8,128)(2,1)S(1)}, u32[]{:S(2)}, u32[]{:S(2)}) %collective-permute-start.15) | collective-permute-done | bytes 524320 | tf_op jit(solution)/shard_map/ppermute | solution.py:322
  94.8 3.2 %d_right.1 = bf16[8,272,128]{2,1,0:T(8,128)(2,1)} custom-call(s32[1]{0:T(128)} %bitcast.1.scalars, bf16[16,4,32,128]{3,2,1,0:T(8,128)(2,1)S(1)} %all-to-all-done.3.near_ref, bf16[16,4,32,128]{3,2,1,0:T(8,128)(2,1)S(1)} %collective-permute-done.15.far_ref, f32[2,8,128]{2,1,0:T(8,128)S(1)} %pad_maximum_fusion.extra_ref, ...), custom_call_target="tpu_custom_call" | custom-call | tf_op jit(solution)/shard_map/d_right/pallas_call | solution.py:380
  98.0 3.8 %all-to-all-start.4 = ((bf16[8,272,128]{2,1,0:T(8,128)(2,1)}), bf16[8,272,128]{2,1,0:T(8,128)(2,1)S(1)}, u32[]{:S(2)}, u32[]{:S(2)}) async-start(bf16[8,272,128]{2,1,0:T(8,128)(2,1)} %d_right.1), calls=%async_computation.4 | async-start | bytes 1114112 | tf_op jit(solution)/shard_map/all_to_all | solution.py:390
  101.8 0.1 pad_add_fusion.scalars
  101.9 3.2 %d_left.1 = (bf16[16,64,128]{2,1,0:T(8,128)(2,1)S(1)}, bf16[16,64,128]{2,1,0:T(8,128)(2,1)S(1)}) custom-call(s32[2]{0:T(128)S(1)} %pad_add_fusion.scalars, bf16[16,4,32,128]{3,2,1,0:T(8,128)(2,1)S(1)} %all-to-all-done.3.near_ref, f32[2,8,128]{2,1,0:T(8,128)S(1)} %pad_maximum_fusion.extra_ref, bf16[8,8,32,128]{3,2,1,0:T(8,128)(2,1)S(1)} %all-to-all-done.1.refs_0_, ...), custom_call_target="tpu_custom_call" | custom-call | tf_op jit(solution)/shard_map/d_left/pallas_call | solution.py:393
  105.0 0.6 collective-permute-start.11
  105.7 2.1 %collective-permute-start.13 = (bf16[3,256,128]{2,1,0:T(8,128)(2,1)S(1)}, bf16[3,256,128]{2,1,0:T(8,128)(2,1)S(1)}, u32[]{:S(2)}, u32[]{:S(2)}) collective-permute-start(bf16[3,256,128]{2,1,0:T(8,128)(2,1)S(1)} %copy-done.12), channel_id=1, source_target_pairs={{0,4},{1,5},{2,6},{3,7},{4,0},{5,1},{6,2},{7,3},{8,12},{9,13},{10,... | collective-permute-start | bytes 589832 | tf_op jit(solution)/shard_map/ppermute | solution.py:319
  107.7 0.1 collective-permute-start.14
  107.9 0.0 collective-permute-done.12.refs_1_
  107.9 7.8 %collective-permute-done.13.refs_2_ = bf16[3,256,128]{2,1,0:T(8,128)(2,1)S(1)} collective-permute-done((bf16[3,256,128]{2,1,0:T(8,128)(2,1)S(1)}, bf16[3,256,128]{2,1,0:T(8,128)(2,1)S(1)}, u32[]{:S(2)}, u32[]{:S(2)}) %collective-permute-start.13) | collective-permute-done | bytes 196640 | tf_op jit(solution)/shard_map/ppermute | solution.py:319
  115.7 4.0 %collective-permute-done.14.refs_3_ = bf16[3,256,128]{2,1,0:T(8,128)(2,1)S(1)} collective-permute-done((bf16[3,256,128]{2,1,0:T(8,128)(2,1)S(1)}, bf16[3,256,128]{2,1,0:T(8,128)(2,1)S(1)}, u32[]{:S(2)}, u32[]{:S(2)}) %collective-permute-start.14) | collective-permute-done | bytes 196640 | tf_op jit(solution)/shard_map/ppermute | solution.py:319
  119.7 0.0 collective-permute-done.11.refs_1_
  119.7 1.1 unpack.1
  120.7 1.0 place.1
  (32 shorter events, 0.1 us)
Async XLA Ops:
  0.6 1.0 copy-start
  1.7 9.7 %copy-start.6 = (bf16[2,256,256]{2,1,0:T(8,128)(2,1)S(1)}, bf16[2,256,256]{2,1,0:T(8,128)(2,1)}, u32[]{:S(2)}) copy-start(bf16[2,256,256]{2,1,0:T(8,128)(2,1)} %refs_3_.1) | copy-start | bytes 786436
  3.1 8.3 %copy-start.5 = (bf16[2,256,256]{2,1,0:T(8,128)(2,1)S(1)}, bf16[2,256,256]{2,1,0:T(8,128)(2,1)}, u32[]{:S(2)}) copy-start(bf16[2,256,256]{2,1,0:T(8,128)(2,1)} %refs_2_.1) | copy-start | bytes 786436
  3.1 8.3 %copy-start.3 = (bf16[2,256,256]{2,1,0:T(8,128)(2,1)S(1)}, bf16[2,256,256]{2,1,0:T(8,128)(2,1)}, u32[]{:S(2)}) copy-start(bf16[2,256,256]{2,1,0:T(8,128)(2,1)} %refs_0_.1) | copy-start | bytes 786436
  3.1 8.3 %copy-start.4 = (bf16[2,256,256]{2,1,0:T(8,128)(2,1)S(1)}, bf16[2,256,256]{2,1,0:T(8,128)(2,1)}, u32[]{:S(2)}) copy-start(bf16[2,256,256]{2,1,0:T(8,128)(2,1)} %refs_1_.1) | copy-start | bytes 786436
  4.0 7.4 %copy-start.1 = (bf16[32,64,128]{2,1,0:T(8,128)(2,1)S(1)}, bf16[32,64,128]{2,1,0:T(8,128)(2,1)}, u32[]{:S(2)}) copy-start(bf16[32,64,128]{2,1,0:T(8,128)(2,1)} %refs_4_.1) | copy-start | bytes 1572868
  4.0 7.4 %copy-start.2 = (bf16[64,32,128]{2,1,0:T(8,128)(2,1)S(1)}, bf16[64,32,128]{2,1,0:T(8,128)(2,1)}, u32[]{:S(2)}) copy-start(bf16[64,32,128]{2,1,0:T(8,128)(2,1)} %param.17) | copy-start | bytes 1572868
  4.0 29.4 %all-to-all-start = ((f32[32,32,128]{2,1,0:T(8,128)}), f32[32,32,128]{2,1,0:T(8,128)S(1)}, u32[]{:S(2)}, u32[]{:S(2)}) async-start(f32[32,32,128]{2,1,0:T(8,128)} %bitcast.35), calls=%async_computation | async-start | bytes 1048576 | tf_op jit(solution)/shard_map/all_to_all | solution.py:278
  11.4 0.7 copy-start.7
  14.1 4.1 %collective-permute-start = (bf16[2,256,256]{2,1,0:T(8,128)(2,1)S(1)}, bf16[2,256,256]{2,1,0:T(8,128)(2,1)S(1)}, u32[]{:S(2)}, u32[]{:S(2)}) collective-permute-start(bf16[2,256,256]{2,1,0:T(8,128)(2,1)S(1)} %get-tuple-element.54), channel_id=1, source_target_pairs={{0,1},{1,0},{2,3},{3,2},{4,5},{5,4},{6,7},{7,6},{8,9},{9,8},{10,11... | collective-permute-start | bytes 786440 | tf_op jit(solution)/shard_map/ppermute | solution.py:319
  14.4 11.9 %collective-permute-start.1 = (bf16[2,256,256]{2,1,0:T(8,128)(2,1)S(1)}, bf16[2,256,256]{2,1,0:T(8,128)(2,1)S(1)}, u32[]{:S(2)}, u32[]{:S(2)}) collective-permute-start(bf16[2,256,256]{2,1,0:T(8,128)(2,1)S(1)} %get-tuple-element.55), channel_id=1, source_target_pairs={{0,4},{1,5},{2,6},{3,7},{4,0},{5,1},{6,2},{7,3},{8,12},{9,13},{10,... | collective-permute-start | bytes 786440 | tf_op jit(solution)/shard_map/ppermute | solution.py:319
  16.1 15.4 %collective-permute-start.2 = (bf16[2,256,256]{2,1,0:T(8,128)(2,1)S(1)}, bf16[2,256,256]{2,1,0:T(8,128)(2,1)S(1)}, u32[]{:S(2)}, u32[]{:S(2)}) collective-permute-start(bf16[2,256,256]{2,1,0:T(8,128)(2,1)S(1)} %get-tuple-element.56), channel_id=1, source_target_pairs={{0,5},{1,4},{2,7},{3,6},{4,1},{5,0},{6,3},{7,2},{8,13},{9,12},{10,... | collective-permute-start | bytes 786440 | tf_op jit(solution)/shard_map/ppermute | solution.py:319
  16.1 15.4 %collective-permute-start.3 = (bf16[2,8,64,128]{3,2,1,0:T(8,128)(2,1)S(1)}, bf16[2,8,64,128]{3,2,1,0:T(8,128)(2,1)S(1)}, u32[]{:S(2)}, u32[]{:S(2)}) collective-permute-start(bf16[2,8,64,128]{3,2,1,0:T(8,128)(2,1)S(1)} %get-tuple-element.58), channel_id=1, source_target_pairs={{0,1},{1,0},{2,3},{3,2},{4,5},{5,4},{6,7},{7,6},{8,9},{9,8},{10,11... | collective-permute-start | bytes 786440 | tf_op jit(solution)/shard_map/ppermute | solution.py:322
  16.5 15.0 %collective-permute-start.4 = (bf16[2,8,64,128]{3,2,1,0:T(8,128)(2,1)S(1)}, bf16[2,8,64,128]{3,2,1,0:T(8,128)(2,1)S(1)}, u32[]{:S(2)}, u32[]{:S(2)}) collective-permute-start(bf16[2,8,64,128]{3,2,1,0:T(8,128)(2,1)S(1)} %get-tuple-element.59), channel_id=1, source_target_pairs={{0,2},{1,3},{2,0},{3,1},{4,6},{5,7},{6,4},{7,5},{8,10},{9,11},{10,... | collective-permute-start | bytes 786440 | tf_op jit(solution)/shard_map/ppermute | solution.py:322
  18.2 13.5 %collective-permute-start.5 = (bf16[2,8,64,128]{3,2,1,0:T(8,128)(2,1)S(1)}, bf16[2,8,64,128]{3,2,1,0:T(8,128)(2,1)S(1)}, u32[]{:S(2)}, u32[]{:S(2)}) collective-permute-start(bf16[2,8,64,128]{3,2,1,0:T(8,128)(2,1)S(1)} %get-tuple-element.60), channel_id=1, source_target_pairs={{0,3},{1,2},{2,1},{3,0},{4,7},{5,6},{6,5},{7,4},{8,11},{9,10},{10,... | collective-permute-start | bytes 786440 | tf_op jit(solution)/shard_map/ppermute | solution.py:322
  32.6 0.8 copy-start.8
  33.4 21.6 %all-to-all-start.1 = ((bf16[8,8,32,128]{3,2,1,0:T(8,128)(2,1)}), bf16[8,8,32,128]{3,2,1,0:T(8,128)(2,1)S(1)}, u32[]{:S(2)}, u32[]{:S(2)}) async-start(bf16[8,8,32,128]{3,2,1,0:T(8,128)(2,1)} %get-tuple-element.70), calls=%async_computation.1 | async-start | bytes 1048576 | tf_op jit(solution)/shard_map/all_to_all | solution.py:346
  38.9 23.4 %collective-permute-start.6 = (bf16[8,256,128]{2,1,0:T(8,128)(2,1)}, bf16[8,256,128]{2,1,0:T(8,128)(2,1)S(1)}, u32[]{:S(2)}, u32[]{:S(2)}) collective-permute-start(bf16[8,256,128]{2,1,0:T(8,128)(2,1)} %copy-done.8), channel_id=1, source_target_pairs={{0,0},{1,16},{2,8},{3,24},{4,4},{5,20},{6,12},{7,28},{8,1},{9,17},... | collective-permute-start | bytes 1572872 | tf_op jit(solution)/shard_map/ppermute | solution.py:345
  48.6 0.7 copy-start.9
  49.3 0.7 copy-start.11
  50.0 0.7 copy-start.13
  55.0 17.9 %all-to-all-start.2 = ((bf16[32,32,128]{2,1,0:T(8,128)(2,1)}), bf16[32,32,128]{2,1,0:T(8,128)(2,1)S(1)}, u32[]{:S(2)}, u32[]{:S(2)}) async-start(bf16[32,32,128]{2,1,0:T(8,128)(2,1)} %get-tuple-element.71), calls=%async_computation.2 | async-start | bytes 524288 | tf_op jit(solution)/shard_map/all_to_all | solution.py:361
  73.9 19.0 %all-to-all-start.3 = ((bf16[16,4,32,128]{3,2,1,0:T(8,128)(2,1)}), bf16[16,4,32,128]{3,2,1,0:T(8,128)(2,1)S(1)}, u32[]{:S(2)}, u32[]{:S(2)}) async-start(bf16[16,4,32,128]{3,2,1,0:T(8,128)(2,1)} %broadcast_in_dim.15), calls=%async_computation.3 | async-start | bytes 1048576 | tf_op jit(solution)/shard_map/all_to_all | solution.py:367
  77.6 6.3 %collective-permute-start.10 = (bf16[8,8,32,128]{3,2,1,0:T(8,128)(2,1)S(1)}, bf16[8,8,32,128]{3,2,1,0:T(8,128)(2,1)S(1)}, u32[]{:S(2)}, u32[]{:S(2)}) collective-permute-start(bf16[8,8,32,128]{3,2,1,0:T(8,128)(2,1)S(1)} %all-to-all-done.1.refs_0_), channel_id=1, source_target_pairs={{0,1},{1,0},{2,3},{3,2},{4,5},{5,4},{6,7},{7,6},{8,9},{9,8},{10,11... | collective-permute-start | bytes 1572872 | tf_op jit(solution)/shard_map/ppermute | solution.py:322
  77.9 2.6 %copy-start.15 = (bf16[128,8]{0,1:T(8,128)(2,1)S(1)}, bf16[128,8]{0,1:T(8,128)(2,1)}, u32[]{:S(2)}) copy-start(bf16[128,8]{0,1:T(8,128)(2,1)} %param.15) | copy-start | bytes 6148
  78.4 3.3 %collective-permute-start.9 = (f32[8,128]{1,0:T(8,128)S(1)}, f32[8,128]{1,0:T(8,128)S(1)}, u32[]{:S(2)}, u32[]{:S(2)}) collective-permute-start(f32[8,128]{1,0:T(8,128)S(1)} %convolution_bitcast_fusion), channel_id=1, source_target_pairs={{0,3},{1,2},{2,1},{3,0},{4,7},{5,6},{6,5},{7,4},{8,11},{9,10},{10,... | collective-permute-start | bytes 12296 | tf_op jit(solution)/shard_map/ppermute | solution.py:322
  80.3 3.6 %collective-permute-start.8 = (f32[8,128]{1,0:T(8,128)S(1)}, f32[8,128]{1,0:T(8,128)S(1)}, u32[]{:S(2)}, u32[]{:S(2)}) collective-permute-start(f32[8,128]{1,0:T(8,128)S(1)} %convolution_bitcast_fusion), channel_id=1, source_target_pairs={{0,2},{1,3},{2,0},{3,1},{4,6},{5,7},{6,4},{7,5},{8,10},{9,11},{10,... | collective-permute-start | bytes 12296 | tf_op jit(solution)/shard_map/ppermute | solution.py:322
  80.5 3.4 %collective-permute-start.7 = (f32[8,128]{1,0:T(8,128)S(1)}, f32[8,128]{1,0:T(8,128)S(1)}, u32[]{:S(2)}, u32[]{:S(2)}) collective-permute-start(f32[8,128]{1,0:T(8,128)S(1)} %convolution_bitcast_fusion), channel_id=1, source_target_pairs={{0,1},{1,0},{2,3},{3,2},{4,5},{5,4},{6,7},{7,6},{8,9},{9,8},{10,11... | collective-permute-start | bytes 12296 | tf_op jit(solution)/shard_map/ppermute | solution.py:322
  92.9 1.9 %collective-permute-start.15 = (bf16[16,4,32,128]{3,2,1,0:T(8,128)(2,1)S(1)}, bf16[16,4,32,128]{3,2,1,0:T(8,128)(2,1)S(1)}, u32[]{:S(2)}, u32[]{:S(2)}) collective-permute-start(bf16[16,4,32,128]{3,2,1,0:T(8,128)(2,1)S(1)} %all-to-all-done.3.near_ref), channel_id=1, source_target_pairs={{0,1},{1,0},{2,3},{3,2},{4,5},{5,4},{6,7},{7,6},{8,9},{9,8},{10,11... | collective-permute-start | bytes 1572872 | tf_op jit(solution)/shard_map/ppermute | solution.py:322
  98.0 22.7 %all-to-all-start.4 = ((bf16[8,272,128]{2,1,0:T(8,128)(2,1)}), bf16[8,272,128]{2,1,0:T(8,128)(2,1)S(1)}, u32[]{:S(2)}, u32[]{:S(2)}) async-start(bf16[8,272,128]{2,1,0:T(8,128)(2,1)} %d_right.1), calls=%async_computation.4 | async-start | bytes 1114112 | tf_op jit(solution)/shard_map/all_to_all | solution.py:390
  101.8 3.8 %copy-start.14 = (bf16[3,256,128]{2,1,0:T(8,128)(2,1)S(1)}, bf16[3,256,128]{2,1,0:T(8,128)(2,1)}, u32[]{:S(2)}) copy-start(bf16[3,256,128]{2,1,0:T(8,128)(2,1)} %copy-done.13) | copy-start | bytes 589828
  101.9 3.8 %copy-start.12 = (bf16[3,256,128]{2,1,0:T(8,128)(2,1)S(1)}, bf16[3,256,128]{2,1,0:T(8,128)(2,1)}, u32[]{:S(2)}) copy-start(bf16[3,256,128]{2,1,0:T(8,128)(2,1)} %copy-done.11) | copy-start | bytes 589828
  101.9 5.9 %copy-start.10 = (bf16[3,256,128]{2,1,0:T(8,128)(2,1)S(1)}, bf16[3,256,128]{2,1,0:T(8,128)(2,1)}, u32[]{:S(2)}) copy-start(bf16[3,256,128]{2,1,0:T(8,128)(2,1)} %copy-done.9) | copy-start | bytes 589828
  105.0 14.6 %collective-permute-start.11 = (bf16[16,64,128]{2,1,0:T(8,128)(2,1)S(1)}, bf16[16,64,128]{2,1,0:T(8,128)(2,1)S(1)}, u32[]{:S(2)}, u32[]{:S(2)}) collective-permute-start(bf16[16,64,128]{2,1,0:T(8,128)(2,1)S(1)} %get-tuple-element.80), channel_id=1, source_target_pairs={{0,2},{1,3},{2,0},{3,1},{4,6},{5,7},{6,4},{7,5},{8,10},{9,11},{10,... | collective-permute-start | bytes 786440 | tf_op jit(solution)/shard_map/ppermute | solution.py:322
  105.6 2.2 %collective-permute-start.12 = (bf16[3,256,128]{2,1,0:T(8,128)(2,1)S(1)}, bf16[3,256,128]{2,1,0:T(8,128)(2,1)S(1)}, u32[]{:S(2)}, u32[]{:S(2)}) collective-permute-start(bf16[3,256,128]{2,1,0:T(8,128)(2,1)S(1)} %copy-done.14), channel_id=1, source_target_pairs={{0,1},{1,0},{2,3},{3,2},{4,5},{5,4},{6,7},{7,6},{8,9},{9,8},{10,11... | collective-permute-start | bytes 589832 | tf_op jit(solution)/shard_map/ppermute | solution.py:319
  105.7 10.0 %collective-permute-start.13 = (bf16[3,256,128]{2,1,0:T(8,128)(2,1)S(1)}, bf16[3,256,128]{2,1,0:T(8,128)(2,1)S(1)}, u32[]{:S(2)}, u32[]{:S(2)}) collective-permute-start(bf16[3,256,128]{2,1,0:T(8,128)(2,1)S(1)} %copy-done.12), channel_id=1, source_target_pairs={{0,4},{1,5},{2,6},{3,7},{4,0},{5,1},{6,2},{7,3},{8,12},{9,13},{10,... | collective-permute-start | bytes 589832 | tf_op jit(solution)/shard_map/ppermute | solution.py:319
  107.7 11.9 %collective-permute-start.14 = (bf16[3,256,128]{2,1,0:T(8,128)(2,1)S(1)}, bf16[3,256,128]{2,1,0:T(8,128)(2,1)S(1)}, u32[]{:S(2)}, u32[]{:S(2)}) collective-permute-start(bf16[3,256,128]{2,1,0:T(8,128)(2,1)S(1)} %copy-done.10), channel_id=1, source_target_pairs={{0,5},{1,4},{2,7},{3,6},{4,1},{5,0},{6,3},{7,2},{8,13},{9,12},{10,... | collective-permute-start | bytes 589832 | tf_op jit(solution)/shard_map/ppermute | solution.py:319

commit v3 on v2

--- a/solution.py
+++ b/solution.py
@@ -154,6 +154,10 @@
             chunks_ref[b * each + y] = piece[1, :, y * cols : (y + 1) * cols]
 
 
+def pairs_of(block):
+    return [(k, min(2, block - k)) for k in range(0, block, 2)]
+
+
 def d_left_kernel(n_seq, n_res, scalars, near_ref, extra_ref, *refs):
     rights, outs = refs[:2], refs[2:-2]
     flat, right = refs[-2:]
@@ -184,14 +188,18 @@
         )
         flat[h] = turned.astype(f32).T.astype(bf16)
     sums = outs[-1]
+    channels = right.shape[-1]
     for c in range(2):
-        for k in range(block):
-            row = jnp.zeros((count, right.shape[-1]), f32)
+        for k, wide in pairs_of(block):
+            both = jnp.concatenate([right[c, k + n] for n in range(wide)], axis=-1)
+            row = jnp.zeros((count, wide * channels), f32)
             for h in range(heads):
-                product = jnp.dot(flat[h], right[c, k], preferred_element_type=f32)
-                row += product * extra_ref[0, h : h + 1, :]
-            for u in range(across):
-                sums[u, c * block + k] = row[u * rows : (u + 1) * rows].astype(bf16)
+                weight = jnp.concatenate([extra_ref[0, h : h + 1, :]] * wide, axis=-1)
+                row += jnp.dot(flat[h], both, preferred_element_type=f32) * weight
+            for n in range(wide):
+                part = row[:, n * channels : (n + 1) * channels].astype(bf16)
+                for u in range(across):
+                    sums[u, c * block + k + n] = part[u * rows : (u + 1) * rows]
     for s in range(across):
         outs[s][...] = sums[x ^ s]
 
@@ -213,13 +221,17 @@
                 )
                 band.append(jnp.where(core == b % 2, near_ref[piece], far_ref[piece]))
             turned[h, a * cols : (a + 1) * cols, :] = jnp.concatenate(band, axis=-1)
-    for k in range(block):
-        row = jnp.zeros((residues, left.shape[-1]), f32)
+    channels = left.shape[-1]
+    for k, wide in pairs_of(block):
+        both = jnp.concatenate([left[k + n] for n in range(wide)], axis=-1)
+        row = jnp.zeros((residues, wide * channels), f32)
         for h in range(heads):
-            product = jnp.dot(turned[h], left[k], preferred_element_type=f32)
-            row += product * extra_ref[0, h : h + 1, :]
-        for a in range(n_seq):
-            out[a, k * cols : (k + 1) * cols] = row[a * cols : (a + 1) * cols].astype(bf16)
+            weight = jnp.concatenate([extra_ref[0, h : h + 1, :]] * wide, axis=-1)
+            row += jnp.dot(turned[h], both, preferred_element_type=f32) * weight
+        for n in range(wide):
+            part = row[:, n * channels : (n + 1) * channels].astype(bf16)
+            for a in range(n_seq):
+                out[a, (k + n) * cols : (k + n + 1) * cols] = part[a * cols : (a + 1) * cols]
     term = extra_ref[1]
     high = term.astype(bf16).astype(f32)
     both = jnp.concatenate([high, term - high], axis=0).astype(bf16)
@@ -373,7 +385,13 @@
     term = sum([term] + [partner(term, s) for s in range(1, n_res)])
     rights = [rights, partner(rights, 1)]
     extra = jnp.stack([pair_bias_matrix.astype(f32).T, term])
-    near, extra, rights = lax.optimization_barrier((near, extra, rights))
+    grads = list(grads)
+    for s in (1, 3):
+        grads[s] = peer(grads[s], s)
+    early = [grads[s] for s in (1, 3)]
+    near, extra, rights, early = lax.optimization_barrier((near, extra, rights, early))
+    for s, piece in zip((1, 3), early):
+        grads[s] = piece
     far = partner(near, 1)
 
     across = n_res // 2
@@ -403,7 +421,9 @@
         name="d_left",
     )(jnp.stack([b % 2, b // 2]).astype(jnp.int32), near, extra, *rights)
     d_left = list(d_left[:1]) + [partner(d_left[s], 2 * s) for s in range(1, across)]
-    grads = [grads[0]] + [peer(grads[s], s) for s in range(1, groups)]
+    for s in range(1, groups):
+        if s not in (1, 3):
+            grads[s] = peer(grads[s], s)
     d_left, grads = lax.optimization_barrier((d_left, grads))
     query_gradient, key_gradient, value_gradient = pl.pallas_call(
         unpack_kernel,

time: 122 us -> 118 us (0.967)
  waiting for transfers between devices: 54.4 us -> 49.7 us
  starting transfers between devices: 38.6 us -> 40.9 us
  Pallas kernels: 19.3 us -> 17.2 us
    all_to_all x1, waiting for transfers between devices: 8.91 us -> 2.74 us  [shards(): lax.all_to_all(near, BOTH, 0, 0, axis_index_groups=parity, tiled=True)]
    ppermute x9, waiting for transfers between devices: 5.51 us -> 3.16 us  [partner(): return lax.ppermute(x, 'res', [(i, i ^ s) for i in range(n_res)])]
    ppermute x6, starting transfers between devices: 4.22 us -> 6.36 us  [peer(): return lax.ppermute(x, BOTH, pairs)]
    all_to_all x1, waiting for transfers between devices: 0.01 us -> 1.96 us  [shards(): d_right = lax.all_to_all(d_right, 'seq', 0, 0, tiled=True)]
    ppermute x6, waiting for transfers between devices: 25.1 us -> 27 us  [peer(): return lax.ppermute(x, BOTH, pairs)]
  transfers between devices with their start and end apart: 21 -> 21, of which waited for: 11 -> 12; matrix products, arithmetic and copies ran while one was open for 1% -> 1% of each run, Pallas kernels for 12% -> 12%
where the time goes in v3:
time: 118 us; the launch traced here: 117 us
  waiting for transfers between devices  49.7 us (42%)
  starting transfers between devices  40.9 us (35%)
  Pallas kernels  17.2 us (15%)
  local copies, waits for them, and re-layouts  6.67 us (6%)
  matrix products  1.65 us (1%)
    ppermute x6, waiting for transfers between devices, peer(): return lax.ppermute(x, BOTH, pairs)  27 us
    all_to_all x1, waiting for transfers between devices, shards(): share = lax.all_to_all(share, BOTH, 0, 0, tiled=True)  10.6 us
    pallas_call x1, Pallas kernels, shards(): pl.pallas_call(functools.partial(attention_kernel, n_seq, n_res, groups),...  8.01 us
    all_to_all x1, starting transfers between devices, shards(): share = lax.all_to_all(share, BOTH, 0, 0, tiled=True)  7.32 us
    all_to_all x1, starting transfers between devices, shards(): lax.all_to_all(bias.reshape(devices, cols, held * rows), BOTH, 0, 0, tile...  7.3 us
    ppermute x6, starting transfers between devices, peer(): return lax.ppermute(x, BOTH, pairs)  6.36 us
    all_to_all x1, starting transfers between devices, shards(): rights = lax.all_to_all(rights, 'seq', 0, 0, tiled=True)  5.56 us
    ppermute x9, starting transfers between devices, partner(): return lax.ppermute(x, 'res', [(i, i ^ s) for i in range(n_res)])  5.13 us
  transfers between devices with their start and end apart: 21, of which 12 were waited for; matrix products, arithmetic and copies ran while one was open for 1% of the time, Pallas kernels for 12%

profile of v3, /device:TPU:0, one launch (start us, length us, event | category | flops | bytes accessed | tf_op | source)
XLA Modules:
  0.0 117.3 jit_solution(4949890542918490626)
XLA Ops:
  0.6 0.0 copy-start
  0.6 1.0 copy-done
  1.7 1.2 %fusion.1 = f32[8,64,32]{1,0,2:T(8,128)S(1)} fusion(bf16[64,32,128]{2,1,0:T(8,128)(2,1)S(1)} %copy-done, bf16[128,8]{0,1:T(8,128)(2,1)} %param.15), kind=kOutput, calls=%fused_computation.3 | convolution fusion | flops 4194304 | bytes 591872 | tf_op jit(solution)/shard_map/ijc,ch->hij/dot_general | solution.py:285
  2.9 0.2 broadcast_in_dim.6
  3.1 0.0 copy-start.5
  3.1 0.0 copy-start.3
  3.1 0.0 copy-start.4
  3.1 0.9 broadcast_in_dim.14
  4.0 7.3 %all-to-all-start = ((f32[32,32,128]{2,1,0:T(8,128)}), f32[32,32,128]{2,1,0:T(8,128)S(1)}, u32[]{:S(2)}, u32[]{:S(2)}) async-start(f32[32,32,128]{2,1,0:T(8,128)} %bitcast.35), calls=%async_computation | async-start | bytes 1048576 | tf_op jit(solution)/shard_map/all_to_all | solution.py:290
  11.3 0.1 pad_add_fusion.1.scalars
  11.4 0.6 copy-done.7
  12.1 2.0 %pack.1 = (s32[1,256]{1,0:T(1,128)S(1)}, bf16[2,256,256]{2,1,0:T(8,128)(2,1)S(1)}, bf16[2,256,256]{2,1,0:T(8,128)(2,1)S(1)}, bf16[2,256,256]{2,1,0:T(8,128)(2,1)...) custom-call(s32[2]{0:T(128)S(1)} %pad_add_fusion.1.scalars, ...), custom_call_target="tpu_custom_call" | custom-call | tf_op jit(solution)/shard_map/pack/pallas_call | solution.py:300
  14.1 0.3 collective-permute-start
  14.4 1.7 %collective-permute-start.1 = (bf16[2,256,256]{2,1,0:T(8,128)(2,1)S(1)}, bf16[2,256,256]{2,1,0:T(8,128)(2,1)S(1)}, u32[]{:S(2)}, u32[]{:S(2)}) collective-permute-start(bf16[2,256,256]{2,1,0:T(8,128)(2,1)S(1)} %get-tuple-element.57), channel_id=1, source_target_pairs={{0,4},{1,5},{2,6},{3,7},{4,0},{5,1},{6,2},{7,3},{8,12},{9,13},{10,... | collective-permute-start | bytes 786440 | tf_op jit(solution)/shard_map/ppermute | solution.py:331
  16.1 0.0 collective-permute-start.2
  16.1 0.5 collective-permute-start.3
  16.5 1.7 %collective-permute-start.4 = (bf16[2,8,64,128]{3,2,1,0:T(8,128)(2,1)S(1)}, bf16[2,8,64,128]{3,2,1,0:T(8,128)(2,1)S(1)}, u32[]{:S(2)}, u32[]{:S(2)}) collective-permute-start(bf16[2,8,64,128]{3,2,1,0:T(8,128)(2,1)S(1)} %get-tuple-element.61), channel_id=1, source_target_pairs={{0,2},{1,3},{2,0},{3,1},{4,6},{5,7},{6,4},{7,5},{8,10},{9,11},{10,... | collective-permute-start | bytes 786440 | tf_op jit(solution)/shard_map/ppermute | solution.py:334
  18.2 0.0 collective-permute-done.refs_1_
  18.2 0.0 collective-permute-start.5
  18.2 8.1 %collective-permute-done.1.refs_2_ = bf16[2,256,256]{2,1,0:T(8,128)(2,1)S(1)} collective-permute-done((bf16[2,256,256]{2,1,0:T(8,128)(2,1)S(1)}, bf16[2,256,256]{2,1,0:T(8,128)(2,1)S(1)}, u32[]{:S(2)}, u32[]{:S(2)}) %collective-permute-start.1) | collective-permute-done | bytes 262176 | tf_op jit(solution)/shard_map/ppermute | solution.py:331
  26.3 5.2 %collective-permute-done.2.refs_3_ = bf16[2,256,256]{2,1,0:T(8,128)(2,1)S(1)} collective-permute-done((bf16[2,256,256]{2,1,0:T(8,128)(2,1)S(1)}, bf16[2,256,256]{2,1,0:T(8,128)(2,1)S(1)}, u32[]{:S(2)}, u32[]{:S(2)}) %collective-permute-start.2) | collective-permute-done | bytes 262176 | tf_op jit(solution)/shard_map/ppermute | solution.py:331
  31.5 0.0 collective-permute-done.3.refs_1_
  31.5 0.0 collective-permute-done.4.refs_2_
  31.5 0.2 collective-permute-done.5.refs_3_
  31.7 0.9 order.1
  32.6 0.8 copy-done.8
  33.4 0.0 all-to-all-done.bias_ref
  33.4 5.6 %all-to-all-start.1 = ((bf16[8,8,32,128]{3,2,1,0:T(8,128)(2,1)}), bf16[8,8,32,128]{3,2,1,0:T(8,128)(2,1)S(1)}, u32[]{:S(2)}, u32[]{:S(2)}) async-start(bf16[8,8,32,128]{3,2,1,0:T(8,128)(2,1)} %get-tuple-element.72), calls=%async_computation.1 | async-start | bytes 1048576 | tf_op jit(solution)/shard_map/all_to_all | solution.py:358
  38.9 1.7 %collective-permute-start.6 = (bf16[8,256,128]{2,1,0:T(8,128)(2,1)}, bf16[8,256,128]{2,1,0:T(8,128)(2,1)S(1)}, u32[]{:S(2)}, u32[]{:S(2)}) collective-permute-start(bf16[8,256,128]{2,1,0:T(8,128)(2,1)} %copy-done.8), channel_id=1, source_target_pairs={{0,0},{1,16},{2,8},{3,24},{4,4},{5,20},{6,12},{7,28},{8,1},{9,17},... | collective-permute-start | bytes 1572872 | tf_op jit(solution)/shard_map/ppermute | solution.py:357
  40.6 8.0 %attention.1 = (bf16[3,256,128]{2,1,0:T(8,128)(2,1)S(1)}, bf16[3,256,128]{2,1,0:T(8,128)(2,1)S(1)}, bf16[3,256,128]{2,1,0:T(8,128)(2,1)S(1)}, bf16[3,256,128]{2,1,0:T(8,128)(2,1)S(1)}, bf16[32,32,128]{2,1,0:T(8,128)(2,1)}) custom-call(f32[32,32,128]{2,1,0:T(8,128)S(1)} %all-to-all-done.bias_ref, s32[1,256]{1,0:T(1,128)S(1)} %get-tuple-element.54.chain_ref, ...), custom_call_target="tpu_custom_call" | custom-call | tf_op jit(solution)/shard_map/attention/pallas_call | solution.py:362
  48.6 0.7 copy-done.9
  49.3 0.7 copy-done.11
  50.0 0.7 copy-done.13
  50.7 4.3 %all-to-all-done.1.refs_0_ = bf16[8,8,32,128]{3,2,1,0:T(8,128)(2,1)S(1)} async-done(((bf16[8,8,32,128]{3,2,1,0:T(8,128)(2,1)}), bf16[8,8,32,128]{3,2,1,0:T(8,128)(2,1)S(1)}, u32[]{:S(2)}, u32[]{:S(2)}) %all-to-all-start.1) | async-done | bytes 524320 | tf_op jit(solution)/shard_map/all_to_all | solution.py:358
  55.0 7.3 %all-to-all-start.2 = ((bf16[32,32,128]{2,1,0:T(8,128)(2,1)}), bf16[32,32,128]{2,1,0:T(8,128)(2,1)S(1)}, u32[]{:S(2)}, u32[]{:S(2)}) async-start(bf16[32,32,128]{2,1,0:T(8,128)(2,1)} %get-tuple-element.73), calls=%async_computation.2 | async-start | bytes 524288 | tf_op jit(solution)/shard_map/all_to_all | solution.py:373
  62.3 10.6 %all-to-all-done.2 = bf16[32,32,128]{2,1,0:T(8,128)(2,1)S(1)} async-done(((bf16[32,32,128]{2,1,0:T(8,128)(2,1)}), bf16[32,32,128]{2,1,0:T(8,128)(2,1)S(1)}, u32[]{:S(2)}, u32[]{:S(2)}) %all-to-all-start.2) | async-done | bytes 262176 | tf_op jit(solution)/shard_map/all_to_all | solution.py:373
  73.0 0.9 broadcast_in_dim.15
  73.9 3.8 %all-to-all-start.3 = ((bf16[16,4,32,128]{3,2,1,0:T(8,128)(2,1)}), bf16[16,4,32,128]{3,2,1,0:T(8,128)(2,1)S(1)}, u32[]{:S(2)}, u32[]{:S(2)}) async-start(bf16[16,4,32,128]{3,2,1,0:T(8,128)(2,1)} %broadcast_in_dim.15), calls=%async_computation.3 | async-start | bytes 1048576 | tf_op jit(solution)/shard_map/all_to_all | solution.py:379
  77.6 0.1 collective-permute-start.10
  77.7 0.1 copy.17
  77.8 0.1 reshape_reshape.3
  77.9 0.0 copy-start.15
  77.9 0.0 copy-start.14
  78.0 0.4 convolution_bitcast_fusion
  78.4 1.9 %collective-permute-start.9 = (f32[8,128]{1,0:T(8,128)S(1)}, f32[8,128]{1,0:T(8,128)S(1)}, u32[]{:S(2)}, u32[]{:S(2)}) collective-permute-start(f32[8,128]{1,0:T(8,128)S(1)} %convolution_bitcast_fusion), channel_id=1, source_target_pairs={{0,3},{1,2},{2,1},{3,0},{4,7},{5,6},{6,5},{7,4},{8,11},{9,10},{10,... | collective-permute-start | bytes 12296 | tf_op jit(solution)/shard_map/ppermute | solution.py:334
  80.3 0.3 collective-permute-start.8
  80.6 0.0 collective-permute-start.7
  80.6 0.6 collective-permute-start.11
  81.1 0.5 collective-permute-done.9
  81.6 1.8 %collective-permute-start.12 = (bf16[3,256,128]{2,1,0:T(8,128)(2,1)S(1)}, bf16[3,256,128]{2,1,0:T(8,128)(2,1)S(1)}, u32[]{:S(2)}, u32[]{:S(2)}) collective-permute-start(bf16[3,256,128]{2,1,0:T(8,128)(2,1)S(1)} %copy-done.12), channel_id=1, source_target_pairs={{0,5},{1,4},{2,7},{3,6},{4,1},{5,0},{6,3},{7,2},{8,13},{9,12},{10,... | collective-permute-start | bytes 589832 | tf_op jit(solution)/shard_map/ppermute | solution.py:331
  83.4 0.5 collective-permute-done.8
  84.0 6.1 %collective-permute-done.12.refs_3_ = bf16[3,256,128]{2,1,0:T(8,128)(2,1)S(1)} collective-permute-done((bf16[3,256,128]{2,1,0:T(8,128)(2,1)S(1)}, bf16[3,256,128]{2,1,0:T(8,128)(2,1)S(1)}, u32[]{:S(2)}, u32[]{:S(2)}) %collective-permute-start.12) | collective-permute-done | bytes 196640 | tf_op jit(solution)/shard_map/ppermute | solution.py:331
  90.1 2.7 %all-to-all-done.3.near_ref = bf16[16,4,32,128]{3,2,1,0:T(8,128)(2,1)S(1)} async-done(((bf16[16,4,32,128]{3,2,1,0:T(8,128)(2,1)}), bf16[16,4,32,128]{3,2,1,0:T(8,128)(2,1)S(1)}, u32[]{:S(2)}, u32[]{:S(2)}) %all-to-all-start.3) | async-done | bytes 524320 | tf_op jit(solution)/shard_map/all_to_all | solution.py:379
  92.9 1.9 %collective-permute-done.15.far_ref = bf16[16,4,32,128]{3,2,1,0:T(8,128)(2,1)S(1)} collective-permute-done((bf16[16,4,32,128]{3,2,1,0:T(8,128)(2,1)S(1)}, bf16[16,4,32,128]{3,2,1,0:T(8,128)(2,1)S(1)}, u32[]{:S(2)}, u32[]{:S(2)}) %collective-permute-start.15) | collective-permute-done | bytes 524320 | tf_op jit(solution)/shard_map/ppermute | solution.py:334
  94.8 2.2 %d_right.1 = bf16[8,272,128]{2,1,0:T(8,128)(2,1)} custom-call(s32[1]{0:T(128)} %bitcast.1.scalars, bf16[16,4,32,128]{3,2,1,0:T(8,128)(2,1)S(1)} %all-to-all-done.3.near_ref, bf16[16,4,32,128]{3,2,1,0:T(8,128)(2,1)S(1)} %collective-permute-done.15.far_ref, f32[2,8,128]{2,1,0:T(8,128)S(1)} %pad_maximum_fusion.extra_ref, ...), custom_call_target="tpu_custom_call" | custom-call | tf_op jit(solution)/shard_map/d_right/pallas_call | solution.py:398
  97.0 3.8 %all-to-all-start.4 = ((bf16[8,272,128]{2,1,0:T(8,128)(2,1)}), bf16[8,272,128]{2,1,0:T(8,128)(2,1)S(1)}, u32[]{:S(2)}, u32[]{:S(2)}) async-start(bf16[8,272,128]{2,1,0:T(8,128)(2,1)} %d_right.1), calls=%async_computation.4 | async-start | bytes 1114112 | tf_op jit(solution)/shard_map/all_to_all | solution.py:408
  100.7 0.1 pad_add_fusion.scalars
  100.8 2.1 %d_left.1 = (bf16[16,64,128]{2,1,0:T(8,128)(2,1)S(1)}, bf16[16,64,128]{2,1,0:T(8,128)(2,1)S(1)}) custom-call(s32[2]{0:T(128)S(1)} %pad_add_fusion.scalars, bf16[16,4,32,128]{3,2,1,0:T(8,128)(2,1)S(1)} %all-to-all-done.3.near_ref, f32[2,8,128]{2,1,0:T(8,128)S(1)} %pad_maximum_fusion.extra_ref, bf16[8,8,32,128]{3,2,1,0:T(8,128)(2,1)S(1)} %all-to-all-done.1.refs_0_, ...), custom_call_target="tpu_custom_call" | custom-call | tf_op jit(solution)/shard_map/d_left/pallas_call | solution.py:411
  102.9 0.7 collective-permute-start.13
  103.6 2.0 %collective-permute-start.14 = (bf16[3,256,128]{2,1,0:T(8,128)(2,1)S(1)}, bf16[3,256,128]{2,1,0:T(8,128)(2,1)S(1)}, u32[]{:S(2)}, u32[]{:S(2)}) collective-permute-start(bf16[3,256,128]{2,1,0:T(8,128)(2,1)S(1)} %copy-done.10), channel_id=1, source_target_pairs={{0,4},{1,5},{2,6},{3,7},{4,0},{5,1},{6,2},{7,3},{8,12},{9,13},{10,... | collective-permute-start | bytes 589832 | tf_op jit(solution)/shard_map/ppermute | solution.py:331
  105.6 7.5 %collective-permute-done.14.refs_2_ = bf16[3,256,128]{2,1,0:T(8,128)(2,1)S(1)} collective-permute-done((bf16[3,256,128]{2,1,0:T(8,128)(2,1)S(1)}, bf16[3,256,128]{2,1,0:T(8,128)(2,1)S(1)}, u32[]{:S(2)}, u32[]{:S(2)}) %collective-permute-start.14) | collective-permute-done | bytes 196640 | tf_op jit(solution)/shard_map/ppermute | solution.py:331
  113.2 1.1 unpack.1
  114.3 2.0 %all-to-all-done.4.received_ref = bf16[8,272,128]{2,1,0:T(8,128)(2,1)S(1)} async-done(((bf16[8,272,128]{2,1,0:T(8,128)(2,1)}), bf16[8,272,128]{2,1,0:T(8,128)(2,1)S(1)}, u32[]{:S(2)}, u32[]{:S(2)}) %all-to-all-start.4) | async-done | bytes 557088 | tf_op jit(solution)/shard_map/all_to_all | solution.py:408
  116.2 1.0 place.1
  (32 shorter events, 0.1 us)
Async XLA Ops:
  0.6 1.0 copy-start
  1.7 9.7 %copy-start.6 = (bf16[2,256,256]{2,1,0:T(8,128)(2,1)S(1)}, bf16[2,256,256]{2,1,0:T(8,128)(2,1)}, u32[]{:S(2)}) copy-start(bf16[2,256,256]{2,1,0:T(8,128)(2,1)} %refs_3_.1) | copy-start | bytes 786436
  3.1 8.3 %copy-start.5 = (bf16[2,256,256]{2,1,0:T(8,128)(2,1)S(1)}, bf16[2,256,256]{2,1,0:T(8,128)(2,1)}, u32[]{:S(2)}) copy-start(bf16[2,256,256]{2,1,0:T(8,128)(2,1)} %refs_2_.1) | copy-start | bytes 786436
  3.1 8.3 %copy-start.3 = (bf16[2,256,256]{2,1,0:T(8,128)(2,1)S(1)}, bf16[2,256,256]{2,1,0:T(8,128)(2,1)}, u32[]{:S(2)}) copy-start(bf16[2,256,256]{2,1,0:T(8,128)(2,1)} %refs_0_.1) | copy-start | bytes 786436
  3.1 8.3 %copy-start.4 = (bf16[2,256,256]{2,1,0:T(8,128)(2,1)S(1)}, bf16[2,256,256]{2,1,0:T(8,128)(2,1)}, u32[]{:S(2)}) copy-start(bf16[2,256,256]{2,1,0:T(8,128)(2,1)} %refs_1_.1) | copy-start | bytes 786436
  4.0 7.4 %copy-start.1 = (bf16[32,64,128]{2,1,0:T(8,128)(2,1)S(1)}, bf16[32,64,128]{2,1,0:T(8,128)(2,1)}, u32[]{:S(2)}) copy-start(bf16[32,64,128]{2,1,0:T(8,128)(2,1)} %refs_4_.1) | copy-start | bytes 1572868
  4.0 7.4 %copy-start.2 = (bf16[64,32,128]{2,1,0:T(8,128)(2,1)S(1)}, bf16[64,32,128]{2,1,0:T(8,128)(2,1)}, u32[]{:S(2)}) copy-start(bf16[64,32,128]{2,1,0:T(8,128)(2,1)} %param.17) | copy-start | bytes 1572868
  4.0 29.4 %all-to-all-start = ((f32[32,32,128]{2,1,0:T(8,128)}), f32[32,32,128]{2,1,0:T(8,128)S(1)}, u32[]{:S(2)}, u32[]{:S(2)}) async-start(f32[32,32,128]{2,1,0:T(8,128)} %bitcast.35), calls=%async_computation | async-start | bytes 1048576 | tf_op jit(solution)/shard_map/all_to_all | solution.py:290
  11.4 0.7 copy-start.7
  14.1 4.1 %collective-permute-start = (bf16[2,256,256]{2,1,0:T(8,128)(2,1)S(1)}, bf16[2,256,256]{2,1,0:T(8,128)(2,1)S(1)}, u32[]{:S(2)}, u32[]{:S(2)}) collective-permute-start(bf16[2,256,256]{2,1,0:T(8,128)(2,1)S(1)} %get-tuple-element.56), channel_id=1, source_target_pairs={{0,1},{1,0},{2,3},{3,2},{4,5},{5,4},{6,7},{7,6},{8,9},{9,8},{10,11... | collective-permute-start | bytes 786440 | tf_op jit(solution)/shard_map/ppermute | solution.py:331
  14.4 11.9 %collective-permute-start.1 = (bf16[2,256,256]{2,1,0:T(8,128)(2,1)S(1)}, bf16[2,256,256]{2,1,0:T(8,128)(2,1)S(1)}, u32[]{:S(2)}, u32[]{:S(2)}) collective-permute-start(bf16[2,256,256]{2,1,0:T(8,128)(2,1)S(1)} %get-tuple-element.57), channel_id=1, source_target_pairs={{0,4},{1,5},{2,6},{3,7},{4,0},{5,1},{6,2},{7,3},{8,12},{9,13},{10,... | collective-permute-start | bytes 786440 | tf_op jit(solution)/shard_map/ppermute | solution.py:331
  16.1 15.4 %collective-permute-start.2 = (bf16[2,256,256]{2,1,0:T(8,128)(2,1)S(1)}, bf16[2,256,256]{2,1,0:T(8,128)(2,1)S(1)}, u32[]{:S(2)}, u32[]{:S(2)}) collective-permute-start(bf16[2,256,256]{2,1,0:T(8,128)(2,1)S(1)} %get-tuple-element.58), channel_id=1, source_target_pairs={{0,5},{1,4},{2,7},{3,6},{4,1},{5,0},{6,3},{7,2},{8,13},{9,12},{10,... | collective-permute-start | bytes 786440 | tf_op jit(solution)/shard_map/ppermute | solution.py:331
  16.1 15.4 %collective-permute-start.3 = (bf16[2,8,64,128]{3,2,1,0:T(8,128)(2,1)S(1)}, bf16[2,8,64,128]{3,2,1,0:T(8,128)(2,1)S(1)}, u32[]{:S(2)}, u32[]{:S(2)}) collective-permute-start(bf16[2,8,64,128]{3,2,1,0:T(8,128)(2,1)S(1)} %get-tuple-element.60), channel_id=1, source_target_pairs={{0,1},{1,0},{2,3},{3,2},{4,5},{5,4},{6,7},{7,6},{8,9},{9,8},{10,11... | collective-permute-start | bytes 786440 | tf_op jit(solution)/shard_map/ppermute | solution.py:334
  16.5 15.0 %collective-permute-start.4 = (bf16[2,8,64,128]{3,2,1,0:T(8,128)(2,1)S(1)}, bf16[2,8,64,128]{3,2,1,0:T(8,128)(2,1)S(1)}, u32[]{:S(2)}, u32[]{:S(2)}) collective-permute-start(bf16[2,8,64,128]{3,2,1,0:T(8,128)(2,1)S(1)} %get-tuple-element.61), channel_id=1, source_target_pairs={{0,2},{1,3},{2,0},{3,1},{4,6},{5,7},{6,4},{7,5},{8,10},{9,11},{10,... | collective-permute-start | bytes 786440 | tf_op jit(solution)/shard_map/ppermute | solution.py:334
  18.2 13.5 %collective-permute-start.5 = (bf16[2,8,64,128]{3,2,1,0:T(8,128)(2,1)S(1)}, bf16[2,8,64,128]{3,2,1,0:T(8,128)(2,1)S(1)}, u32[]{:S(2)}, u32[]{:S(2)}) collective-permute-start(bf16[2,8,64,128]{3,2,1,0:T(8,128)(2,1)S(1)} %get-tuple-element.62), channel_id=1, source_target_pairs={{0,3},{1,2},{2,1},{3,0},{4,7},{5,6},{6,5},{7,4},{8,11},{9,10},{10,... | collective-permute-start | bytes 786440 | tf_op jit(solution)/shard_map/ppermute | solution.py:334
  32.6 0.8 copy-start.8
  33.4 21.6 %all-to-all-start.1 = ((bf16[8,8,32,128]{3,2,1,0:T(8,128)(2,1)}), bf16[8,8,32,128]{3,2,1,0:T(8,128)(2,1)S(1)}, u32[]{:S(2)}, u32[]{:S(2)}) async-start(bf16[8,8,32,128]{3,2,1,0:T(8,128)(2,1)} %get-tuple-element.72), calls=%async_computation.1 | async-start | bytes 1048576 | tf_op jit(solution)/shard_map/all_to_all | solution.py:358
  38.9 23.4 %collective-permute-start.6 = (bf16[8,256,128]{2,1,0:T(8,128)(2,1)}, bf16[8,256,128]{2,1,0:T(8,128)(2,1)S(1)}, u32[]{:S(2)}, u32[]{:S(2)}) collective-permute-start(bf16[8,256,128]{2,1,0:T(8,128)(2,1)} %copy-done.8), channel_id=1, source_target_pairs={{0,0},{1,16},{2,8},{3,24},{4,4},{5,20},{6,12},{7,28},{8,1},{9,17},... | collective-permute-start | bytes 1572872 | tf_op jit(solution)/shard_map/ppermute | solution.py:357
  48.6 0.7 copy-start.9
  49.3 0.7 copy-start.11
  50.0 0.7 copy-start.13
  55.0 17.9 %all-to-all-start.2 = ((bf16[32,32,128]{2,1,0:T(8,128)(2,1)}), bf16[32,32,128]{2,1,0:T(8,128)(2,1)S(1)}, u32[]{:S(2)}, u32[]{:S(2)}) async-start(bf16[32,32,128]{2,1,0:T(8,128)(2,1)} %get-tuple-element.73), calls=%async_computation.2 | async-start | bytes 524288 | tf_op jit(solution)/shard_map/all_to_all | solution.py:373
  73.9 19.0 %all-to-all-start.3 = ((bf16[16,4,32,128]{3,2,1,0:T(8,128)(2,1)}), bf16[16,4,32,128]{3,2,1,0:T(8,128)(2,1)S(1)}, u32[]{:S(2)}, u32[]{:S(2)}) async-start(bf16[16,4,32,128]{3,2,1,0:T(8,128)(2,1)} %broadcast_in_dim.15), calls=%async_computation.3 | async-start | bytes 1048576 | tf_op jit(solution)/shard_map/all_to_all | solution.py:379
  77.6 12.5 %collective-permute-start.10 = (bf16[8,8,32,128]{3,2,1,0:T(8,128)(2,1)S(1)}, bf16[8,8,32,128]{3,2,1,0:T(8,128)(2,1)S(1)}, u32[]{:S(2)}, u32[]{:S(2)}) collective-permute-start(bf16[8,8,32,128]{3,2,1,0:T(8,128)(2,1)S(1)} %all-to-all-done.1.refs_0_), channel_id=1, source_target_pairs={{0,1},{1,0},{2,3},{3,2},{4,5},{5,4},{6,7},{7,6},{8,9},{9,8},{10,11... | collective-permute-start | bytes 1572872 | tf_op jit(solution)/shard_map/ppermute | solution.py:334
  77.9 2.6 %copy-start.15 = (bf16[128,8]{0,1:T(8,128)(2,1)S(1)}, bf16[128,8]{0,1:T(8,128)(2,1)}, u32[]{:S(2)}) copy-start(bf16[128,8]{0,1:T(8,128)(2,1)} %param.15) | copy-start | bytes 6148
  77.9 2.6 %copy-start.14 = (bf16[3,256,128]{2,1,0:T(8,128)(2,1)S(1)}, bf16[3,256,128]{2,1,0:T(8,128)(2,1)}, u32[]{:S(2)}) copy-start(bf16[3,256,128]{2,1,0:T(8,128)(2,1)} %copy-done.13) | copy-start | bytes 589828
  77.9 3.7 %copy-start.12 = (bf16[3,256,128]{2,1,0:T(8,128)(2,1)S(1)}, bf16[3,256,128]{2,1,0:T(8,128)(2,1)}, u32[]{:S(2)}) copy-start(bf16[3,256,128]{2,1,0:T(8,128)(2,1)} %copy-done.11) | copy-start | bytes 589828
  78.4 3.3 %collective-permute-start.9 = (f32[8,128]{1,0:T(8,128)S(1)}, f32[8,128]{1,0:T(8,128)S(1)}, u32[]{:S(2)}, u32[]{:S(2)}) collective-permute-start(f32[8,128]{1,0:T(8,128)S(1)} %convolution_bitcast_fusion), channel_id=1, source_target_pairs={{0,3},{1,2},{2,1},{3,0},{4,7},{5,6},{6,5},{7,4},{8,11},{9,10},{10,... | collective-permute-start | bytes 12296 | tf_op jit(solution)/shard_map/ppermute | solution.py:334
  80.3 3.6 %collective-permute-start.8 = (f32[8,128]{1,0:T(8,128)S(1)}, f32[8,128]{1,0:T(8,128)S(1)}, u32[]{:S(2)}, u32[]{:S(2)}) collective-permute-start(f32[8,128]{1,0:T(8,128)S(1)} %convolution_bitcast_fusion), channel_id=1, source_target_pairs={{0,2},{1,3},{2,0},{3,1},{4,6},{5,7},{6,4},{7,5},{8,10},{9,11},{10,... | collective-permute-start | bytes 12296 | tf_op jit(solution)/shard_map/ppermute | solution.py:334
  80.6 3.4 %collective-permute-start.7 = (f32[8,128]{1,0:T(8,128)S(1)}, f32[8,128]{1,0:T(8,128)S(1)}, u32[]{:S(2)}, u32[]{:S(2)}) collective-permute-start(f32[8,128]{1,0:T(8,128)S(1)} %convolution_bitcast_fusion), channel_id=1, source_target_pairs={{0,1},{1,0},{2,3},{3,2},{4,5},{5,4},{6,7},{7,6},{8,9},{9,8},{10,11... | collective-permute-start | bytes 12296 | tf_op jit(solution)/shard_map/ppermute | solution.py:334
  80.6 3.4 %collective-permute-start.11 = (bf16[3,256,128]{2,1,0:T(8,128)(2,1)S(1)}, bf16[3,256,128]{2,1,0:T(8,128)(2,1)S(1)}, u32[]{:S(2)}, u32[]{:S(2)}) collective-permute-start(bf16[3,256,128]{2,1,0:T(8,128)(2,1)S(1)} %copy-done.14), channel_id=1, source_target_pairs={{0,1},{1,0},{2,3},{3,2},{4,5},{5,4},{6,7},{7,6},{8,9},{9,8},{10,11... | collective-permute-start | bytes 589832 | tf_op jit(solution)/shard_map/ppermute | solution.py:331
  81.6 8.5 %collective-permute-start.12 = (bf16[3,256,128]{2,1,0:T(8,128)(2,1)S(1)}, bf16[3,256,128]{2,1,0:T(8,128)(2,1)S(1)}, u32[]{:S(2)}, u32[]{:S(2)}) collective-permute-start(bf16[3,256,128]{2,1,0:T(8,128)(2,1)S(1)} %copy-done.12), channel_id=1, source_target_pairs={{0,5},{1,4},{2,7},{3,6},{4,1},{5,0},{6,3},{7,2},{8,13},{9,12},{10,... | collective-permute-start | bytes 589832 | tf_op jit(solution)/shard_map/ppermute | solution.py:331
  92.9 1.9 %collective-permute-start.15 = (bf16[16,4,32,128]{3,2,1,0:T(8,128)(2,1)S(1)}, bf16[16,4,32,128]{3,2,1,0:T(8,128)(2,1)S(1)}, u32[]{:S(2)}, u32[]{:S(2)}) collective-permute-start(bf16[16,4,32,128]{3,2,1,0:T(8,128)(2,1)S(1)} %all-to-all-done.3.near_ref), channel_id=1, source_target_pairs={{0,1},{1,0},{2,3},{3,2},{4,5},{5,4},{6,7},{7,6},{8,9},{9,8},{10,11... | collective-permute-start | bytes 1572872 | tf_op jit(solution)/shard_map/ppermute | solution.py:334
  97.0 19.3 %all-to-all-start.4 = ((bf16[8,272,128]{2,1,0:T(8,128)(2,1)}), bf16[8,272,128]{2,1,0:T(8,128)(2,1)S(1)}, u32[]{:S(2)}, u32[]{:S(2)}) async-start(bf16[8,272,128]{2,1,0:T(8,128)(2,1)} %d_right.1), calls=%async_computation.4 | async-start | bytes 1114112 | tf_op jit(solution)/shard_map/all_to_all | solution.py:408
  100.8 2.8 %copy-start.10 = (bf16[3,256,128]{2,1,0:T(8,128)(2,1)S(1)}, bf16[3,256,128]{2,1,0:T(8,128)(2,1)}, u32[]{:S(2)}) copy-start(bf16[3,256,128]{2,1,0:T(8,128)(2,1)} %copy-done.9) | copy-start | bytes 589828
  102.9 10.3 %collective-permute-start.13 = (bf16[16,64,128]{2,1,0:T(8,128)(2,1)S(1)}, bf16[16,64,128]{2,1,0:T(8,128)(2,1)S(1)}, u32[]{:S(2)}, u32[]{:S(2)}) collective-permute-start(bf16[16,64,128]{2,1,0:T(8,128)(2,1)S(1)} %get-tuple-element.84), channel_id=1, source_target_pairs={{0,2},{1,3},{2,0},{3,1},{4,6},{5,7},{6,4},{7,5},{8,10},{9,11},{10,... | collective-permute-start | bytes 786440 | tf_op jit(solution)/shard_map/ppermute | solution.py:334
  103.6 9.6 %collective-permute-start.14 = (bf16[3,256,128]{2,1,0:T(8,128)(2,1)S(1)}, bf16[3,256,128]{2,1,0:T(8,128)(2,1)S(1)}, u32[]{:S(2)}, u32[]{:S(2)}) collective-permute-start(bf16[3,256,128]{2,1,0:T(8,128)(2,1)S(1)} %copy-done.10), channel_id=1, source_target_pairs={{0,4},{1,5},{2,6},{3,7},{4,0},{5,1},{6,2},{7,3},{8,12},{9,13},{10,... | collective-permute-start | bytes 589832 | tf_op jit(solution)/shard_map/ppermute | solution.py:331

commit v4 on v3

--- a/solution.py
+++ b/solution.py
@@ -104,39 +104,23 @@
 
 def pack_kernel(groups, n_res, scalars, chain_ref, *refs):
     arrays, (left_ref, right_ref), refs = refs[:4], refs[4:6], refs[6:]
-    chain_out, outs, triangles = refs[0], refs[1 : 1 + groups], refs[1 + groups : -4]
-    whole, held, loaded, sent = refs[-4:]
+    chain_out, outs, triangles, held = refs[0], refs[1 : 1 + groups], refs[1 + groups : -1], refs[-1]
     place, b = scalars[0], scalars[1]
     block, rows = triangles[0].shape[1:3]
     cols = right_ref.shape[-2]
-    loads = [
-        pltpu.make_async_copy(x, whole.at[n], loaded.at[n]) for n, x in enumerate(arrays)
-    ]
-    for load in loads:
-        load.start()
-    copies = []
-    for s in range(n_res):
-        t = turn(b ^ s, n_res) * block
-        copies.append((left_ref.at[pl.ds(t, block)], triangles[s].at[0]))
-        for y in range(rows // cols):
-            copies.append(
-                (right_ref.at[y, b ^ s], triangles[s].at[1, :, y * cols : (y + 1) * cols])
-            )
-    copies = [pltpu.make_async_copy(x, y, sent.at[n]) for n, (x, y) in enumerate(copies)]
-    for copy in copies:
-        copy.start()
-    chain_out[...] = chain_ref[...]
-    for load in loads:
-        load.wait()
-    width = whole.shape[-1] // groups
+    width = held.shape[-1] // 4
     for g in range(groups):
         held[g] = jnp.concatenate(
-            [whole[n, :, :, g * width : (g + 1) * width] for n in range(4)], axis=-1
+            [x[:, :, g * width : (g + 1) * width] for x in arrays], axis=-1
         )
     for s in range(groups):
         outs[s][...] = held[place ^ s]
-    for copy in copies:
-        copy.wait()
+    for s in range(n_res):
+        t = turn(b ^ s, n_res) * block
+        triangles[s][0] = left_ref[pl.ds(t, block)]
+        for y in range(rows // cols):
+            triangles[s][1, :, y * cols : (y + 1) * cols] = right_ref[y, b ^ s]
+    chain_out[...] = chain_ref[...]
 
 
 def turn(b, n_res):
@@ -294,20 +278,16 @@
     place = a % spread[0] * spread[1] + b % spread[1]
     smem, vmem = [pl.BlockSpec(memory_space=s) for s in (pltpu.SMEM, pltpu.VMEM)]
     params = pltpu.CompilerParams(vmem_limit_bytes=12 * 1024 * 1024)
-    hbm = pl.BlockSpec(memory_space=pl.ANY)
     packed = (own, residues, 4 * width)
     right_parts = (n_seq // n_res, n_res, block, cols, pair_channels)
     pieces = pl.pallas_call(
         functools.partial(pack_kernel, groups, n_res),
-        in_specs=[smem, vmem] + [hbm] * 6,
+        in_specs=[smem] + [vmem] * 7,
         out_shape=[jax.ShapeDtypeStruct((1, residues), jnp.int32)]
         + [jax.ShapeDtypeStruct(packed, bf16)] * groups
         + [jax.ShapeDtypeStruct((2, block, rows, pair_channels), bf16)] * n_res,
         scratch_shapes=[
-            pltpu.VMEM((4,) + alignment_query.shape, bf16),
             pltpu.VMEM((groups,) + packed, bf16),
-            pltpu.SemaphoreType.DMA((4,)),
-            pltpu.SemaphoreType.DMA((n_res * (1 + n_seq // n_res),)),
         ],
         compiler_params=params,
         name="pack",

time: 118 us -> 117 us (level)
  waiting for transfers between devices: 49.7 us -> 51.6 us
  starting transfers between devices: 40.9 us -> 39.2 us
    all_to_all x1, starting transfers between devices: 5.56 us -> 4.22 us  [shards(): rights = lax.all_to_all(rights, 'seq', 0, 0, tiled=True)]
  transfers between devices with their start and end apart: 21 -> 21, of which waited for: 12 -> 12; matrix products, arithmetic and copies ran while one was open for 1% -> 1% of each run, Pallas kernels for 12% -> 11%
where the time goes in v4:
time: 117 us; the launch traced here: 116 us
  waiting for transfers between devices  51.6 us (44%)
  starting transfers between devices  39.2 us (34%)
  Pallas kernels  16.2 us (14%)
  local copies, waits for them, and re-layouts  6.67 us (6%)
  matrix products  1.65 us (1%)
    ppermute x6, waiting for transfers between devices, peer(): return lax.ppermute(x, BOTH, pairs)  27.8 us
    all_to_all x1, waiting for transfers between devices, shards(): share = lax.all_to_all(share, BOTH, 0, 0, tiled=True)  10.6 us
    pallas_call x1, Pallas kernels, shards(): pl.pallas_call(functools.partial(attention_kernel, n_seq, n_res, groups),...  8.01 us
    all_to_all x1, starting transfers between devices, shards(): lax.all_to_all(bias.reshape(devices, cols, held * rows), BOTH, 0, 0, tile...  7.3 us
    all_to_all x1, starting transfers between devices, shards(): share = lax.all_to_all(share, BOTH, 0, 0, tiled=True)  6.97 us
    ppermute x6, starting transfers between devices, peer(): return lax.ppermute(x, BOTH, pairs)  6.36 us
    ppermute x9, starting transfers between devices, partner(): return lax.ppermute(x, 'res', [(i, i ^ s) for i in range(n_res)])  5.12 us
    all_to_all x1, waiting for transfers between devices, shards(): rights = lax.all_to_all(rights, 'seq', 0, 0, tiled=True)  4.93 us
  transfers between devices with their start and end apart: 21, of which 12 were waited for; matrix products, arithmetic and copies ran while one was open for 1% of the time, Pallas kernels for 11%

profile of v4, /device:TPU:0, one launch (start us, length us, event | category | flops | bytes accessed | tf_op | source)
XLA Modules:
  0.0 116.4 jit_solution(13288572853759833281)
XLA Ops:
  0.6 0.0 copy-start
  0.6 1.0 copy-done
  1.7 1.2 %fusion.1 = f32[8,64,32]{1,0,2:T(8,128)S(1)} fusion(bf16[64,32,128]{2,1,0:T(8,128)(2,1)S(1)} %copy-done, bf16[128,8]{0,1:T(8,128)(2,1)} %param.15), kind=kOutput, calls=%fused_computation.3 | convolution fusion | flops 4194304 | bytes 591872 | tf_op jit(solution)/shard_map/ijc,ch->hij/dot_general | solution.py:269
  2.9 0.2 broadcast_in_dim.6
  3.1 0.0 copy-start.5
  3.1 0.0 copy-start.3
  3.1 0.0 copy-start.4
  3.1 0.9 broadcast_in_dim.14
  4.0 7.3 %all-to-all-start = ((f32[32,32,128]{2,1,0:T(8,128)}), f32[32,32,128]{2,1,0:T(8,128)S(1)}, u32[]{:S(2)}, u32[]{:S(2)}) async-start(f32[32,32,128]{2,1,0:T(8,128)} %bitcast.35), calls=%async_computation | async-start | bytes 1048576 | tf_op jit(solution)/shard_map/all_to_all | solution.py:274
  11.3 0.1 pad_add_fusion.1.scalars
  11.4 0.6 copy-done.7
  12.1 1.0 pack.1
  13.1 0.3 collective-permute-start
  13.4 1.7 %collective-permute-start.1 = (bf16[2,256,256]{2,1,0:T(8,128)(2,1)S(1)}, bf16[2,256,256]{2,1,0:T(8,128)(2,1)S(1)}, u32[]{:S(2)}, u32[]{:S(2)}) collective-permute-start(bf16[2,256,256]{2,1,0:T(8,128)(2,1)S(1)} %get-tuple-element.57), channel_id=1, source_target_pairs={{0,4},{1,5},{2,6},{3,7},{4,0},{5,1},{6,2},{7,3},{8,12},{9,13},{10,... | collective-permute-start | bytes 786440 | tf_op jit(solution)/shard_map/ppermute | solution.py:311
  15.1 0.0 collective-permute-start.2
  15.1 0.5 collective-permute-start.3
  15.5 1.7 %collective-permute-start.4 = (bf16[2,8,64,128]{3,2,1,0:T(8,128)(2,1)S(1)}, bf16[2,8,64,128]{3,2,1,0:T(8,128)(2,1)S(1)}, u32[]{:S(2)}, u32[]{:S(2)}) collective-permute-start(bf16[2,8,64,128]{3,2,1,0:T(8,128)(2,1)S(1)} %get-tuple-element.61), channel_id=1, source_target_pairs={{0,2},{1,3},{2,0},{3,1},{4,6},{5,7},{6,4},{7,5},{8,10},{9,11},{10,... | collective-permute-start | bytes 786440 | tf_op jit(solution)/shard_map/ppermute | solution.py:314
  17.2 8.3 %collective-permute-done.1.refs_2_ = bf16[2,256,256]{2,1,0:T(8,128)(2,1)S(1)} collective-permute-done((bf16[2,256,256]{2,1,0:T(8,128)(2,1)S(1)}, bf16[2,256,256]{2,1,0:T(8,128)(2,1)S(1)}, u32[]{:S(2)}, u32[]{:S(2)}) %collective-permute-start.1) | collective-permute-done | bytes 262176 | tf_op jit(solution)/shard_map/ppermute | solution.py:311
  25.5 5.9 %collective-permute-done.2.refs_3_ = bf16[2,256,256]{2,1,0:T(8,128)(2,1)S(1)} collective-permute-done((bf16[2,256,256]{2,1,0:T(8,128)(2,1)S(1)}, bf16[2,256,256]{2,1,0:T(8,128)(2,1)S(1)}, u32[]{:S(2)}, u32[]{:S(2)}) %collective-permute-start.2) | collective-permute-done | bytes 262176 | tf_op jit(solution)/shard_map/ppermute | solution.py:311
  31.4 0.6 collective-permute-done.5.refs_3_
  31.9 0.9 order.1
  32.8 0.8 copy-done.8
  33.6 0.0 all-to-all-done.bias_ref
  33.6 4.2 %all-to-all-start.1 = ((bf16[8,8,32,128]{3,2,1,0:T(8,128)(2,1)}), bf16[8,8,32,128]{3,2,1,0:T(8,128)(2,1)S(1)}, u32[]{:S(2)}, u32[]{:S(2)}) async-start(bf16[8,8,32,128]{3,2,1,0:T(8,128)(2,1)} %get-tuple-element.72), calls=%async_computation.1 | async-start | bytes 1048576 | tf_op jit(solution)/shard_map/all_to_all | solution.py:338
  37.8 1.7 %collective-permute-start.6 = (bf16[8,256,128]{2,1,0:T(8,128)(2,1)}, bf16[8,256,128]{2,1,0:T(8,128)(2,1)S(1)}, u32[]{:S(2)}, u32[]{:S(2)}) collective-permute-start(bf16[8,256,128]{2,1,0:T(8,128)(2,1)} %copy-done.8), channel_id=1, source_target_pairs={{0,0},{1,16},{2,8},{3,24},{4,4},{5,20},{6,12},{7,28},{8,1},{9,17},... | collective-permute-start | bytes 1572872 | tf_op jit(solution)/shard_map/ppermute | solution.py:337
  39.5 8.0 %attention.1 = (bf16[3,256,128]{2,1,0:T(8,128)(2,1)S(1)}, bf16[3,256,128]{2,1,0:T(8,128)(2,1)S(1)}, bf16[3,256,128]{2,1,0:T(8,128)(2,1)S(1)}, bf16[3,256,128]{2,1,0:T(8,128)(2,1)S(1)}, bf16[32,32,128]{2,1,0:T(8,128)(2,1)}) custom-call(f32[32,32,128]{2,1,0:T(8,128)S(1)} %all-to-all-done.bias_ref, s32[1,256]{1,0:T(1,128)S(1)} %get-tuple-element.54.chain_ref, ...), custom_call_target="tpu_custom_call" | custom-call | tf_op jit(solution)/shard_map/attention/pallas_call | solution.py:342
  47.5 0.7 copy-done.9
  48.2 0.7 copy-done.11
  48.8 0.7 copy-done.13
  49.5 4.9 %all-to-all-done.1.refs_0_ = bf16[8,8,32,128]{3,2,1,0:T(8,128)(2,1)S(1)} async-done(((bf16[8,8,32,128]{3,2,1,0:T(8,128)(2,1)}), bf16[8,8,32,128]{3,2,1,0:T(8,128)(2,1)S(1)}, u32[]{:S(2)}, u32[]{:S(2)}) %all-to-all-start.1) | async-done | bytes 524320 | tf_op jit(solution)/shard_map/all_to_all | solution.py:338
  54.4 7.0 %all-to-all-start.2 = ((bf16[32,32,128]{2,1,0:T(8,128)(2,1)}), bf16[32,32,128]{2,1,0:T(8,128)(2,1)S(1)}, u32[]{:S(2)}, u32[]{:S(2)}) async-start(bf16[32,32,128]{2,1,0:T(8,128)(2,1)} %get-tuple-element.73), calls=%async_computation.2 | async-start | bytes 524288 | tf_op jit(solution)/shard_map/all_to_all | solution.py:353
  61.4 0.0 collective-permute-done.6.left
  61.4 10.6 %all-to-all-done.2 = bf16[32,32,128]{2,1,0:T(8,128)(2,1)S(1)} async-done(((bf16[32,32,128]{2,1,0:T(8,128)(2,1)}), bf16[32,32,128]{2,1,0:T(8,128)(2,1)S(1)}, u32[]{:S(2)}, u32[]{:S(2)}) %all-to-all-start.2) | async-done | bytes 262176 | tf_op jit(solution)/shard_map/all_to_all | solution.py:353
  72.1 0.9 broadcast_in_dim.15
  73.0 3.8 %all-to-all-start.3 = ((bf16[16,4,32,128]{3,2,1,0:T(8,128)(2,1)}), bf16[16,4,32,128]{3,2,1,0:T(8,128)(2,1)S(1)}, u32[]{:S(2)}, u32[]{:S(2)}) async-start(bf16[16,4,32,128]{3,2,1,0:T(8,128)(2,1)} %broadcast_in_dim.15), calls=%async_computation.3 | async-start | bytes 1048576 | tf_op jit(solution)/shard_map/all_to_all | solution.py:359
  76.8 0.1 collective-permute-start.10
  76.8 0.1 copy.17
  76.9 0.1 reshape_reshape.3
  77.1 0.0 copy-start.15
  77.1 0.0 copy-start.14
  77.1 0.4 convolution_bitcast_fusion
  77.5 2.0 %collective-permute-start.9 = (f32[8,128]{1,0:T(8,128)S(1)}, f32[8,128]{1,0:T(8,128)S(1)}, u32[]{:S(2)}, u32[]{:S(2)}) collective-permute-start(f32[8,128]{1,0:T(8,128)S(1)} %convolution_bitcast_fusion), channel_id=1, source_target_pairs={{0,3},{1,2},{2,1},{3,0},{4,7},{5,6},{6,5},{7,4},{8,11},{9,10},{10,... | collective-permute-start | bytes 12296 | tf_op jit(solution)/shard_map/ppermute | solution.py:314
  79.5 0.2 collective-permute-start.8
  79.7 0.6 collective-permute-start.11
  80.3 0.5 collective-permute-done.9
  80.8 1.8 %collective-permute-start.12 = (bf16[3,256,128]{2,1,0:T(8,128)(2,1)S(1)}, bf16[3,256,128]{2,1,0:T(8,128)(2,1)S(1)}, u32[]{:S(2)}, u32[]{:S(2)}) collective-permute-start(bf16[3,256,128]{2,1,0:T(8,128)(2,1)S(1)} %copy-done.12), channel_id=1, source_target_pairs={{0,5},{1,4},{2,7},{3,6},{4,1},{5,0},{6,3},{7,2},{8,13},{9,12},{10,... | collective-permute-start | bytes 589832 | tf_op jit(solution)/shard_map/ppermute | solution.py:311
  82.6 0.5 collective-permute-done.8
  83.1 0.0 collective-permute-done.7
  83.1 0.0 collective-permute-done.11.refs_1_
  83.1 6.1 %collective-permute-done.12.refs_3_ = bf16[3,256,128]{2,1,0:T(8,128)(2,1)S(1)} collective-permute-done((bf16[3,256,128]{2,1,0:T(8,128)(2,1)S(1)}, bf16[3,256,128]{2,1,0:T(8,128)(2,1)S(1)}, u32[]{:S(2)}, u32[]{:S(2)}) %collective-permute-start.12) | collective-permute-done | bytes 196640 | tf_op jit(solution)/shard_map/ppermute | solution.py:311
  89.3 0.0 collective-permute-done.10.refs_1_
  89.3 2.7 %all-to-all-done.3.near_ref = bf16[16,4,32,128]{3,2,1,0:T(8,128)(2,1)S(1)} async-done(((bf16[16,4,32,128]{3,2,1,0:T(8,128)(2,1)}), bf16[16,4,32,128]{3,2,1,0:T(8,128)(2,1)S(1)}, u32[]{:S(2)}, u32[]{:S(2)}) %all-to-all-start.3) | async-done | bytes 524320 | tf_op jit(solution)/shard_map/all_to_all | solution.py:359
  92.0 0.0 collective-permute-start.15
  92.0 1.9 %collective-permute-done.15.far_ref = bf16[16,4,32,128]{3,2,1,0:T(8,128)(2,1)S(1)} collective-permute-done((bf16[16,4,32,128]{3,2,1,0:T(8,128)(2,1)S(1)}, bf16[16,4,32,128]{3,2,1,0:T(8,128)(2,1)S(1)}, u32[]{:S(2)}, u32[]{:S(2)}) %collective-permute-start.15) | collective-permute-done | bytes 524320 | tf_op jit(solution)/shard_map/ppermute | solution.py:314
  93.9 2.2 %d_right.1 = bf16[8,272,128]{2,1,0:T(8,128)(2,1)} custom-call(s32[1]{0:T(128)} %bitcast.1.scalars, bf16[16,4,32,128]{3,2,1,0:T(8,128)(2,1)S(1)} %all-to-all-done.3.near_ref, bf16[16,4,32,128]{3,2,1,0:T(8,128)(2,1)S(1)} %collective-permute-done.15.far_ref, f32[2,8,128]{2,1,0:T(8,128)S(1)} %pad_maximum_fusion.extra_ref, ...), custom_call_target="tpu_custom_call" | custom-call | tf_op jit(solution)/shard_map/d_right/pallas_call | solution.py:378
  96.1 3.8 %all-to-all-start.4 = ((bf16[8,272,128]{2,1,0:T(8,128)(2,1)}), bf16[8,272,128]{2,1,0:T(8,128)(2,1)S(1)}, u32[]{:S(2)}, u32[]{:S(2)}) async-start(bf16[8,272,128]{2,1,0:T(8,128)(2,1)} %d_right.1), calls=%async_computation.4 | async-start | bytes 1114112 | tf_op jit(solution)/shard_map/all_to_all | solution.py:388
  99.9 0.1 pad_add_fusion.scalars
  99.9 2.1 %d_left.1 = (bf16[16,64,128]{2,1,0:T(8,128)(2,1)S(1)}, bf16[16,64,128]{2,1,0:T(8,128)(2,1)S(1)}) custom-call(s32[2]{0:T(128)S(1)} %pad_add_fusion.scalars, bf16[16,4,32,128]{3,2,1,0:T(8,128)(2,1)S(1)} %all-to-all-done.3.near_ref, f32[2,8,128]{2,1,0:T(8,128)S(1)} %pad_maximum_fusion.extra_ref, bf16[8,8,32,128]{3,2,1,0:T(8,128)(2,1)S(1)} %all-to-all-done.1.refs_0_, ...), custom_call_target="tpu_custom_call" | custom-call | tf_op jit(solution)/shard_map/d_left/pallas_call | solution.py:391
  102.0 0.7 collective-permute-start.13
  102.7 2.0 %collective-permute-start.14 = (bf16[3,256,128]{2,1,0:T(8,128)(2,1)S(1)}, bf16[3,256,128]{2,1,0:T(8,128)(2,1)S(1)}, u32[]{:S(2)}, u32[]{:S(2)}) collective-permute-start(bf16[3,256,128]{2,1,0:T(8,128)(2,1)S(1)} %copy-done.10), channel_id=1, source_target_pairs={{0,4},{1,5},{2,6},{3,7},{4,0},{5,1},{6,2},{7,3},{8,12},{9,13},{10,... | collective-permute-start | bytes 589832 | tf_op jit(solution)/shard_map/ppermute | solution.py:311
  104.8 7.6 %collective-permute-done.14.refs_2_ = bf16[3,256,128]{2,1,0:T(8,128)(2,1)S(1)} collective-permute-done((bf16[3,256,128]{2,1,0:T(8,128)(2,1)S(1)}, bf16[3,256,128]{2,1,0:T(8,128)(2,1)S(1)}, u32[]{:S(2)}, u32[]{:S(2)}) %collective-permute-start.14) | collective-permute-done | bytes 196640 | tf_op jit(solution)/shard_map/ppermute | solution.py:311
  112.3 1.1 unpack.1
  113.4 2.0 %all-to-all-done.4.received_ref = bf16[8,272,128]{2,1,0:T(8,128)(2,1)S(1)} async-done(((bf16[8,272,128]{2,1,0:T(8,128)(2,1)}), bf16[8,272,128]{2,1,0:T(8,128)(2,1)S(1)}, u32[]{:S(2)}, u32[]{:S(2)}) %all-to-all-start.4) | async-done | bytes 557088 | tf_op jit(solution)/shard_map/all_to_all | solution.py:388
  115.3 1.0 place.1
  (32 shorter events, 0.1 us)
Async XLA Ops:
  0.6 1.0 copy-start
  1.7 9.7 %copy-start.6 = (bf16[2,256,256]{2,1,0:T(8,128)(2,1)S(1)}, bf16[2,256,256]{2,1,0:T(8,128)(2,1)}, u32[]{:S(2)}) copy-start(bf16[2,256,256]{2,1,0:T(8,128)(2,1)} %refs_3_.1) | copy-start | bytes 786436
  3.1 8.3 %copy-start.5 = (bf16[2,256,256]{2,1,0:T(8,128)(2,1)S(1)}, bf16[2,256,256]{2,1,0:T(8,128)(2,1)}, u32[]{:S(2)}) copy-start(bf16[2,256,256]{2,1,0:T(8,128)(2,1)} %refs_2_.1) | copy-start | bytes 786436
  3.1 8.3 %copy-start.3 = (bf16[2,256,256]{2,1,0:T(8,128)(2,1)S(1)}, bf16[2,256,256]{2,1,0:T(8,128)(2,1)}, u32[]{:S(2)}) copy-start(bf16[2,256,256]{2,1,0:T(8,128)(2,1)} %refs_0_.1) | copy-start | bytes 786436
  3.1 8.3 %copy-start.4 = (bf16[2,256,256]{2,1,0:T(8,128)(2,1)S(1)}, bf16[2,256,256]{2,1,0:T(8,128)(2,1)}, u32[]{:S(2)}) copy-start(bf16[2,256,256]{2,1,0:T(8,128)(2,1)} %refs_1_.1) | copy-start | bytes 786436
  4.0 7.4 %copy-start.1 = (bf16[32,64,128]{2,1,0:T(8,128)(2,1)S(1)}, bf16[32,64,128]{2,1,0:T(8,128)(2,1)}, u32[]{:S(2)}) copy-start(bf16[32,64,128]{2,1,0:T(8,128)(2,1)} %refs_4_.1) | copy-start | bytes 1572868
  4.0 7.4 %copy-start.2 = (bf16[64,32,128]{2,1,0:T(8,128)(2,1)S(1)}, bf16[64,32,128]{2,1,0:T(8,128)(2,1)}, u32[]{:S(2)}) copy-start(bf16[64,32,128]{2,1,0:T(8,128)(2,1)} %param.17) | copy-start | bytes 1572868
  4.0 29.6 %all-to-all-start = ((f32[32,32,128]{2,1,0:T(8,128)}), f32[32,32,128]{2,1,0:T(8,128)S(1)}, u32[]{:S(2)}, u32[]{:S(2)}) async-start(f32[32,32,128]{2,1,0:T(8,128)} %bitcast.35), calls=%async_computation | async-start | bytes 1048576 | tf_op jit(solution)/shard_map/all_to_all | solution.py:274
  11.4 0.7 copy-start.7
  13.1 4.1 %collective-permute-start = (bf16[2,256,256]{2,1,0:T(8,128)(2,1)S(1)}, bf16[2,256,256]{2,1,0:T(8,128)(2,1)S(1)}, u32[]{:S(2)}, u32[]{:S(2)}) collective-permute-start(bf16[2,256,256]{2,1,0:T(8,128)(2,1)S(1)} %get-tuple-element.56), channel_id=1, source_target_pairs={{0,1},{1,0},{2,3},{3,2},{4,5},{5,4},{6,7},{7,6},{8,9},{9,8},{10,11... | collective-permute-start | bytes 786440 | tf_op jit(solution)/shard_map/ppermute | solution.py:311
  13.4 12.1 %collective-permute-start.1 = (bf16[2,256,256]{2,1,0:T(8,128)(2,1)S(1)}, bf16[2,256,256]{2,1,0:T(8,128)(2,1)S(1)}, u32[]{:S(2)}, u32[]{:S(2)}) collective-permute-start(bf16[2,256,256]{2,1,0:T(8,128)(2,1)S(1)} %get-tuple-element.57), channel_id=1, source_target_pairs={{0,4},{1,5},{2,6},{3,7},{4,0},{5,1},{6,2},{7,3},{8,12},{9,13},{10,... | collective-permute-start | bytes 786440 | tf_op jit(solution)/shard_map/ppermute | solution.py:311
  15.1 16.3 %collective-permute-start.2 = (bf16[2,256,256]{2,1,0:T(8,128)(2,1)S(1)}, bf16[2,256,256]{2,1,0:T(8,128)(2,1)S(1)}, u32[]{:S(2)}, u32[]{:S(2)}) collective-permute-start(bf16[2,256,256]{2,1,0:T(8,128)(2,1)S(1)} %get-tuple-element.58), channel_id=1, source_target_pairs={{0,5},{1,4},{2,7},{3,6},{4,1},{5,0},{6,3},{7,2},{8,13},{9,12},{10,... | collective-permute-start | bytes 786440 | tf_op jit(solution)/shard_map/ppermute | solution.py:311
  15.1 16.3 %collective-permute-start.3 = (bf16[2,8,64,128]{3,2,1,0:T(8,128)(2,1)S(1)}, bf16[2,8,64,128]{3,2,1,0:T(8,128)(2,1)S(1)}, u32[]{:S(2)}, u32[]{:S(2)}) collective-permute-start(bf16[2,8,64,128]{3,2,1,0:T(8,128)(2,1)S(1)} %get-tuple-element.60), channel_id=1, source_target_pairs={{0,1},{1,0},{2,3},{3,2},{4,5},{5,4},{6,7},{7,6},{8,9},{9,8},{10,11... | collective-permute-start | bytes 786440 | tf_op jit(solution)/shard_map/ppermute | solution.py:314
  15.5 15.8 %collective-permute-start.4 = (bf16[2,8,64,128]{3,2,1,0:T(8,128)(2,1)S(1)}, bf16[2,8,64,128]{3,2,1,0:T(8,128)(2,1)S(1)}, u32[]{:S(2)}, u32[]{:S(2)}) collective-permute-start(bf16[2,8,64,128]{3,2,1,0:T(8,128)(2,1)S(1)} %get-tuple-element.61), channel_id=1, source_target_pairs={{0,2},{1,3},{2,0},{3,1},{4,6},{5,7},{6,4},{7,5},{8,10},{9,11},{10,... | collective-permute-start | bytes 786440 | tf_op jit(solution)/shard_map/ppermute | solution.py:314
  17.2 14.7 %collective-permute-start.5 = (bf16[2,8,64,128]{3,2,1,0:T(8,128)(2,1)S(1)}, bf16[2,8,64,128]{3,2,1,0:T(8,128)(2,1)S(1)}, u32[]{:S(2)}, u32[]{:S(2)}) collective-permute-start(bf16[2,8,64,128]{3,2,1,0:T(8,128)(2,1)S(1)} %get-tuple-element.62), channel_id=1, source_target_pairs={{0,3},{1,2},{2,1},{3,0},{4,7},{5,6},{6,5},{7,4},{8,11},{9,10},{10,... | collective-permute-start | bytes 786440 | tf_op jit(solution)/shard_map/ppermute | solution.py:314
  32.8 0.8 copy-start.8
  33.6 20.9 %all-to-all-start.1 = ((bf16[8,8,32,128]{3,2,1,0:T(8,128)(2,1)}), bf16[8,8,32,128]{3,2,1,0:T(8,128)(2,1)S(1)}, u32[]{:S(2)}, u32[]{:S(2)}) async-start(bf16[8,8,32,128]{3,2,1,0:T(8,128)(2,1)} %get-tuple-element.72), calls=%async_computation.1 | async-start | bytes 1048576 | tf_op jit(solution)/shard_map/all_to_all | solution.py:338
  37.8 23.6 %collective-permute-start.6 = (bf16[8,256,128]{2,1,0:T(8,128)(2,1)}, bf16[8,256,128]{2,1,0:T(8,128)(2,1)S(1)}, u32[]{:S(2)}, u32[]{:S(2)}) collective-permute-start(bf16[8,256,128]{2,1,0:T(8,128)(2,1)} %copy-done.8), channel_id=1, source_target_pairs={{0,0},{1,16},{2,8},{3,24},{4,4},{5,20},{6,12},{7,28},{8,1},{9,17},... | collective-permute-start | bytes 1572872 | tf_op jit(solution)/shard_map/ppermute | solution.py:337
  47.5 0.7 copy-start.9
  48.2 0.7 copy-start.11
  48.8 0.7 copy-start.13
  54.4 17.6 %all-to-all-start.2 = ((bf16[32,32,128]{2,1,0:T(8,128)(2,1)}), bf16[32,32,128]{2,1,0:T(8,128)(2,1)S(1)}, u32[]{:S(2)}, u32[]{:S(2)}) async-start(bf16[32,32,128]{2,1,0:T(8,128)(2,1)} %get-tuple-element.73), calls=%async_computation.2 | async-start | bytes 524288 | tf_op jit(solution)/shard_map/all_to_all | solution.py:353
  73.0 19.0 %all-to-all-start.3 = ((bf16[16,4,32,128]{3,2,1,0:T(8,128)(2,1)}), bf16[16,4,32,128]{3,2,1,0:T(8,128)(2,1)S(1)}, u32[]{:S(2)}, u32[]{:S(2)}) async-start(bf16[16,4,32,128]{3,2,1,0:T(8,128)(2,1)} %broadcast_in_dim.15), calls=%async_computation.3 | async-start | bytes 1048576 | tf_op jit(solution)/shard_map/all_to_all | solution.py:359
  76.8 12.5 %collective-permute-start.10 = (bf16[8,8,32,128]{3,2,1,0:T(8,128)(2,1)S(1)}, bf16[8,8,32,128]{3,2,1,0:T(8,128)(2,1)S(1)}, u32[]{:S(2)}, u32[]{:S(2)}) collective-permute-start(bf16[8,8,32,128]{3,2,1,0:T(8,128)(2,1)S(1)} %all-to-all-done.1.refs_0_), channel_id=1, source_target_pairs={{0,1},{1,0},{2,3},{3,2},{4,5},{5,4},{6,7},{7,6},{8,9},{9,8},{10,11... | collective-permute-start | bytes 1572872 | tf_op jit(solution)/shard_map/ppermute | solution.py:314
  77.1 2.6 %copy-start.15 = (bf16[128,8]{0,1:T(8,128)(2,1)S(1)}, bf16[128,8]{0,1:T(8,128)(2,1)}, u32[]{:S(2)}) copy-start(bf16[128,8]{0,1:T(8,128)(2,1)} %param.15) | copy-start | bytes 6148
  77.1 2.6 %copy-start.14 = (bf16[3,256,128]{2,1,0:T(8,128)(2,1)S(1)}, bf16[3,256,128]{2,1,0:T(8,128)(2,1)}, u32[]{:S(2)}) copy-start(bf16[3,256,128]{2,1,0:T(8,128)(2,1)} %copy-done.13) | copy-start | bytes 589828
  77.1 3.7 %copy-start.12 = (bf16[3,256,128]{2,1,0:T(8,128)(2,1)S(1)}, bf16[3,256,128]{2,1,0:T(8,128)(2,1)}, u32[]{:S(2)}) copy-start(bf16[3,256,128]{2,1,0:T(8,128)(2,1)} %copy-done.11) | copy-start | bytes 589828
  77.5 3.3 %collective-permute-start.9 = (f32[8,128]{1,0:T(8,128)S(1)}, f32[8,128]{1,0:T(8,128)S(1)}, u32[]{:S(2)}, u32[]{:S(2)}) collective-permute-start(f32[8,128]{1,0:T(8,128)S(1)} %convolution_bitcast_fusion), channel_id=1, source_target_pairs={{0,3},{1,2},{2,1},{3,0},{4,7},{5,6},{6,5},{7,4},{8,11},{9,10},{10,... | collective-permute-start | bytes 12296 | tf_op jit(solution)/shard_map/ppermute | solution.py:314
  79.5 3.6 %collective-permute-start.8 = (f32[8,128]{1,0:T(8,128)S(1)}, f32[8,128]{1,0:T(8,128)S(1)}, u32[]{:S(2)}, u32[]{:S(2)}) collective-permute-start(f32[8,128]{1,0:T(8,128)S(1)} %convolution_bitcast_fusion), channel_id=1, source_target_pairs={{0,2},{1,3},{2,0},{3,1},{4,6},{5,7},{6,4},{7,5},{8,10},{9,11},{10,... | collective-permute-start | bytes 12296 | tf_op jit(solution)/shard_map/ppermute | solution.py:314
  79.7 3.4 %collective-permute-start.7 = (f32[8,128]{1,0:T(8,128)S(1)}, f32[8,128]{1,0:T(8,128)S(1)}, u32[]{:S(2)}, u32[]{:S(2)}) collective-permute-start(f32[8,128]{1,0:T(8,128)S(1)} %convolution_bitcast_fusion), channel_id=1, source_target_pairs={{0,1},{1,0},{2,3},{3,2},{4,5},{5,4},{6,7},{7,6},{8,9},{9,8},{10,11... | collective-permute-start | bytes 12296 | tf_op jit(solution)/shard_map/ppermute | solution.py:314
  79.7 3.4 %collective-permute-start.11 = (bf16[3,256,128]{2,1,0:T(8,128)(2,1)S(1)}, bf16[3,256,128]{2,1,0:T(8,128)(2,1)S(1)}, u32[]{:S(2)}, u32[]{:S(2)}) collective-permute-start(bf16[3,256,128]{2,1,0:T(8,128)(2,1)S(1)} %copy-done.14), channel_id=1, source_target_pairs={{0,1},{1,0},{2,3},{3,2},{4,5},{5,4},{6,7},{7,6},{8,9},{9,8},{10,11... | collective-permute-start | bytes 589832 | tf_op jit(solution)/shard_map/ppermute | solution.py:311
  80.8 8.5 %collective-permute-start.12 = (bf16[3,256,128]{2,1,0:T(8,128)(2,1)S(1)}, bf16[3,256,128]{2,1,0:T(8,128)(2,1)S(1)}, u32[]{:S(2)}, u32[]{:S(2)}) collective-permute-start(bf16[3,256,128]{2,1,0:T(8,128)(2,1)S(1)} %copy-done.12), channel_id=1, source_target_pairs={{0,5},{1,4},{2,7},{3,6},{4,1},{5,0},{6,3},{7,2},{8,13},{9,12},{10,... | collective-permute-start | bytes 589832 | tf_op jit(solution)/shard_map/ppermute | solution.py:311
  92.0 1.9 %collective-permute-start.15 = (bf16[16,4,32,128]{3,2,1,0:T(8,128)(2,1)S(1)}, bf16[16,4,32,128]{3,2,1,0:T(8,128)(2,1)S(1)}, u32[]{:S(2)}, u32[]{:S(2)}) collective-permute-start(bf16[16,4,32,128]{3,2,1,0:T(8,128)(2,1)S(1)} %all-to-all-done.3.near_ref), channel_id=1, source_target_pairs={{0,1},{1,0},{2,3},{3,2},{4,5},{5,4},{6,7},{7,6},{8,9},{9,8},{10,11... | collective-permute-start | bytes 1572872 | tf_op jit(solution)/shard_map/ppermute | solution.py:314
  96.1 19.2 %all-to-all-start.4 = ((bf16[8,272,128]{2,1,0:T(8,128)(2,1)}), bf16[8,272,128]{2,1,0:T(8,128)(2,1)S(1)}, u32[]{:S(2)}, u32[]{:S(2)}) async-start(bf16[8,272,128]{2,1,0:T(8,128)(2,1)} %d_right.1), calls=%async_computation.4 | async-start | bytes 1114112 | tf_op jit(solution)/shard_map/all_to_all | solution.py:388
  99.9 2.8 %copy-start.10 = (bf16[3,256,128]{2,1,0:T(8,128)(2,1)S(1)}, bf16[3,256,128]{2,1,0:T(8,128)(2,1)}, u32[]{:S(2)}) copy-start(bf16[3,256,128]{2,1,0:T(8,128)(2,1)} %copy-done.9) | copy-start | bytes 589828
  102.0 10.3 %collective-permute-start.13 = (bf16[16,64,128]{2,1,0:T(8,128)(2,1)S(1)}, bf16[16,64,128]{2,1,0:T(8,128)(2,1)S(1)}, u32[]{:S(2)}, u32[]{:S(2)}) collective-permute-start(bf16[16,64,128]{2,1,0:T(8,128)(2,1)S(1)} %get-tuple-element.84), channel_id=1, source_target_pairs={{0,2},{1,3},{2,0},{3,1},{4,6},{5,7},{6,4},{7,5},{8,10},{9,11},{10,... | collective-permute-start | bytes 786440 | tf_op jit(solution)/shard_map/ppermute | solution.py:314
  102.7 9.6 %collective-permute-start.14 = (bf16[3,256,128]{2,1,0:T(8,128)(2,1)S(1)}, bf16[3,256,128]{2,1,0:T(8,128)(2,1)S(1)}, u32[]{:S(2)}, u32[]{:S(2)}) collective-permute-start(bf16[3,256,128]{2,1,0:T(8,128)(2,1)S(1)} %copy-done.10), channel_id=1, source_target_pairs={{0,4},{1,5},{2,6},{3,7},{4,0},{5,1},{6,2},{7,3},{8,12},{9,13},{10,... | collective-permute-start | bytes 589832 | tf_op jit(solution)/shard_map/ppermute | solution.py:311

commit v5 on v4

--- a/solution.py
+++ b/solution.py
@@ -102,9 +102,9 @@
             )
 
 
-def pack_kernel(groups, n_res, scalars, chain_ref, *refs):
+def pack_kernel(groups, n_res, scalars, *refs):
     arrays, (left_ref, right_ref), refs = refs[:4], refs[4:6], refs[6:]
-    chain_out, outs, triangles, held = refs[0], refs[1 : 1 + groups], refs[1 + groups : -1], refs[-1]
+    outs, triangles, held = refs[:groups], refs[groups:-1], refs[-1]
     place, b = scalars[0], scalars[1]
     block, rows = triangles[0].shape[1:3]
     cols = right_ref.shape[-2]
@@ -120,22 +120,27 @@
         triangles[s][0] = left_ref[pl.ds(t, block)]
         for y in range(rows // cols):
             triangles[s][1, :, y * cols : (y + 1) * cols] = right_ref[y, b ^ s]
-    chain_out[...] = chain_ref[...]
 
 
 def turn(b, n_res):
     return b % 2 * (n_res // 2) + b // 2
 
 
-def order_kernel(scalars, *refs):
-    pieces, (left_ref, chunks_ref) = refs[:-2], refs[-2:]
+def order_rights_kernel(scalars, *refs):
+    pieces, chunks_ref = refs[:-1], refs[-1]
     rows, cols = pieces[0].shape[2], chunks_ref.shape[2]
     each = rows // cols
     for s, piece in enumerate(pieces):
+        for y in range(each):
+            chunks_ref[(scalars[0] ^ s) * each + y] = piece[1, :, y * cols : (y + 1) * cols]
+
+
+def order_lefts_kernel(scalars, *refs):
+    pieces, left_ref = refs[:-1], refs[-1]
+    rows = pieces[0].shape[2]
+    for s, piece in enumerate(pieces):
         b = scalars[0] ^ s
         left_ref[:, pl.ds(pl.multiple_of(b * rows, rows), rows), :] = piece[0]
-        for y in range(each):
-            chunks_ref[b * each + y] = piece[1, :, y * cols : (y + 1) * cols]
 
 
 def pairs_of(block):
@@ -282,9 +287,8 @@
     right_parts = (n_seq // n_res, n_res, block, cols, pair_channels)
     pieces = pl.pallas_call(
         functools.partial(pack_kernel, groups, n_res),
-        in_specs=[smem] + [vmem] * 7,
-        out_shape=[jax.ShapeDtypeStruct((1, residues), jnp.int32)]
-        + [jax.ShapeDtypeStruct(packed, bf16)] * groups
+        in_specs=[smem] + [vmem] * 6,
+        out_shape=[jax.ShapeDtypeStruct(packed, bf16)] * groups
         + [jax.ShapeDtypeStruct((2, block, rows, pair_channels), bf16)] * n_res,
         scratch_shapes=[
             pltpu.VMEM((groups,) + packed, bf16),
@@ -293,7 +297,6 @@
         name="pack",
     )(
         jnp.stack([place, b]).astype(jnp.int32),
-        chain_index_per_residue.reshape(1, residues),
         alignment_query,
         alignment_key,
         attended_vectors,
@@ -301,7 +304,7 @@
         left_operand_input,
         right_operand_input.reshape(right_parts),
     )
-    chain, arrays, triangles = pieces[0], pieces[1 : 1 + groups], pieces[1 + groups :]
+    arrays, triangles = pieces[:groups], pieces[groups:]
 
     def peer(x, s):
         pairs = [
@@ -319,15 +322,19 @@
     half = n_seq // inner
     triangles = list(triangles[:1]) + [partner(triangles[s], s) for s in range(1, n_res)]
     arrays, triangles = lax.optimization_barrier((arrays, triangles))
-    left, rights = pl.pallas_call(
-        order_kernel,
+    rights = pl.pallas_call(
+        order_rights_kernel,
         in_specs=[smem] + [vmem] * n_res,
-        out_shape=[
-            jax.ShapeDtypeStruct((block, residues, pair_channels), bf16),
-            jax.ShapeDtypeStruct((n_seq, block, cols, pair_channels), bf16),
-        ],
-        compiler_params=params,
-        name="order",
+        out_shape=jax.ShapeDtypeStruct((n_seq, block, cols, pair_channels), bf16),
+        compiler_params=params,
+        name="order_rights",
+    )(b.reshape(1), *triangles)
+    left = pl.pallas_call(
+        order_lefts_kernel,
+        in_specs=[smem] + [vmem] * n_res,
+        out_shape=jax.ShapeDtypeStruct((block, residues, pair_channels), bf16),
+        compiler_params=params,
+        name="order_lefts",
     )(b.reshape(1), *triangles)
     pairs = []
     for d in range(devices):
@@ -345,8 +352,9 @@
         + [jax.ShapeDtypeStruct(bias.shape, bf16)],
         scratch_shapes=[pltpu.VMEM((held, residues, residues), f32)] * 2,
         compiler_params=params,
+        cost_estimate=pl.CostEstimate(flops=4 * 10**9, bytes_accessed=0, transcendentals=0),
         name="attention",
-    )(bias, chain, *arrays)
+    )(bias, chain_index_per_residue.reshape(1, residues), *arrays)
     grads, share = outs[:groups], outs[groups]
 
     share, rights = lax.optimization_barrier((share, rights))

time: 117 us -> 116 us (level)
    unnamed x32 -> x50, local copies, waits for them, and re-layouts: 4.55 us -> 4.8 us
where the time goes in v5:
time: 116 us
  waiting for transfers between devices  51.3 us (44%)
  starting transfers between devices  38.3 us (33%)
  Pallas kernels  16.2 us (14%)
  local copies, waits for them, and re-layouts  6.92 us (6%)
  matrix products  1.65 us (1%)
    ppermute x6, waiting for transfers between devices, peer(): return lax.ppermute(x, BOTH, pairs)  27.1 us
    all_to_all x1, waiting for transfers between devices, shards(): share = lax.all_to_all(share, BOTH, 0, 0, tiled=True)  10.6 us
    pallas_call x1, Pallas kernels, shards(): pl.pallas_call(functools.partial(attention_kernel, n_seq, n_res, groups),...  8.02 us
    all_to_all x1, starting transfers between devices, shards(): lax.all_to_all(bias.reshape(devices, cols, held * rows), BOTH, 0, 0, tile...  7.3 us
    all_to_all x1, starting transfers between devices, shards(): share = lax.all_to_all(share, BOTH, 0, 0, tiled=True)  6.97 us
    ppermute x6, starting transfers between devices, peer(): return lax.ppermute(x, BOTH, pairs)  6.3 us
    all_to_all x1, waiting for transfers between devices, shards(): rights = lax.all_to_all(rights, 'seq', 0, 0, tiled=True)  5.42 us
    ppermute x9, starting transfers between devices, partner(): return lax.ppermute(x, 'res', [(i, i ^ s) for i in range(n_res)])  5.12 us
  transfers between devices with their start and end apart: 21, of which 12 were waited for; matrix products, arithmetic and copies ran while one was open for 1% of the time, Pallas kernels for 11%

profile of v5, /device:TPU:0, one launch (start us, length us, event | category | flops | bytes accessed | tf_op | source)
XLA Modules:
  0.0 115.6 jit_solution(16257601266526927289)
XLA Ops:
  0.6 0.0 copy-start
  0.6 1.0 copy-done
  1.7 1.2 %fusion.1 = f32[8,64,32]{1,0,2:T(8,128)S(1)} fusion(bf16[64,32,128]{2,1,0:T(8,128)(2,1)S(1)} %copy-done, bf16[128,8]{0,1:T(8,128)(2,1)} %param.15), kind=kOutput, calls=%fused_computation.3 | convolution fusion | flops 4194304 | bytes 591872 | tf_op jit(solution)/shard_map/ijc,ch->hij/dot_general | solution.py:274
  2.9 0.2 broadcast_in_dim.6
  3.1 0.0 copy-start.5
  3.1 0.0 copy-start.3
  3.1 0.0 copy-start.4
  3.1 0.9 broadcast_in_dim.14
  4.0 7.3 %all-to-all-start = ((f32[32,32,128]{2,1,0:T(8,128)}), f32[32,32,128]{2,1,0:T(8,128)S(1)}, u32[]{:S(2)}, u32[]{:S(2)}) async-start(f32[32,32,128]{2,1,0:T(8,128)} %bitcast.35), calls=%async_computation | async-start | bytes 1048576 | tf_op jit(solution)/shard_map/all_to_all | solution.py:279
  11.3 0.1 pad_add_fusion.1.scalars
  11.4 1.0 pack.1
  12.4 0.0 copy-start.9
  12.5 0.7 copy-done.9
  13.1 0.3 collective-permute-start
  13.4 1.7 %collective-permute-start.1 = (bf16[2,256,256]{2,1,0:T(8,128)(2,1)S(1)}, bf16[2,256,256]{2,1,0:T(8,128)(2,1)S(1)}, u32[]{:S(2)}, u32[]{:S(2)}) collective-permute-start(bf16[2,256,256]{2,1,0:T(8,128)(2,1)S(1)} %get-tuple-element.53), channel_id=1, source_target_pairs={{0,4},{1,5},{2,6},{3,7},{4,0},{5,1},{6,2},{7,3},{8,12},{9,13},{10,... | collective-permute-start | bytes 786440 | tf_op jit(solution)/shard_map/ppermute | solution.py:314
  15.1 0.5 collective-permute-start.3
  15.5 1.7 %collective-permute-start.4 = (bf16[2,8,64,128]{3,2,1,0:T(8,128)(2,1)S(1)}, bf16[2,8,64,128]{3,2,1,0:T(8,128)(2,1)S(1)}, u32[]{:S(2)}, u32[]{:S(2)}) collective-permute-start(bf16[2,8,64,128]{3,2,1,0:T(8,128)(2,1)S(1)} %get-tuple-element.57), channel_id=1, source_target_pairs={{0,2},{1,3},{2,0},{3,1},{4,6},{5,7},{6,4},{7,5},{8,10},{9,11},{10,... | collective-permute-start | bytes 786440 | tf_op jit(solution)/shard_map/ppermute | solution.py:317
  17.2 0.7 copy-done.11
  17.9 7.6 %collective-permute-done.1.refs_2_ = bf16[2,256,256]{2,1,0:T(8,128)(2,1)S(1)} collective-permute-done((bf16[2,256,256]{2,1,0:T(8,128)(2,1)S(1)}, bf16[2,256,256]{2,1,0:T(8,128)(2,1)S(1)}, u32[]{:S(2)}, u32[]{:S(2)}) %collective-permute-start.1) | collective-permute-done | bytes 262176 | tf_op jit(solution)/shard_map/ppermute | solution.py:314
  25.5 5.9 %collective-permute-done.2.refs_3_ = bf16[2,256,256]{2,1,0:T(8,128)(2,1)S(1)} collective-permute-done((bf16[2,256,256]{2,1,0:T(8,128)(2,1)S(1)}, bf16[2,256,256]{2,1,0:T(8,128)(2,1)S(1)}, u32[]{:S(2)}, u32[]{:S(2)}) %collective-permute-start.2) | collective-permute-done | bytes 262176 | tf_op jit(solution)/shard_map/ppermute | solution.py:314
  31.4 0.6 collective-permute-done.5.refs_3_
  31.9 0.8 order_rights.1
  32.8 4.2 %all-to-all-start.1 = ((bf16[8,8,32,128]{3,2,1,0:T(8,128)(2,1)}), bf16[8,8,32,128]{3,2,1,0:T(8,128)(2,1)S(1)}, u32[]{:S(2)}, u32[]{:S(2)}) async-start(bf16[8,8,32,128]{3,2,1,0:T(8,128)(2,1)} %order_rights.1), calls=%async_computation.1 | async-start | bytes 1048576 | tf_op jit(solution)/shard_map/all_to_all | solution.py:345
  37.0 0.0 copy-start.12
  37.1 0.0 copy-start.23
  37.1 0.8 collective-permute-start.6
  37.9 0.0 copy-done.10
  37.9 0.1 copy-done.12
  38.0 0.1 copy-done.14
  38.1 0.1 copy-done.16
  38.2 8.0 %attention.1 = (bf16[3,256,128]{2,1,0:T(8,128)(2,1)S(1)}, bf16[3,256,128]{2,1,0:T(8,128)(2,1)S(1)}, bf16[3,256,128]{2,1,0:T(8,128)(2,1)S(1)}, bf16[3,256,128]{2,1,0:T(8,128)(2,1)S(1)}, bf16[32,32,128]{2,1,0:T(8,128)(2,1)}) custom-call(f32[32,32,128]{2,1,0:T(8,128)S(1)} %all-to-all-done.bias_ref, s32[1,256]{1,0:T(1,128)S(1)} %bitcast.34, ...), custom_call_target="tpu_custom_call" | custom-call | flops 4000000000 | tf_op jit(solution)/shard_map/attention/pallas_call | solution.py:349
  46.2 0.7 copy-done.17
  46.9 0.7 copy-done.19
  47.6 0.7 copy-done.21
  48.2 5.4 %all-to-all-done.1.refs_0_ = bf16[8,8,32,128]{3,2,1,0:T(8,128)(2,1)S(1)} async-done(((bf16[8,8,32,128]{3,2,1,0:T(8,128)(2,1)}), bf16[8,8,32,128]{3,2,1,0:T(8,128)(2,1)S(1)}, u32[]{:S(2)}, u32[]{:S(2)}) %all-to-all-start.1) | async-done | bytes 524320 | tf_op jit(solution)/shard_map/all_to_all | solution.py:345
  53.6 7.0 %all-to-all-start.2 = ((bf16[32,32,128]{2,1,0:T(8,128)(2,1)}), bf16[32,32,128]{2,1,0:T(8,128)(2,1)S(1)}, u32[]{:S(2)}, u32[]{:S(2)}) async-start(bf16[32,32,128]{2,1,0:T(8,128)(2,1)} %get-tuple-element.68), calls=%async_computation.2 | async-start | bytes 524288 | tf_op jit(solution)/shard_map/all_to_all | solution.py:361
  60.6 10.6 %all-to-all-done.2 = bf16[32,32,128]{2,1,0:T(8,128)(2,1)S(1)} async-done(((bf16[32,32,128]{2,1,0:T(8,128)(2,1)}), bf16[32,32,128]{2,1,0:T(8,128)(2,1)S(1)}, u32[]{:S(2)}, u32[]{:S(2)}) %all-to-all-start.2) | async-done | bytes 262176 | tf_op jit(solution)/shard_map/all_to_all | solution.py:361
  71.3 0.9 broadcast_in_dim.15
  72.2 3.8 %all-to-all-start.3 = ((bf16[16,4,32,128]{3,2,1,0:T(8,128)(2,1)}), bf16[16,4,32,128]{3,2,1,0:T(8,128)(2,1)S(1)}, u32[]{:S(2)}, u32[]{:S(2)}) async-start(bf16[16,4,32,128]{3,2,1,0:T(8,128)(2,1)} %broadcast_in_dim.15), calls=%async_computation.3 | async-start | bytes 1048576 | tf_op jit(solution)/shard_map/all_to_all | solution.py:367
  76.0 0.1 collective-permute-start.10
  76.0 0.1 copy.17
  76.1 0.1 reshape_reshape.3
  76.2 0.0 copy-start.24
  76.3 0.0 copy-start.22
  76.3 0.4 convolution_bitcast_fusion
  76.7 2.0 %collective-permute-start.9 = (f32[8,128]{1,0:T(8,128)S(1)}, f32[8,128]{1,0:T(8,128)S(1)}, u32[]{:S(2)}, u32[]{:S(2)}) collective-permute-start(f32[8,128]{1,0:T(8,128)S(1)} %convolution_bitcast_fusion), channel_id=1, source_target_pairs={{0,3},{1,2},{2,1},{3,0},{4,7},{5,6},{6,5},{7,4},{8,11},{9,10},{10,... | collective-permute-start | bytes 12296 | tf_op jit(solution)/shard_map/ppermute | solution.py:317
  78.7 0.2 collective-permute-start.8
  78.9 0.6 collective-permute-start.11
  79.5 0.5 collective-permute-done.9
  80.0 1.8 %collective-permute-start.12 = (bf16[3,256,128]{2,1,0:T(8,128)(2,1)S(1)}, bf16[3,256,128]{2,1,0:T(8,128)(2,1)S(1)}, u32[]{:S(2)}, u32[]{:S(2)}) collective-permute-start(bf16[3,256,128]{2,1,0:T(8,128)(2,1)S(1)} %copy-done.20), channel_id=1, source_target_pairs={{0,5},{1,4},{2,7},{3,6},{4,1},{5,0},{6,3},{7,2},{8,13},{9,12},{10,... | collective-permute-start | bytes 589832 | tf_op jit(solution)/shard_map/ppermute | solution.py:314
  81.8 0.5 collective-permute-done.8
  82.3 6.1 %collective-permute-done.12.refs_3_ = bf16[3,256,128]{2,1,0:T(8,128)(2,1)S(1)} collective-permute-done((bf16[3,256,128]{2,1,0:T(8,128)(2,1)S(1)}, bf16[3,256,128]{2,1,0:T(8,128)(2,1)S(1)}, u32[]{:S(2)}, u32[]{:S(2)}) %collective-permute-start.12) | collective-permute-done | bytes 196640 | tf_op jit(solution)/shard_map/ppermute | solution.py:314
  88.5 2.7 %all-to-all-done.3.near_ref = bf16[16,4,32,128]{3,2,1,0:T(8,128)(2,1)S(1)} async-done(((bf16[16,4,32,128]{3,2,1,0:T(8,128)(2,1)}), bf16[16,4,32,128]{3,2,1,0:T(8,128)(2,1)S(1)}, u32[]{:S(2)}, u32[]{:S(2)}) %all-to-all-start.3) | async-done | bytes 524320 | tf_op jit(solution)/shard_map/all_to_all | solution.py:367
  91.2 1.9 %collective-permute-done.15.far_ref = bf16[16,4,32,128]{3,2,1,0:T(8,128)(2,1)S(1)} collective-permute-done((bf16[16,4,32,128]{3,2,1,0:T(8,128)(2,1)S(1)}, bf16[16,4,32,128]{3,2,1,0:T(8,128)(2,1)S(1)}, u32[]{:S(2)}, u32[]{:S(2)}) %collective-permute-start.15) | collective-permute-done | bytes 524320 | tf_op jit(solution)/shard_map/ppermute | solution.py:317
  93.1 2.2 %d_right.1 = bf16[8,272,128]{2,1,0:T(8,128)(2,1)} custom-call(s32[1]{0:T(128)} %bitcast.1.scalars, bf16[16,4,32,128]{3,2,1,0:T(8,128)(2,1)S(1)} %all-to-all-done.3.near_ref, bf16[16,4,32,128]{3,2,1,0:T(8,128)(2,1)S(1)} %collective-permute-done.15.far_ref, f32[2,8,128]{2,1,0:T(8,128)S(1)} %pad_maximum_fusion.extra_ref, ...), custom_call_target="tpu_custom_call" | custom-call | tf_op jit(solution)/shard_map/d_right/pallas_call | solution.py:386
  95.3 3.8 %all-to-all-start.4 = ((bf16[8,272,128]{2,1,0:T(8,128)(2,1)}), bf16[8,272,128]{2,1,0:T(8,128)(2,1)S(1)}, u32[]{:S(2)}, u32[]{:S(2)}) async-start(bf16[8,272,128]{2,1,0:T(8,128)(2,1)} %d_right.1), calls=%async_computation.4 | async-start | bytes 1114112 | tf_op jit(solution)/shard_map/all_to_all | solution.py:396
  99.0 0.1 pad_add_fusion.scalars
  99.1 2.1 %d_left.1 = (bf16[16,64,128]{2,1,0:T(8,128)(2,1)S(1)}, bf16[16,64,128]{2,1,0:T(8,128)(2,1)S(1)}) custom-call(s32[2]{0:T(128)S(1)} %pad_add_fusion.scalars, bf16[16,4,32,128]{3,2,1,0:T(8,128)(2,1)S(1)} %all-to-all-done.3.near_ref, f32[2,8,128]{2,1,0:T(8,128)S(1)} %pad_maximum_fusion.extra_ref, bf16[8,8,32,128]{3,2,1,0:T(8,128)(2,1)S(1)} %all-to-all-done.1.refs_0_, ...), custom_call_target="tpu_custom_call" | custom-call | tf_op jit(solution)/shard_map/d_left/pallas_call | solution.py:399
  101.2 0.7 collective-permute-start.13
  101.9 2.0 %collective-permute-start.14 = (bf16[3,256,128]{2,1,0:T(8,128)(2,1)S(1)}, bf16[3,256,128]{2,1,0:T(8,128)(2,1)S(1)}, u32[]{:S(2)}, u32[]{:S(2)}) collective-permute-start(bf16[3,256,128]{2,1,0:T(8,128)(2,1)S(1)} %copy-done.18), channel_id=1, source_target_pairs={{0,4},{1,5},{2,6},{3,7},{4,0},{5,1},{6,2},{7,3},{8,12},{9,13},{10,... | collective-permute-start | bytes 589832 | tf_op jit(solution)/shard_map/ppermute | solution.py:314
  104.0 7.5 %collective-permute-done.14.refs_2_ = bf16[3,256,128]{2,1,0:T(8,128)(2,1)S(1)} collective-permute-done((bf16[3,256,128]{2,1,0:T(8,128)(2,1)S(1)}, bf16[3,256,128]{2,1,0:T(8,128)(2,1)S(1)}, u32[]{:S(2)}, u32[]{:S(2)}) %collective-permute-start.14) | collective-permute-done | bytes 196640 | tf_op jit(solution)/shard_map/ppermute | solution.py:314
  111.5 1.1 unpack.1
  112.6 2.0 %all-to-all-done.4.received_ref = bf16[8,272,128]{2,1,0:T(8,128)(2,1)S(1)} async-done(((bf16[8,272,128]{2,1,0:T(8,128)(2,1)}), bf16[8,272,128]{2,1,0:T(8,128)(2,1)S(1)}, u32[]{:S(2)}, u32[]{:S(2)}) %all-to-all-start.4) | async-done | bytes 557088 | tf_op jit(solution)/shard_map/all_to_all | solution.py:396
  114.5 1.0 place.1
  (51 shorter events, 0.2 us)
Async XLA Ops:
  0.6 1.0 copy-start
  1.7 9.7 %copy-start.6 = (bf16[2,256,256]{2,1,0:T(8,128)(2,1)S(1)}, bf16[2,256,256]{2,1,0:T(8,128)(2,1)}, u32[]{:S(2)}) copy-start(bf16[2,256,256]{2,1,0:T(8,128)(2,1)} %refs_3_.1) | copy-start | bytes 786436
  3.1 8.3 %copy-start.5 = (bf16[2,256,256]{2,1,0:T(8,128)(2,1)S(1)}, bf16[2,256,256]{2,1,0:T(8,128)(2,1)}, u32[]{:S(2)}) copy-start(bf16[2,256,256]{2,1,0:T(8,128)(2,1)} %refs_2_.1) | copy-start | bytes 786436
  3.1 8.3 %copy-start.3 = (bf16[2,256,256]{2,1,0:T(8,128)(2,1)S(1)}, bf16[2,256,256]{2,1,0:T(8,128)(2,1)}, u32[]{:S(2)}) copy-start(bf16[2,256,256]{2,1,0:T(8,128)(2,1)} %refs_0_.1) | copy-start | bytes 786436
  3.1 8.3 %copy-start.4 = (bf16[2,256,256]{2,1,0:T(8,128)(2,1)S(1)}, bf16[2,256,256]{2,1,0:T(8,128)(2,1)}, u32[]{:S(2)}) copy-start(bf16[2,256,256]{2,1,0:T(8,128)(2,1)} %refs_1_.1) | copy-start | bytes 786436
  4.0 7.4 %copy-start.1 = (bf16[32,64,128]{2,1,0:T(8,128)(2,1)S(1)}, bf16[32,64,128]{2,1,0:T(8,128)(2,1)}, u32[]{:S(2)}) copy-start(bf16[32,64,128]{2,1,0:T(8,128)(2,1)} %refs_4_.1) | copy-start | bytes 1572868
  4.0 7.4 %copy-start.2 = (bf16[64,32,128]{2,1,0:T(8,128)(2,1)S(1)}, bf16[64,32,128]{2,1,0:T(8,128)(2,1)}, u32[]{:S(2)}) copy-start(bf16[64,32,128]{2,1,0:T(8,128)(2,1)} %param.17) | copy-start | bytes 1572868
  4.0 28.8 %all-to-all-start = ((f32[32,32,128]{2,1,0:T(8,128)}), f32[32,32,128]{2,1,0:T(8,128)S(1)}, u32[]{:S(2)}, u32[]{:S(2)}) async-start(f32[32,32,128]{2,1,0:T(8,128)} %bitcast.35), calls=%async_computation | async-start | bytes 1048576 | tf_op jit(solution)/shard_map/all_to_all | solution.py:279
  12.4 0.7 copy-start.9
  13.1 4.1 %collective-permute-start = (bf16[2,256,256]{2,1,0:T(8,128)(2,1)S(1)}, bf16[2,256,256]{2,1,0:T(8,128)(2,1)S(1)}, u32[]{:S(2)}, u32[]{:S(2)}) collective-permute-start(bf16[2,256,256]{2,1,0:T(8,128)(2,1)S(1)} %get-tuple-element.52), channel_id=1, source_target_pairs={{0,1},{1,0},{2,3},{3,2},{4,5},{5,4},{6,7},{7,6},{8,9},{9,8},{10,11... | collective-permute-start | bytes 786440 | tf_op jit(solution)/shard_map/ppermute | solution.py:314
  13.4 12.1 %collective-permute-start.1 = (bf16[2,256,256]{2,1,0:T(8,128)(2,1)S(1)}, bf16[2,256,256]{2,1,0:T(8,128)(2,1)S(1)}, u32[]{:S(2)}, u32[]{:S(2)}) collective-permute-start(bf16[2,256,256]{2,1,0:T(8,128)(2,1)S(1)} %get-tuple-element.53), channel_id=1, source_target_pairs={{0,4},{1,5},{2,6},{3,7},{4,0},{5,1},{6,2},{7,3},{8,12},{9,13},{10,... | collective-permute-start | bytes 786440 | tf_op jit(solution)/shard_map/ppermute | solution.py:314
  15.1 16.3 %collective-permute-start.2 = (bf16[2,256,256]{2,1,0:T(8,128)(2,1)S(1)}, bf16[2,256,256]{2,1,0:T(8,128)(2,1)S(1)}, u32[]{:S(2)}, u32[]{:S(2)}) collective-permute-start(bf16[2,256,256]{2,1,0:T(8,128)(2,1)S(1)} %get-tuple-element.54), channel_id=1, source_target_pairs={{0,5},{1,4},{2,7},{3,6},{4,1},{5,0},{6,3},{7,2},{8,13},{9,12},{10,... | collective-permute-start | bytes 786440 | tf_op jit(solution)/shard_map/ppermute | solution.py:314
  15.1 16.3 %collective-permute-start.3 = (bf16[2,8,64,128]{3,2,1,0:T(8,128)(2,1)S(1)}, bf16[2,8,64,128]{3,2,1,0:T(8,128)(2,1)S(1)}, u32[]{:S(2)}, u32[]{:S(2)}) collective-permute-start(bf16[2,8,64,128]{3,2,1,0:T(8,128)(2,1)S(1)} %get-tuple-element.56), channel_id=1, source_target_pairs={{0,1},{1,0},{2,3},{3,2},{4,5},{5,4},{6,7},{7,6},{8,9},{9,8},{10,11... | collective-permute-start | bytes 786440 | tf_op jit(solution)/shard_map/ppermute | solution.py:317
  15.5 15.8 %collective-permute-start.4 = (bf16[2,8,64,128]{3,2,1,0:T(8,128)(2,1)S(1)}, bf16[2,8,64,128]{3,2,1,0:T(8,128)(2,1)S(1)}, u32[]{:S(2)}, u32[]{:S(2)}) collective-permute-start(bf16[2,8,64,128]{3,2,1,0:T(8,128)(2,1)S(1)} %get-tuple-element.57), channel_id=1, source_target_pairs={{0,2},{1,3},{2,0},{3,1},{4,6},{5,7},{6,4},{7,5},{8,10},{9,11},{10,... | collective-permute-start | bytes 786440 | tf_op jit(solution)/shard_map/ppermute | solution.py:317
  17.2 0.7 copy-start.11
  17.9 14.0 %collective-permute-start.5 = (bf16[2,8,64,128]{3,2,1,0:T(8,128)(2,1)S(1)}, bf16[2,8,64,128]{3,2,1,0:T(8,128)(2,1)S(1)}, u32[]{:S(2)}, u32[]{:S(2)}) collective-permute-start(bf16[2,8,64,128]{3,2,1,0:T(8,128)(2,1)S(1)} %get-tuple-element.58), channel_id=1, source_target_pairs={{0,3},{1,2},{2,1},{3,0},{4,7},{5,6},{6,5},{7,4},{8,11},{9,10},{10,... | collective-permute-start | bytes 786440 | tf_op jit(solution)/shard_map/ppermute | solution.py:317
  25.5 7.3 %copy-start.13 = (bf16[2,256,256]{2,1,0:T(8,128)(2,1)}, bf16[2,256,256]{2,1,0:T(8,128)(2,1)S(1)}, u32[]{:S(2)}) copy-start(bf16[2,256,256]{2,1,0:T(8,128)(2,1)S(1)} %collective-permute-done.1.refs_2_) | copy-start | bytes 786436
  31.4 1.4 %copy-start.15 = (bf16[2,256,256]{2,1,0:T(8,128)(2,1)}, bf16[2,256,256]{2,1,0:T(8,128)(2,1)S(1)}, u32[]{:S(2)}) copy-start(bf16[2,256,256]{2,1,0:T(8,128)(2,1)S(1)} %collective-permute-done.2.refs_3_) | copy-start | bytes 786436
  32.8 20.9 %all-to-all-start.1 = ((bf16[8,8,32,128]{3,2,1,0:T(8,128)(2,1)}), bf16[8,8,32,128]{3,2,1,0:T(8,128)(2,1)S(1)}, u32[]{:S(2)}, u32[]{:S(2)}) async-start(bf16[8,8,32,128]{3,2,1,0:T(8,128)(2,1)} %order_rights.1), calls=%async_computation.1 | async-start | bytes 1048576 | tf_op jit(solution)/shard_map/all_to_all | solution.py:345
  37.0 0.9 copy-start.10
  37.0 1.0 copy-start.12
  37.0 1.1 copy-start.14
  37.0 1.2 %copy-start.16 = (bf16[2,256,256]{2,1,0:T(8,128)(2,1)S(1)}, bf16[2,256,256]{2,1,0:T(8,128)(2,1)}, u32[]{:S(2)}) copy-start(bf16[2,256,256]{2,1,0:T(8,128)(2,1)} %copy-done.15) | copy-start | bytes 786436
  37.1 1.1 copy-start.23
  37.1 23.5 %collective-permute-start.6 = (bf16[8,256,128]{2,1,0:T(8,128)(2,1)S(1)}, bf16[8,256,128]{2,1,0:T(8,128)(2,1)S(1)}, u32[]{:S(2)}, u32[]{:S(2)}) collective-permute-start(bf16[8,256,128]{2,1,0:T(8,128)(2,1)S(1)} %order_lefts.1), channel_id=1, source_target_pairs={{0,0},{1,16},{2,8},{3,24},{4,4},{5,20},{6,12},{7,28},{8,1},{9,17},... | collective-permute-start | bytes 1572872 | tf_op jit(solution)/shard_map/ppermute | solution.py:344
  46.2 0.7 copy-start.17
  46.9 0.7 copy-start.19
  47.6 0.7 copy-start.21
  53.6 17.6 %all-to-all-start.2 = ((bf16[32,32,128]{2,1,0:T(8,128)(2,1)}), bf16[32,32,128]{2,1,0:T(8,128)(2,1)S(1)}, u32[]{:S(2)}, u32[]{:S(2)}) async-start(bf16[32,32,128]{2,1,0:T(8,128)(2,1)} %get-tuple-element.68), calls=%async_computation.2 | async-start | bytes 524288 | tf_op jit(solution)/shard_map/all_to_all | solution.py:361
  72.2 19.0 %all-to-all-start.3 = ((bf16[16,4,32,128]{3,2,1,0:T(8,128)(2,1)}), bf16[16,4,32,128]{3,2,1,0:T(8,128)(2,1)S(1)}, u32[]{:S(2)}, u32[]{:S(2)}) async-start(bf16[16,4,32,128]{3,2,1,0:T(8,128)(2,1)} %broadcast_in_dim.15), calls=%async_computation.3 | async-start | bytes 1048576 | tf_op jit(solution)/shard_map/all_to_all | solution.py:367
  76.0 12.5 %collective-permute-start.10 = (bf16[8,8,32,128]{3,2,1,0:T(8,128)(2,1)S(1)}, bf16[8,8,32,128]{3,2,1,0:T(8,128)(2,1)S(1)}, u32[]{:S(2)}, u32[]{:S(2)}) collective-permute-start(bf16[8,8,32,128]{3,2,1,0:T(8,128)(2,1)S(1)} %all-to-all-done.1.refs_0_), channel_id=1, source_target_pairs={{0,1},{1,0},{2,3},{3,2},{4,5},{5,4},{6,7},{7,6},{8,9},{9,8},{10,11... | collective-permute-start | bytes 1572872 | tf_op jit(solution)/shard_map/ppermute | solution.py:317
  76.2 2.6 %copy-start.24 = (bf16[128,8]{0,1:T(8,128)(2,1)S(1)}, bf16[128,8]{0,1:T(8,128)(2,1)}, u32[]{:S(2)}) copy-start(bf16[128,8]{0,1:T(8,128)(2,1)} %param.15) | copy-start | bytes 6148
  76.3 2.6 %copy-start.22 = (bf16[3,256,128]{2,1,0:T(8,128)(2,1)S(1)}, bf16[3,256,128]{2,1,0:T(8,128)(2,1)}, u32[]{:S(2)}) copy-start(bf16[3,256,128]{2,1,0:T(8,128)(2,1)} %copy-done.21) | copy-start | bytes 589828
  76.3 3.7 %copy-start.20 = (bf16[3,256,128]{2,1,0:T(8,128)(2,1)S(1)}, bf16[3,256,128]{2,1,0:T(8,128)(2,1)}, u32[]{:S(2)}) copy-start(bf16[3,256,128]{2,1,0:T(8,128)(2,1)} %copy-done.19) | copy-start | bytes 589828
  76.7 3.3 %collective-permute-start.9 = (f32[8,128]{1,0:T(8,128)S(1)}, f32[8,128]{1,0:T(8,128)S(1)}, u32[]{:S(2)}, u32[]{:S(2)}) collective-permute-start(f32[8,128]{1,0:T(8,128)S(1)} %convolution_bitcast_fusion), channel_id=1, source_target_pairs={{0,3},{1,2},{2,1},{3,0},{4,7},{5,6},{6,5},{7,4},{8,11},{9,10},{10,... | collective-permute-start | bytes 12296 | tf_op jit(solution)/shard_map/ppermute | solution.py:317
  78.7 3.6 %collective-permute-start.8 = (f32[8,128]{1,0:T(8,128)S(1)}, f32[8,128]{1,0:T(8,128)S(1)}, u32[]{:S(2)}, u32[]{:S(2)}) collective-permute-start(f32[8,128]{1,0:T(8,128)S(1)} %convolution_bitcast_fusion), channel_id=1, source_target_pairs={{0,2},{1,3},{2,0},{3,1},{4,6},{5,7},{6,4},{7,5},{8,10},{9,11},{10,... | collective-permute-start | bytes 12296 | tf_op jit(solution)/shard_map/ppermute | solution.py:317
  78.9 3.4 %collective-permute-start.7 = (f32[8,128]{1,0:T(8,128)S(1)}, f32[8,128]{1,0:T(8,128)S(1)}, u32[]{:S(2)}, u32[]{:S(2)}) collective-permute-start(f32[8,128]{1,0:T(8,128)S(1)} %convolution_bitcast_fusion), channel_id=1, source_target_pairs={{0,1},{1,0},{2,3},{3,2},{4,5},{5,4},{6,7},{7,6},{8,9},{9,8},{10,11... | collective-permute-start | bytes 12296 | tf_op jit(solution)/shard_map/ppermute | solution.py:317
  78.9 3.4 %collective-permute-start.11 = (bf16[3,256,128]{2,1,0:T(8,128)(2,1)S(1)}, bf16[3,256,128]{2,1,0:T(8,128)(2,1)S(1)}, u32[]{:S(2)}, u32[]{:S(2)}) collective-permute-start(bf16[3,256,128]{2,1,0:T(8,128)(2,1)S(1)} %copy-done.22), channel_id=1, source_target_pairs={{0,1},{1,0},{2,3},{3,2},{4,5},{5,4},{6,7},{7,6},{8,9},{9,8},{10,11... | collective-permute-start | bytes 589832 | tf_op jit(solution)/shard_map/ppermute | solution.py:314
  80.0 8.5 %collective-permute-start.12 = (bf16[3,256,128]{2,1,0:T(8,128)(2,1)S(1)}, bf16[3,256,128]{2,1,0:T(8,128)(2,1)S(1)}, u32[]{:S(2)}, u32[]{:S(2)}) collective-permute-start(bf16[3,256,128]{2,1,0:T(8,128)(2,1)S(1)} %copy-done.20), channel_id=1, source_target_pairs={{0,5},{1,4},{2,7},{3,6},{4,1},{5,0},{6,3},{7,2},{8,13},{9,12},{10,... | collective-permute-start | bytes 589832 | tf_op jit(solution)/shard_map/ppermute | solution.py:314
  88.5 6.8 %copy-start.7 = (bf16[3,256,128]{2,1,0:T(8,128)(2,1)}, bf16[3,256,128]{2,1,0:T(8,128)(2,1)S(1)}, u32[]{:S(2)}) copy-start(bf16[3,256,128]{2,1,0:T(8,128)(2,1)S(1)} %collective-permute-done.12.refs_3_) | copy-start | bytes 589828
  91.2 1.9 %collective-permute-start.15 = (bf16[16,4,32,128]{3,2,1,0:T(8,128)(2,1)S(1)}, bf16[16,4,32,128]{3,2,1,0:T(8,128)(2,1)S(1)}, u32[]{:S(2)}, u32[]{:S(2)}) collective-permute-start(bf16[16,4,32,128]{3,2,1,0:T(8,128)(2,1)S(1)} %all-to-all-done.3.near_ref), channel_id=1, source_target_pairs={{0,1},{1,0},{2,3},{3,2},{4,5},{5,4},{6,7},{7,6},{8,9},{9,8},{10,11... | collective-permute-start | bytes 1572872 | tf_op jit(solution)/shard_map/ppermute | solution.py:317
  95.3 19.2 %all-to-all-start.4 = ((bf16[8,272,128]{2,1,0:T(8,128)(2,1)}), bf16[8,272,128]{2,1,0:T(8,128)(2,1)S(1)}, u32[]{:S(2)}, u32[]{:S(2)}) async-start(bf16[8,272,128]{2,1,0:T(8,128)(2,1)} %d_right.1), calls=%async_computation.4 | async-start | bytes 1114112 | tf_op jit(solution)/shard_map/all_to_all | solution.py:396
  99.1 2.8 %copy-start.18 = (bf16[3,256,128]{2,1,0:T(8,128)(2,1)S(1)}, bf16[3,256,128]{2,1,0:T(8,128)(2,1)}, u32[]{:S(2)}) copy-start(bf16[3,256,128]{2,1,0:T(8,128)(2,1)} %copy-done.17) | copy-start | bytes 589828
  99.1 12.4 %copy-start.8 = (bf16[3,256,128]{2,1,0:T(8,128)(2,1)S(1)}, bf16[3,256,128]{2,1,0:T(8,128)(2,1)}, u32[]{:S(2)}) copy-start(bf16[3,256,128]{2,1,0:T(8,128)(2,1)} %copy-done.7) | copy-start | bytes 589828
  101.2 10.3 %collective-permute-start.13 = (bf16[16,64,128]{2,1,0:T(8,128)(2,1)S(1)}, bf16[16,64,128]{2,1,0:T(8,128)(2,1)S(1)}, u32[]{:S(2)}, u32[]{:S(2)}) collective-permute-start(bf16[16,64,128]{2,1,0:T(8,128)(2,1)S(1)} %get-tuple-element.78), channel_id=1, source_target_pairs={{0,2},{1,3},{2,0},{3,1},{4,6},{5,7},{6,4},{7,5},{8,10},{9,11},{10,... | collective-permute-start | bytes 786440 | tf_op jit(solution)/shard_map/ppermute | solution.py:317
  101.9 9.6 %collective-permute-start.14 = (bf16[3,256,128]{2,1,0:T(8,128)(2,1)S(1)}, bf16[3,256,128]{2,1,0:T(8,128)(2,1)S(1)}, u32[]{:S(2)}, u32[]{:S(2)}) collective-permute-start(bf16[3,256,128]{2,1,0:T(8,128)(2,1)S(1)} %copy-done.18), channel_id=1, source_target_pairs={{0,4},{1,5},{2,6},{3,7},{4,0},{5,1},{6,2},{7,3},{8,12},{9,13},{10,... | collective-permute-start | bytes 589832 | tf_op jit(solution)/shard_map/ppermute | solution.py:314
